TPU v7x, 256 devices: a whole 4x4x8 slice. The times are simulated.
256 devices in a mesh: row: 32 (over z, y_hi, core), col: 8 (over y_lo, x).
Axes of the slice: x: 4, y: 4 (y_hi: 2, y_lo: 2; y = y_hi * 2 + y_lo), z: 8, core: 2. Of those that a mesh axis runs over, the one named last changes fastest.
Arguments:
- images: float32 [16384, 1152], P(('row', 'col')), may hold values from -0.17677669 to 0.17677669
- texts: float32 [16384, 1152], P(('row', 'col')), may hold values from -0.17677669 to 0.17677669
- logit_scale: float32 [1], replicated, may hold values from 40 to 120
- logit_bias: float32 [1], replicated, may hold values from -8 to -4
Outputs:
- image_grad: float32 [16384, 1152], P(('row', 'col'))
- text_grad: float32 [16384, 1152], P(('row', 'col'))
All inputs are finite; a program needn't handle non-finite values.
Results may differ from a plain program's by a relative error of at most 0.009.
Values may be sent and summed in bfloat16 or wider, within the bound.
No kernel may reach another device: no remote copies, remote signals or barrier semaphores. Data moves between devices by JAX's collectives and lax.ppermute only.
A program may use at most 64 MiB of HBM per device.

v0:
```python
import jax
import jax.numpy as jnp
from jax import lax
from jax.sharding import PartitionSpec as P


def shifted(value, axis, by):
    length = lax.axis_size(axis)
    return lax.ppermute(value, axis, [(i, (i + by) % length) for i in range(length)])


def normalize(raw):
    inv = lax.rsqrt(jnp.sum(raw * raw, axis=1, keepdims=True) + 1e-06)
    return ((raw * inv).astype(jnp.bfloat16), inv)


def unnormalize(raw, inv, grad):
    return inv * grad - raw * (inv * inv * inv) * jnp.sum(raw * grad, axis=1, keepdims=True)


def pair_tile(moving, wide, moving_ids, wide_ids, scale, bias):
    logits = (
        scale
        * lax.dot_general(
            moving, wide, (((1,), (1,)), ((), ())), preferred_element_type=jnp.float32
        )
        + bias
    )
    sign = jnp.where(moving_ids[:, None] == wide_ids[None, :], 1.0, -1.0).astype(jnp.float32)
    weights = (-sign * jax.nn.sigmoid(-sign * logits)).astype(jnp.bfloat16)
    d_moving = scale * jnp.dot(weights, wide, preferred_element_type=jnp.float32)
    d_wide = scale * lax.dot_general(
        weights, moving, (((0,), (0,)), ((), ())), preferred_element_type=jnp.float32
    )
    return (d_moving, d_wide)


def body(images, texts, logit_scale, logit_bias):
    rows = images.shape[0]
    width = images.shape[1]
    n_row = lax.axis_size("row")
    n_col = lax.axis_size("col")
    row_idx = lax.axis_index("row")
    col_idx = lax.axis_index("col")
    scale = logit_scale[0]
    bias = logit_bias[0]
    img_norm, img_inv = normalize(images)
    txt_norm, txt_inv = normalize(texts)
    wide_local, moving_local = (img_norm, txt_norm)
    own = jnp.arange(rows, dtype=jnp.int32)
    wide = lax.all_gather(wide_local, "row", axis=0, tiled=True)
    places = jnp.arange(rows * n_row, dtype=jnp.int32)
    wide_ids = (places // rows * n_col + col_idx) * rows + places % rows
    d_wide = jnp.zeros((rows * n_row, width), jnp.float32)
    block = moving_local
    accum = jnp.zeros((rows, width), jnp.float32)
    for step in range(n_col):
        if step > 0:
            block = shifted(block, "col", 1)
        source = (col_idx - step) % n_col
        block_ids = (row_idx * n_col + source) * rows + own
        d_block, d_part = pair_tile(block, wide, block_ids, wide_ids, scale, bias)
        d_wide = d_wide + d_part
        accum = shifted(accum + d_block, "col", 1)
    d_wide_own = lax.psum_scatter(d_wide, "row", scatter_dimension=0, tiled=True)
    img_dir, txt_dir = (d_wide_own, accum)
    return (unnormalize(images, img_inv, img_dir), unnormalize(texts, txt_inv, txt_dir))


def solution(mesh):
    placed = (P(("row", "col"), None), P(("row", "col"), None), P(), P())
    return jax.shard_map(
        body,
        mesh=mesh,
        in_specs=placed,
        out_specs=(P(("row", "col"), None), P(("row", "col"), None)),
        check_vma=False,
    )
```

profile of v0, /device:TPU:8, one launch (start us, length us, event | category | flops | bytes accessed | tf_op | source)
XLA Modules:
  0.0 315.7 jit_solution(12538381273584806978)
XLA Ops:
  8.3 1.7 multiply_convert_fusion
  13.8 6.2 %collective-permute-done = bf16[64,1152]{1,0:T(8,128)(2,1)S(1)} collective-permute-done((bf16[64,1152]{1,0:T(8,128)(2,1)S(1)}, bf16[64,1152]{1,0:T(8,128)(2,1)S(1)}, u32[]{:S(2)}, u32[]{:S(2)}) %collective-permute-start) | collective-permute-done | bytes 147488 | tf_op jit(solution)/shard_map/ppermute | solution.py:9
  20.0 7.2 %collective-permute-done.1 = bf16[64,1152]{1,0:T(8,128)(2,1)S(1)} collective-permute-done((bf16[64,1152]{1,0:T(8,128)(2,1)S(1)}, bf16[64,1152]{1,0:T(8,128)(2,1)S(1)}, u32[]{:S(2)}, u32[]{:S(2)}) %collective-permute-start.1) | collective-permute-done | bytes 147488 | tf_op jit(solution)/shard_map/ppermute | solution.py:9
  27.3 7.2 %collective-permute-done.2 = bf16[64,1152]{1,0:T(8,128)(2,1)S(1)} collective-permute-done((bf16[64,1152]{1,0:T(8,128)(2,1)S(1)}, bf16[64,1152]{1,0:T(8,128)(2,1)S(1)}, u32[]{:S(2)}, u32[]{:S(2)}) %collective-permute-start.2) | collective-permute-done | bytes 147488 | tf_op jit(solution)/shard_map/ppermute | solution.py:9
  34.6 7.2 %collective-permute-done.3 = bf16[64,1152]{1,0:T(8,128)(2,1)S(1)} collective-permute-done((bf16[64,1152]{1,0:T(8,128)(2,1)S(1)}, bf16[64,1152]{1,0:T(8,128)(2,1)S(1)}, u32[]{:S(2)}, u32[]{:S(2)}) %collective-permute-start.3) | collective-permute-done | bytes 147488 | tf_op jit(solution)/shard_map/ppermute | solution.py:9
  41.8 8.1 %collective-permute-done.4 = bf16[64,1152]{1,0:T(8,128)(2,1)S(1)} collective-permute-done((bf16[64,1152]{1,0:T(8,128)(2,1)S(1)}, bf16[64,1152]{1,0:T(8,128)(2,1)S(1)}, u32[]{:S(2)}, u32[]{:S(2)}) %collective-permute-start.4) | collective-permute-done | bytes 147488 | tf_op jit(solution)/shard_map/ppermute | solution.py:9
  51.3 7.0 %collective-permute-done.5 = bf16[64,1152]{1,0:T(8,128)(2,1)S(1)} collective-permute-done((bf16[64,1152]{1,0:T(8,128)(2,1)S(1)}, bf16[64,1152]{1,0:T(8,128)(2,1)S(1)}, u32[]{:S(2)}, u32[]{:S(2)}) %collective-permute-start.5) | collective-permute-done | bytes 147488 | tf_op jit(solution)/shard_map/ppermute | solution.py:9
  58.3 45.4 %all-gather.2.cloned.1.call-done = bf16[2048,1152]{1,0:T(8,128)(2,1)} async-done(((bf16[64,1152]{1,0:T(8,128)(2,1)}), bf16[2048,1152]{1,0:T(8,128)(2,1)}) %all-gather.2.cloned.1.call-update) | async-done | bytes 4718608 | tf_op jit(solution)/shard_map/all_gather | solution.py:51
  103.7 4.1 %fusion.58 = bf16[64,2048]{1,0:T(8,128)(2,1)S(1)} fusion(bf16[64,1152]{1,0:T(8,128)(2,1)S(1)} %multiply_convert_fusion.1, bf16[2048,1152]{1,0:T(8,128)(2,1)} %all-gather.2.cloned.1.call-done, f32[]{:T(128)} %bitcast.67, f32[]{:T(128)} %bitcast.51, s32[2048]{0:T(1024)S(1)} %fusion.75, s32[64]{0:T(128)S(1)} %iota_add_fusion.7), kind=kOutput, calls=%fused_computation.81 | convolution fusion | flops 303431680 | bytes 5136648 | tf_op jit(solution)/shard_map/dot_general | solution.py:24
  115.4 1.6 fusion.61
  123.2 1.7 convolution_add_fusion.2
  129.5 5.1 %fusion = f32[2048,1152]{1,0:T(8,128)} fusion(f32[2048,1152]{1,0:T(8,128)S(1)} %convolution_add_fusion.1, bf16[64,2048]{1,0:T(8,128)(2,1)S(1)} %fusion.65, bf16[64,1152]{1,0:T(8,128)(2,1)S(1)} %collective-permute-done.6, f32[]{:T(128)} %bitcast.50), kind=kOutput, calls=%fused_computation.1 | convolution fusion | flops 306708480 | bytes 19283972 | tf_op jit(solution)/shard_map/dot_general | solution.py:32
  134.7 3.4 %convolution_multiply_fusion.7 = f32[64,1152]{1,0:T(8,128)S(1)} fusion(bf16[64,2048]{1,0:T(8,128)(2,1)S(1)} %fusion.58, bf16[2048,1152]{1,0:T(8,128)(2,1)} %all-gather.2.cloned.1.call-done, f32[]{:T(128)} %bitcast.52), kind=kOutput, calls=%fused_computation.15 | convolution fusion | flops 302063616 | bytes 5275652 | tf_op jit(solution)/shard_map/dot_general | solution.py:31
  138.2 11.3 %collective-permute-done.7 = f32[64,1152]{1,0:T(8,128)S(1)} collective-permute-done((f32[64,1152]{1,0:T(8,128)S(1)}, f32[64,1152]{1,0:T(8,128)S(1)}, u32[]{:S(2)}, u32[]{:S(2)}) %collective-permute-start.7) | collective-permute-done | bytes 294944 | tf_op jit(solution)/shard_map/ppermute | solution.py:9
  149.5 3.5 %fusion.1 = f32[64,1152]{1,0:T(8,128)S(1)} fusion(f32[64,1152]{1,0:T(8,128)S(1)} %collective-permute-done.7, bf16[64,2048]{1,0:T(8,128)(2,1)S(1)} %fusion.59, bf16[2048,1152]{1,0:T(8,128)(2,1)} %all-gather.2.cloned.1.call-done, f32[]{:T(128)} %bitcast.66), kind=kOutput, calls=%fused_computation.16 | convolution fusion | flops 302137344 | bytes 5570564 | tf_op jit(solution)/shard_map/dot_general | solution.py:31
  154.0 9.5 %collective-permute-done.8 = f32[64,1152]{1,0:T(8,128)S(1)} collective-permute-done((f32[64,1152]{1,0:T(8,128)S(1)}, f32[64,1152]{1,0:T(8,128)S(1)}, u32[]{:S(2)}, u32[]{:S(2)}) %collective-permute-start.8) | collective-permute-done | bytes 294944 | tf_op jit(solution)/shard_map/ppermute | solution.py:9
  164.6 8.7 %collective-permute-done.9 = f32[64,1152]{1,0:T(8,128)S(1)} collective-permute-done((f32[64,1152]{1,0:T(8,128)S(1)}, f32[64,1152]{1,0:T(8,128)S(1)}, u32[]{:S(2)}, u32[]{:S(2)}) %collective-permute-start.9) | collective-permute-done | bytes 294944 | tf_op jit(solution)/shard_map/ppermute | solution.py:9
  174.3 7.9 %collective-permute-done.10 = f32[64,1152]{1,0:T(8,128)S(1)} collective-permute-done((f32[64,1152]{1,0:T(8,128)S(1)}, f32[64,1152]{1,0:T(8,128)S(1)}, u32[]{:S(2)}, u32[]{:S(2)}) %collective-permute-start.10) | collective-permute-done | bytes 294944 | tf_op jit(solution)/shard_map/ppermute | solution.py:9
  183.3 8.0 %collective-permute-done.11 = f32[64,1152]{1,0:T(8,128)S(1)} collective-permute-done((f32[64,1152]{1,0:T(8,128)S(1)}, f32[64,1152]{1,0:T(8,128)S(1)}, u32[]{:S(2)}, u32[]{:S(2)}) %collective-permute-start.11) | collective-permute-done | bytes 294944 | tf_op jit(solution)/shard_map/ppermute | solution.py:9
  192.6 9.0 %collective-permute-done.12 = f32[64,1152]{1,0:T(8,128)S(1)} collective-permute-done((f32[64,1152]{1,0:T(8,128)S(1)}, f32[64,1152]{1,0:T(8,128)S(1)}, u32[]{:S(2)}, u32[]{:S(2)}) %collective-permute-start.12) | collective-permute-done | bytes 294944 | tf_op jit(solution)/shard_map/ppermute | solution.py:9
  202.6 10.2 %collective-permute-done.13 = f32[64,1152]{1,0:T(8,128)S(1)} collective-permute-done((f32[64,1152]{1,0:T(8,128)S(1)}, f32[64,1152]{1,0:T(8,128)S(1)}, u32[]{:S(2)}, u32[]{:S(2)}) %collective-permute-start.13) | collective-permute-done | bytes 294944 | tf_op jit(solution)/shard_map/ppermute | solution.py:9
  213.0 8.9 %collective-permute-done.14 = f32[64,1152]{1,0:T(8,128)S(1)} collective-permute-done((f32[64,1152]{1,0:T(8,128)S(1)}, f32[64,1152]{1,0:T(8,128)S(1)}, u32[]{:S(2)}, u32[]{:S(2)}) %collective-permute-start.14) | collective-permute-done | bytes 294944 | tf_op jit(solution)/shard_map/ppermute | solution.py:9
  222.8 83.1 %reduce-scatter.2.cloned.1.call-done = f32[64,1152]{1,0:T(8,128)} async-done(((f32[2048,1152]{1,0:T(8,128)}), f32[64,1152]{1,0:T(8,128)}) %reduce-scatter.2.cloned.1.call-update) | async-done | bytes 294928 | tf_op jit(solution)/shard_map/reduce_scatter | solution.py:65
  307.1 1.8 multiply_subtract_fusion.1
  (75 shorter events, 31.9 us)
Async XLA Ops:
  7.2 96.5 %all-gather.2.cloned.1.call-start = ((), (), s32[]{:S(2)}) async-start(), calls=%async_computation.1 | async-start | bytes 4866048 | tf_op jit(solution)/shard_map/all_gather | solution.py:51
  10.1 295.9 %reduce-scatter.2.cloned.1.call-start = ((), (), s32[]{:S(2)}) async-start(), calls=%async_computation.2 | async-start | bytes 9732096 | tf_op jit(solution)/shard_map/reduce_scatter | solution.py:65
  12.3 7.8 %collective-permute-start = (bf16[64,1152]{1,0:T(8,128)(2,1)S(1)}, bf16[64,1152]{1,0:T(8,128)(2,1)S(1)}, u32[]{:S(2)}, u32[]{:S(2)}) collective-permute-start(bf16[64,1152]{1,0:T(8,128)(2,1)S(1)} %multiply_convert_fusion.1), channel_id=1, source_target_pairs={{0,1},{1,2},{2,3},{3,4},{4,5},{5,6},{6,7},{7,0},{8,9},{9,10},{10,1... | collective-permute-start | bytes 442376 | tf_op jit(solution)/shard_map/ppermute | solution.py:9
  20.0 7.3 %collective-permute-start.1 = (bf16[64,1152]{1,0:T(8,128)(2,1)S(1)}, bf16[64,1152]{1,0:T(8,128)(2,1)S(1)}, u32[]{:S(2)}, u32[]{:S(2)}) collective-permute-start(bf16[64,1152]{1,0:T(8,128)(2,1)S(1)} %collective-permute-done), channel_id=1, source_target_pairs={{0,1},{1,2},{2,3},{3,4},{4,5},{5,6},{6,7},{7,0},{8,9},{9,10},{10,1... | collective-permute-start | bytes 442376 | tf_op jit(solution)/shard_map/ppermute | solution.py:9
  27.3 7.3 %collective-permute-start.2 = (bf16[64,1152]{1,0:T(8,128)(2,1)S(1)}, bf16[64,1152]{1,0:T(8,128)(2,1)S(1)}, u32[]{:S(2)}, u32[]{:S(2)}) collective-permute-start(bf16[64,1152]{1,0:T(8,128)(2,1)S(1)} %collective-permute-done.1), channel_id=1, source_target_pairs={{0,1},{1,2},{2,3},{3,4},{4,5},{5,6},{6,7},{7,0},{8,9},{9,10},{10,1... | collective-permute-start | bytes 442376 | tf_op jit(solution)/shard_map/ppermute | solution.py:9
  34.5 7.3 %collective-permute-start.3 = (bf16[64,1152]{1,0:T(8,128)(2,1)S(1)}, bf16[64,1152]{1,0:T(8,128)(2,1)S(1)}, u32[]{:S(2)}, u32[]{:S(2)}) collective-permute-start(bf16[64,1152]{1,0:T(8,128)(2,1)S(1)} %collective-permute-done.2), channel_id=1, source_target_pairs={{0,1},{1,2},{2,3},{3,4},{4,5},{5,6},{6,7},{7,0},{8,9},{9,10},{10,1... | collective-permute-start | bytes 442376 | tf_op jit(solution)/shard_map/ppermute | solution.py:9
  41.8 8.2 %collective-permute-start.4 = (bf16[64,1152]{1,0:T(8,128)(2,1)S(1)}, bf16[64,1152]{1,0:T(8,128)(2,1)S(1)}, u32[]{:S(2)}, u32[]{:S(2)}) collective-permute-start(bf16[64,1152]{1,0:T(8,128)(2,1)S(1)} %collective-permute-done.3), channel_id=1, source_target_pairs={{0,1},{1,2},{2,3},{3,4},{4,5},{5,6},{6,7},{7,0},{8,9},{9,10},{10,1... | collective-permute-start | bytes 442376 | tf_op jit(solution)/shard_map/ppermute | solution.py:9
  50.0 8.4 %collective-permute-start.5 = (bf16[64,1152]{1,0:T(8,128)(2,1)S(1)}, bf16[64,1152]{1,0:T(8,128)(2,1)S(1)}, u32[]{:S(2)}, u32[]{:S(2)}) collective-permute-start(bf16[64,1152]{1,0:T(8,128)(2,1)S(1)} %collective-permute-done.4), channel_id=1, source_target_pairs={{0,1},{1,2},{2,3},{3,4},{4,5},{5,6},{6,7},{7,0},{8,9},{9,10},{10,1... | collective-permute-start | bytes 442376 | tf_op jit(solution)/shard_map/ppermute | solution.py:9
  58.3 69.6 %collective-permute-start.6 = (bf16[64,1152]{1,0:T(8,128)(2,1)S(1)}, bf16[64,1152]{1,0:T(8,128)(2,1)S(1)}, u32[]{:S(2)}, u32[]{:S(2)}) collective-permute-start(bf16[64,1152]{1,0:T(8,128)(2,1)S(1)} %collective-permute-done.5), channel_id=1, source_target_pairs={{0,1},{1,2},{2,3},{3,4},{4,5},{5,6},{6,7},{7,0},{8,9},{9,10},{10,1... | collective-permute-start | bytes 442376 | tf_op jit(solution)/shard_map/ppermute | solution.py:9
  103.7 5.5 %slice-start = ((s8[4718592]{0:T(1024)(128)(4,1)}), s8[4194304]{0:T(1024)(128)(4,1)S(1)}, s32[]{:S(2)}) async-start(s8[4718592]{0:T(1024)(128)(4,1)} %bitcast.75), calls=%async_computation.3 | async-start | bytes 8388608
  107.8 1.4 slice-start.1
  134.7 18.4 %slice-start.2 = ((s8[4718592]{0:T(1024)(128)(4,1)}), s8[524288]{0:T(1024)(128)(4,1)S(1)}, s32[]{:S(2)}) async-start(s8[4718592]{0:T(1024)(128)(4,1)} %bitcast.77), calls=%async_computation.5 | async-start | bytes 1048576
  134.7 18.4 %slice-start.3 = ((s8[4718592]{0:T(1024)(128)(4,1)}), s8[4194304]{0:T(1024)(128)(4,1)S(1)}, s32[]{:S(2)}) async-start(s8[4718592]{0:T(1024)(128)(4,1)} %bitcast.77), calls=%async_computation.6 | async-start | bytes 8388608
  138.1 11.4 %collective-permute-start.7 = (f32[64,1152]{1,0:T(8,128)S(1)}, f32[64,1152]{1,0:T(8,128)S(1)}, u32[]{:S(2)}, u32[]{:S(2)}) collective-permute-start(f32[64,1152]{1,0:T(8,128)S(1)} %convolution_multiply_fusion.7), channel_id=1, source_target_pairs={{0,1},{1,2},{2,3},{3,4},{4,5},{5,6},{6,7},{7,0},{8,9},{9,10},{10,1... | collective-permute-start | bytes 884744 | tf_op jit(solution)/shard_map/ppermute | solution.py:9
  153.0 10.6 %collective-permute-start.8 = (f32[64,1152]{1,0:T(8,128)S(1)}, f32[64,1152]{1,0:T(8,128)S(1)}, u32[]{:S(2)}, u32[]{:S(2)}) collective-permute-start(f32[64,1152]{1,0:T(8,128)S(1)} %fusion.1), channel_id=1, source_target_pairs={{0,1},{1,2},{2,3},{3,4},{4,5},{5,6},{6,7},{7,0},{8,9},{9,10},{10,1... | collective-permute-start | bytes 884744 | tf_op jit(solution)/shard_map/ppermute | solution.py:9
  163.6 9.7 %collective-permute-start.9 = (f32[64,1152]{1,0:T(8,128)S(1)}, f32[64,1152]{1,0:T(8,128)S(1)}, u32[]{:S(2)}, u32[]{:S(2)}) collective-permute-start(f32[64,1152]{1,0:T(8,128)S(1)} %add.355), channel_id=1, source_target_pairs={{0,1},{1,2},{2,3},{3,4},{4,5},{5,6},{6,7},{7,0},{8,9},{9,10},{10,1... | collective-permute-start | bytes 884744 | tf_op jit(solution)/shard_map/ppermute | solution.py:9
  173.3 8.9 %collective-permute-start.10 = (f32[64,1152]{1,0:T(8,128)S(1)}, f32[64,1152]{1,0:T(8,128)S(1)}, u32[]{:S(2)}, u32[]{:S(2)}) collective-permute-start(f32[64,1152]{1,0:T(8,128)S(1)} %add.356), channel_id=1, source_target_pairs={{0,1},{1,2},{2,3},{3,4},{4,5},{5,6},{6,7},{7,0},{8,9},{9,10},{10,1... | collective-permute-start | bytes 884744 | tf_op jit(solution)/shard_map/ppermute | solution.py:9
  182.2 9.0 %collective-permute-start.11 = (f32[64,1152]{1,0:T(8,128)S(1)}, f32[64,1152]{1,0:T(8,128)S(1)}, u32[]{:S(2)}, u32[]{:S(2)}) collective-permute-start(f32[64,1152]{1,0:T(8,128)S(1)} %add.357), channel_id=1, source_target_pairs={{0,1},{1,2},{2,3},{3,4},{4,5},{5,6},{6,7},{7,0},{8,9},{9,10},{10,1... | collective-permute-start | bytes 884744 | tf_op jit(solution)/shard_map/ppermute | solution.py:9
  191.3 10.3 %collective-permute-start.12 = (f32[64,1152]{1,0:T(8,128)S(1)}, f32[64,1152]{1,0:T(8,128)S(1)}, u32[]{:S(2)}, u32[]{:S(2)}) collective-permute-start(f32[64,1152]{1,0:T(8,128)S(1)} %add.358), channel_id=1, source_target_pairs={{0,1},{1,2},{2,3},{3,4},{4,5},{5,6},{6,7},{7,0},{8,9},{9,10},{10,1... | collective-permute-start | bytes 884744 | tf_op jit(solution)/shard_map/ppermute | solution.py:9
  192.6 29.3 %copy-start = (f32[64,1152]{1,0:T(8,128)S(1)}, f32[64,1152]{1,0:T(8,128)}, u32[]{:S(2)}) copy-start(f32[64,1152]{1,0:T(8,128)} %param.5) | copy-start | bytes 884740
  192.6 113.4 %copy-start.1 = (f32[64,1152]{1,0:T(8,128)S(1)}, f32[64,1152]{1,0:T(8,128)}, u32[]{:S(2)}) copy-start(f32[64,1152]{1,0:T(8,128)} %param.4) | copy-start | bytes 884740
  201.6 11.2 %collective-permute-start.13 = (f32[64,1152]{1,0:T(8,128)S(1)}, f32[64,1152]{1,0:T(8,128)S(1)}, u32[]{:S(2)}, u32[]{:S(2)}) collective-permute-start(f32[64,1152]{1,0:T(8,128)S(1)} %add.359), channel_id=1, source_target_pairs={{0,1},{1,2},{2,3},{3,4},{4,5},{5,6},{6,7},{7,0},{8,9},{9,10},{10,1... | collective-permute-start | bytes 884744 | tf_op jit(solution)/shard_map/ppermute | solution.py:9
  212.9 9.0 %collective-permute-start.14 = (f32[64,1152]{1,0:T(8,128)S(1)}, f32[64,1152]{1,0:T(8,128)S(1)}, u32[]{:S(2)}, u32[]{:S(2)}) collective-permute-start(f32[64,1152]{1,0:T(8,128)S(1)} %add.360), channel_id=1, source_target_pairs={{0,1},{1,2},{2,3},{3,4},{4,5},{5,6},{6,7},{7,0},{8,9},{9,10},{10,1... | collective-permute-start | bytes 884744 | tf_op jit(solution)/shard_map/ppermute | solution.py:9
Sparse Core Ops, SparseCore 0:
  11.3 92.3 all-gather.1
  134.8 171.0 reduce-scatter.1
where the time goes:
time: 317 us; the launch traced here: 316 us
  waiting for transfers between devices  245 us (77%)
  matrix products  43.2 us (14%)
  between operations  15.7 us (5%)
  other arithmetic  9.03 us (3%)
    ppermute x15, waiting for transfers between devices, shifted(): lax.ppermute(value, axis, [(i, (i + by) % length) for i in range(length)])  117 us
    reduce_scatter x1, waiting for transfers between devices, body(): lax.psum_scatter(d_wide, 'row', scatter_dimension=0, tiled=True)  83.1 us
    all_gather x1, waiting for transfers between devices, body(): wide = lax.all_gather(wide_local, 'row', axis=0, tiled=True)  45.4 us
    dot_general x8, matrix products, pair_tile(): lax.dot_general(weights, moving, (((0,), (0,)), ((), ())), preferred_elem...  15.5 us
    dot_general x8, matrix products, pair_tile(): lax.dot_general(moving, wide, (((1,), (1,)), ((), ())), preferred_element...  15.4 us
    dot_general x8, matrix products, pair_tile(): jnp.dot(weights, wide, preferred_element_type=jnp.float32)  12.4 us
  transfers between devices with their start and end apart: 17, of which 16 were waited for; matrix products, arithmetic and copies ran while one was open for 13% of the time, Pallas kernels for 0%

commit v1 on v0

v1 whole, which is shorter than its diff:
```python
import jax
import jax.numpy as jnp
from jax import lax
from jax.sharding import Mesh, PartitionSpec as P

AXES = ("z", "yh", "c", "yl", "x")
PLANE = ("yh", "yl", "x")
BF16 = jnp.bfloat16
F32 = jnp.float32


def shifted(value, axis, by):
    length = lax.axis_size(axis)
    return lax.ppermute(value, axis, [(i, (i + by) % length) for i in range(length)])


def normalize(raw):
    inv = lax.rsqrt(jnp.sum(raw * raw, axis=1, keepdims=True) + 1e-06)
    return ((raw * inv).astype(BF16), inv)


def unnormalize(raw, inv, grad):
    return inv * grad - raw * (inv * inv * inv) * jnp.sum(raw * grad, axis=1, keepdims=True)


def ring_gather(own):
    half = own.shape[0] // 2
    up, down, blocks = (own, own, [own])
    for _ in range(3):
        up, down = (shifted(up, "z", 1), shifted(down, "z", -1))
        blocks += [up, down]
    return blocks + [shifted(up[:half], "z", 1), shifted(down[half:], "z", -1)]


def added(a, b):
    return (a.astype(F32) + b.astype(F32)).astype(BF16)


def ring_scatter(blocks):
    own, m1, p1, m2, p2, m3, p3, far = blocks
    half = own.shape[0] // 2
    up = shifted(far[:half], "z", -1)
    down = shifted(far[half:], "z", 1)
    up = jnp.concatenate([added(m3[:half], up), m3[half:]], axis=0)
    down = jnp.concatenate([p3[:half], added(p3[half:], down)], axis=0)
    up, down = (shifted(up, "z", -1), shifted(down, "z", 1))
    up, down = (shifted(added(m2, up), "z", -1), shifted(added(p2, down), "z", 1))
    up, down = (shifted(added(m1, up), "z", -1), shifted(added(p1, down), "z", 1))
    return own.astype(F32) + up.astype(F32) + down.astype(F32)


def body(images, texts, logit_scale, logit_bias):
    rows, width = images.shape
    plane = lax.axis_size(PLANE)
    scale = logit_scale[0]
    bias = logit_bias[0]
    img_norm, img_inv = normalize(images)
    txt_norm, txt_inv = normalize(texts)

    copies = jnp.broadcast_to(txt_norm[None], (plane, rows, width))
    txt = lax.all_to_all(copies, PLANE, 0, 0, tiled=True).reshape(plane * rows, width)
    mine = jnp.concatenate(ring_gather(img_norm), axis=0)
    theirs = shifted(mine, "c", 1)
    img = jnp.concatenate([mine, theirs], axis=0)

    logits = (
        scale
        * lax.dot_general(txt, img, (((1,), (1,)), ((), ())), preferred_element_type=F32)
        + bias
    )
    place = lax.axis_index(PLANE) * rows
    txt_at = lax.broadcasted_iota(jnp.int32, logits.shape, 0)
    img_at = lax.broadcasted_iota(jnp.int32, logits.shape, 1)
    sign = jnp.where((txt_at - place == img_at) & (img_at < rows), 1.0, -1.0).astype(F32)
    weights = (-sign * jax.nn.sigmoid(-sign * logits)).astype(BF16)

    d_img = (
        scale * lax.dot_general(weights, txt, (((0,), (0,)), ((), ())), preferred_element_type=F32)
    )
    d_txt = (scale * jnp.dot(weights, img, preferred_element_type=F32)).astype(BF16)

    near = mine.shape[0]
    d_mine = d_img[:near] + shifted(d_img[near:].astype(BF16), "c", 1).astype(F32)
    d_mine = d_mine.astype(BF16)
    parts = lax.all_to_all(d_txt.reshape(plane, rows, width), PLANE, 0, 0, tiled=True)
    img_dir = ring_scatter([d_mine[i * rows : (i + 1) * rows] for i in range(near // rows)])
    txt_dir = jnp.sum(parts.astype(F32), axis=0)
    return (unnormalize(images, img_inv, img_dir), unnormalize(texts, txt_inv, txt_dir))


def solution(mesh):
    fine = Mesh(mesh.devices.reshape(8, 2, 2, 2, 4), AXES)
    rows = P(AXES, None)
    return jax.shard_map(
        body,
        mesh=fine,
        in_specs=(rows, rows, P(), P()),
        out_specs=(rows, rows),
        check_vma=False,
    )
```

time: 317 us -> 118 us (0.37)
  waiting for transfers between devices: 245 us -> 36.1 us
  starting transfers between devices: 2.59 us -> 40.7 us
  matrix products: 43.2 us -> 13.3 us
  between operations: 15.7 us -> 2.17 us
  local copies, waits for them, and re-layouts: 0.03 us -> 10.5 us
  other arithmetic: 9.03 us -> 13.5 us
    ppermute x15 -> x18, waiting for transfers between devices: 117 us -> 22.1 us  [shifted(): lax.ppermute(value, axis, [(i, (i + by) % length) for i in range(length)])]
    reduce_scatter x1 -> x0, waiting for transfers between devices: 83.1 us -> none  [body(): lax.psum_scatter(d_wide, 'row', scatter_dimension=0, tiled=True)]
    all_gather x1 -> x0, waiting for transfers between devices: 45.4 us -> none  [body(): wide = lax.all_gather(wide_local, 'row', axis=0, tiled=True)]
    dot_general x24 -> x3, matrix products: 43.2 us -> 13.3 us  [the longest x1 6.22 us: body(): lax.dot_general(txt, img, (((1,), (1,)), ((), ())), preferred_element_typ...]
    ppermute x15 -> x18, starting transfers between devices: 2.51 us -> 28.1 us  [shifted(): lax.ppermute(value, axis, [(i, (i + by) % length) for i in range(length)])]
    all_to_all x0 -> x2, waiting for transfers between devices: none -> 14 us  [the longest x1 7.96 us: body(): lax.all_to_all(copies, PLANE, 0, 0, tiled=True).reshape(plane * rows, width)]
    all_to_all x0 -> x2, starting transfers between devices: none -> 12.5 us  [the longest x1 7.39 us: body(): lax.all_to_all(copies, PLANE, 0, 0, tiled=True).reshape(plane * rows, width)]
    unnamed x12 -> x16, local copies, waits for them, and re-layouts: 0.03 us -> 6.19 us
  transfers between devices with their start and end apart: 17 -> 20, of which waited for: 16 -> 12; matrix products, arithmetic and copies ran while one was open for 13% -> 17% of each run, Pallas kernels for 0% -> 0%
where the time goes in v1:
time: 118 us; the launch traced here: 116 us
  starting transfers between devices  40.7 us (34%)
  waiting for transfers between devices  36.1 us (31%)
  other arithmetic  13.5 us (11%)
  matrix products  13.3 us (11%)
  local copies, waits for them, and re-layouts  10.5 us (9%)
  between operations  2.17 us (2%)
    ppermute x18, starting transfers between devices, shifted(): lax.ppermute(value, axis, [(i, (i + by) % length) for i in range(length)])  28.1 us
    ppermute x18, waiting for transfers between devices, shifted(): lax.ppermute(value, axis, [(i, (i + by) % length) for i in range(length)])  22.1 us
    all_to_all x1, waiting for transfers between devices, body(): lax.all_to_all(copies, PLANE, 0, 0, tiled=True).reshape(plane * rows, width)  7.96 us
    all_to_all x1, starting transfers between devices, body(): lax.all_to_all(copies, PLANE, 0, 0, tiled=True).reshape(plane * rows, width)  7.39 us
    dot_general x1, matrix products, body(): lax.dot_general(txt, img, (((1,), (1,)), ((), ())), preferred_element_typ...  6.22 us
    unnamed x16, local copies, waits for them, and re-layouts  6.19 us
    all_to_all x1, waiting for transfers between devices, body(): lax.all_to_all(d_txt.reshape(plane, rows, width), PLANE, 0, 0, tiled=True)  6.01 us
    all_to_all x1, starting transfers between devices, body(): lax.all_to_all(d_txt.reshape(plane, rows, width), PLANE, 0, 0, tiled=True)  5.14 us
  transfers between devices with their start and end apart: 20, of which 12 were waited for; matrix products, arithmetic and copies ran while one was open for 17% of the time, Pallas kernels for 0%

profile of v1, /device:TPU:8, one launch (start us, length us, event | category | flops | bytes accessed | tf_op | source)
XLA Modules:
  0.0 116.3 jit_solution(5218564854847353042)
XLA Ops:
  1.7 1.7 %constant_dynamic-update-slice_fusion.8 = (bf16[512,1152]{1,0:T(8,128)(2,1)}, bf16[64,1152]{1,0:T(8,128)(2,1)S(1)}) fusion(f32[64,1152]{1,0:T(8,128)} %param.4, f32[64]{0:T(128)S(1)} %get-tuple-element.31), kind=kLoop, calls=%fused_computation.35 | loop fusion | flops 147455 | bytes 590080
  3.4 1.9 %collective-permute-start = (bf16[64,1152]{1,0:T(8,128)(2,1)S(1)}, bf16[64,1152]{1,0:T(8,128)(2,1)S(1)}, u32[]{:S(2)}, u32[]{:S(2)}) collective-permute-start(bf16[64,1152]{1,0:T(8,128)(2,1)S(1)} %get-tuple-element.3), channel_id=1, source_target_pairs={{0,32},{32,64},{64,96},{96,128},{128,160},{160,192},{192,224},{224... | collective-permute-start | bytes 442376 | tf_op jit(solution)/shard_map/ppermute | solution.py:14
  5.4 3.9 %collective-permute-start.1 = (bf16[64,1152]{1,0:T(8,128)(2,1)S(1)}, bf16[64,1152]{1,0:T(8,128)(2,1)S(1)}, u32[]{:S(2)}, u32[]{:S(2)}) collective-permute-start(bf16[64,1152]{1,0:T(8,128)(2,1)S(1)} %get-tuple-element.3), channel_id=1, source_target_pairs={{0,224},{32,0},{64,32},{96,64},{128,96},{160,128},{192,160},{224,1... | collective-permute-start | bytes 442376 | tf_op jit(solution)/shard_map/ppermute | solution.py:14
  12.0 1.7 %broadcast_in_dim.20 = bf16[16,64,1152]{2,1,0:T(8,128)(2,1)} broadcast(bf16[64,1152]{1,0:T(8,128)(2,1)S(1)} %multiply_convert_fusion.2), dimensions={1,2} | broadcast | bytes 2506752 | tf_op jit(solution)/shard_map/broadcast_in_dim | solution.py:60
  13.8 7.4 %all-to-all-start = ((bf16[16,64,1152]{2,1,0:T(8,128)(2,1)}), bf16[16,64,1152]{2,1,0:T(8,128)(2,1)S(1)}, u32[]{:S(2)}, u32[]{:S(2)}) async-start(bf16[16,64,1152]{2,1,0:T(8,128)(2,1)} %broadcast_in_dim.20), calls=%async_computation | async-start | bytes 4718592 | tf_op jit(solution)/shard_map/all_to_all | solution.py:61
  21.3 3.2 %collective-permute-start.3 = (bf16[64,1152]{1,0:T(8,128)(2,1)S(1)}, bf16[64,1152]{1,0:T(8,128)(2,1)S(1)}, u32[]{:S(2)}, u32[]{:S(2)}) collective-permute-start(bf16[64,1152]{1,0:T(8,128)(2,1)S(1)} %collective-permute-done.1), channel_id=1, source_target_pairs={{0,224},{32,0},{64,32},{96,64},{128,96},{160,128},{192,160},{224,1... | collective-permute-start | bytes 442376 | tf_op jit(solution)/shard_map/ppermute | solution.py:14
  25.9 1.8 %collective-permute-done.2 = bf16[64,1152]{1,0:T(8,128)(2,1)S(1)} collective-permute-done((bf16[64,1152]{1,0:T(8,128)(2,1)S(1)}, bf16[64,1152]{1,0:T(8,128)(2,1)S(1)}, u32[]{:S(2)}, u32[]{:S(2)}) %collective-permute-start.2) | collective-permute-done | bytes 147488 | tf_op jit(solution)/shard_map/ppermute | solution.py:14
  27.6 3.2 %collective-permute-start.5 = (bf16[64,1152]{1,0:T(8,128)(2,1)S(1)}, bf16[64,1152]{1,0:T(8,128)(2,1)S(1)}, u32[]{:S(2)}, u32[]{:S(2)}) collective-permute-start(bf16[64,1152]{1,0:T(8,128)(2,1)S(1)} %collective-permute-done.3), channel_id=1, source_target_pairs={{0,224},{32,0},{64,32},{96,64},{128,96},{160,128},{192,160},{224,1... | collective-permute-start | bytes 442376 | tf_op jit(solution)/shard_map/ppermute | solution.py:14
  32.3 1.7 %collective-permute-done.4 = bf16[64,1152]{1,0:T(8,128)(2,1)S(1)} collective-permute-done((bf16[64,1152]{1,0:T(8,128)(2,1)S(1)}, bf16[64,1152]{1,0:T(8,128)(2,1)S(1)}, u32[]{:S(2)}, u32[]{:S(2)}) %collective-permute-start.4) | collective-permute-done | bytes 147488 | tf_op jit(solution)/shard_map/ppermute | solution.py:14
  34.0 3.3 %collective-permute-start.7 = (bf16[32,1152]{1,0:T(8,128)(2,1)S(1)}, bf16[32,1152]{1,0:T(8,128)(2,1)S(1)}, u32[]{:S(2)}, u32[]{:S(2)}) collective-permute-start(bf16[32,1152]{1,0:T(8,128)(2,1)S(1)} %slice.71), channel_id=1, source_target_pairs={{0,224},{32,0},{64,32},{96,64},{128,96},{160,128},{192,160},{224,1... | collective-permute-start | bytes 221192 | tf_op jit(solution)/shard_map/ppermute | solution.py:14
  46.5 8.0 %all-to-all-done = bf16[16,64,1152]{2,1,0:T(8,128)(2,1)S(1)} async-done(((bf16[16,64,1152]{2,1,0:T(8,128)(2,1)}), bf16[16,64,1152]{2,1,0:T(8,128)(2,1)S(1)}, u32[]{:S(2)}, u32[]{:S(2)}) %all-to-all-start) | async-done | bytes 2359328 | tf_op jit(solution)/shard_map/all_to_all | solution.py:61
  54.4 6.2 %multiply_convert_fusion = bf16[1024,1024]{1,0:T(8,128)(2,1)S(1)} fusion(bf16[1024,1152]{1,0:T(8,128)(2,1)S(1)} %bitcast.14, bf16[1024,1152]{1,0:T(8,128)(2,1)} %constant_dynamic-update-slice_fusion.9, f32[]{:T(128)} %bitcast.13, f32[]{:T(128)} %bitcast.11, s32[1024]{0:T(1024)S(1)} %iota_subtract_fusion, pred[1024]{0:T(1024)(128)(4,1)} %iota_compare_fusion.1), kind=kOutput, calls=%fused_computation.3 | convolution fusion | flops 2428502016 | bytes 6820872 | tf_op jit(solution)/shard_map/dot_general | solution.py:68
  60.6 3.0 %convolution_multiply_fusion.1 = f32[1024,1152]{1,0:T(8,128)S(1)} fusion(bf16[1024,1024]{1,0:T(8,128)(2,1)S(1)} %multiply_convert_fusion, bf16[1024,1152]{1,0:T(8,128)(2,1)S(1)} %bitcast.15, f32[]{:T(128)} %bitcast.10), kind=kOutput, calls=%fused_computation.1 | convolution fusion | flops 2417098752 | bytes 9175044 | tf_op jit(solution)/shard_map/dot_general | solution.py:78
  63.9 2.8 %collective-permute-done.9 = bf16[512,1152]{1,0:T(8,128)(2,1)S(1)} collective-permute-done((bf16[512,1152]{1,0:T(8,128)(2,1)S(1)}, bf16[512,1152]{1,0:T(8,128)(2,1)S(1)}, u32[]{:S(2)}, u32[]{:S(2)}) %collective-permute-start.9) | collective-permute-done | bytes 1179680 | tf_op jit(solution)/shard_map/ppermute | solution.py:14
  69.7 4.1 %fusion.1 = bf16[1024,1152]{1,0:T(8,128)(2,1)} fusion(bf16[1024,1024]{1,0:T(8,128)(2,1)S(1)} %multiply_convert_fusion, bf16[1024,1152]{1,0:T(8,128)(2,1)S(1)} %copy-done.2, f32[]{:T(128)} %bitcast.12), kind=kOutput, calls=%fused_computation.6 | convolution fusion | flops 2418278400 | bytes 6815748 | tf_op jit(solution)/shard_map/dot_general | solution.py:80
  73.8 5.1 %all-to-all-start.1 = ((bf16[16,64,1152]{2,1,0:T(8,128)(2,1)}), bf16[16,64,1152]{2,1,0:T(8,128)(2,1)S(1)}, u32[]{:S(2)}, u32[]{:S(2)}) async-start(bf16[16,64,1152]{2,1,0:T(8,128)(2,1)} %bitcast.16), calls=%async_computation.1 | async-start | bytes 4718592 | tf_op jit(solution)/shard_map/all_to_all | solution.py:85
  80.8 2.6 %collective-permute-start.11 = (bf16[64,1152]{1,0:T(8,128)(2,1)S(1)}, bf16[64,1152]{1,0:T(8,128)(2,1)S(1)}, u32[]{:S(2)}, u32[]{:S(2)}) collective-permute-start(bf16[64,1152]{1,0:T(8,128)(2,1)S(1)} %pad_maximum_fusion), channel_id=1, source_target_pairs={{0,224},{32,0},{64,32},{96,64},{128,96},{160,128},{192,160},{224,1... | collective-permute-start | bytes 442376 | tf_op jit(solution)/shard_map/ppermute | solution.py:14
  86.1 3.8 %collective-permute-start.12 = (bf16[64,1152]{1,0:T(8,128)(2,1)S(1)}, bf16[64,1152]{1,0:T(8,128)(2,1)S(1)}, u32[]{:S(2)}, u32[]{:S(2)}) collective-permute-start(bf16[64,1152]{1,0:T(8,128)(2,1)S(1)} %add_convert_fusion.3), channel_id=1, source_target_pairs={{0,224},{32,0},{64,32},{96,64},{128,96},{160,128},{192,160},{224,1... | collective-permute-start | bytes 442376 | tf_op jit(solution)/shard_map/ppermute | solution.py:14
  90.7 1.8 %collective-permute-done.12 = bf16[64,1152]{1,0:T(8,128)(2,1)S(1)} collective-permute-done((bf16[64,1152]{1,0:T(8,128)(2,1)S(1)}, bf16[64,1152]{1,0:T(8,128)(2,1)S(1)}, u32[]{:S(2)}, u32[]{:S(2)}) %collective-permute-start.12) | collective-permute-done | bytes 147488 | tf_op jit(solution)/shard_map/ppermute | solution.py:14
  92.7 3.8 %collective-permute-start.13 = (bf16[64,1152]{1,0:T(8,128)(2,1)S(1)}, bf16[64,1152]{1,0:T(8,128)(2,1)S(1)}, u32[]{:S(2)}, u32[]{:S(2)}) collective-permute-start(bf16[64,1152]{1,0:T(8,128)(2,1)S(1)} %get-tuple-element.4), channel_id=1, source_target_pairs={{0,224},{32,0},{64,32},{96,64},{128,96},{160,128},{192,160},{224,1... | collective-permute-start | bytes 442376 | tf_op jit(solution)/shard_map/ppermute | solution.py:14
  96.5 3.0 %collective-permute-done.16 = bf16[64,1152]{1,0:T(8,128)(2,1)S(1)} collective-permute-done((bf16[64,1152]{1,0:T(8,128)(2,1)S(1)}, bf16[64,1152]{1,0:T(8,128)(2,1)S(1)}, u32[]{:S(2)}, u32[]{:S(2)}) %collective-permute-start.16) | collective-permute-done | bytes 147488 | tf_op jit(solution)/shard_map/ppermute | solution.py:14
  99.7 6.3 %collective-permute-done.17 = bf16[64,1152]{1,0:T(8,128)(2,1)S(1)} collective-permute-done((bf16[64,1152]{1,0:T(8,128)(2,1)S(1)}, bf16[64,1152]{1,0:T(8,128)(2,1)S(1)}, u32[]{:S(2)}, u32[]{:S(2)}) %collective-permute-start.17) | collective-permute-done | bytes 147488 | tf_op jit(solution)/shard_map/ppermute | solution.py:14
  107.0 6.0 %all-to-all-done.1 = bf16[16,64,1152]{2,1,0:T(8,128)(2,1)S(1)} async-done(((bf16[16,64,1152]{2,1,0:T(8,128)(2,1)}), bf16[16,64,1152]{2,1,0:T(8,128)(2,1)S(1)}, u32[]{:S(2)}, u32[]{:S(2)}) %all-to-all-start.1) | async-done | bytes 2359328 | tf_op jit(solution)/shard_map/all_to_all | solution.py:85
  114.5 1.8 %multiply_subtract_fusion = f32[64,1152]{1,0:T(8,128)} fusion(f32[64,1152]{1,0:T(8,128)} %param.5, f32[64,1152]{1,0:T(8,128)S(1)} %convert_reduce_fusion, f32[64]{0:T(128)S(1)} %multiply_reduce_fusion, f32[64]{0:T(128)S(1)} %copy-done.3, f32[64]{0:T(128)S(1)} %get-tuple-element.29), kind=kLoop, calls=%fused_computation.10 | loop fusion | flops 294912 | bytes 885504 | tf_op jit(solution)/shard_map/sub | solution.py:23
  (62 shorter events, 25.9 us)
Async XLA Ops:
  3.4 17.8 %collective-permute-start = (bf16[64,1152]{1,0:T(8,128)(2,1)S(1)}, bf16[64,1152]{1,0:T(8,128)(2,1)S(1)}, u32[]{:S(2)}, u32[]{:S(2)}) collective-permute-start(bf16[64,1152]{1,0:T(8,128)(2,1)S(1)} %get-tuple-element.3), channel_id=1, source_target_pairs={{0,32},{32,64},{64,96},{96,128},{128,160},{160,192},{192,224},{224... | collective-permute-start | bytes 442376 | tf_op jit(solution)/shard_map/ppermute | solution.py:14
  5.4 15.9 %collective-permute-start.1 = (bf16[64,1152]{1,0:T(8,128)(2,1)S(1)}, bf16[64,1152]{1,0:T(8,128)(2,1)S(1)}, u32[]{:S(2)}, u32[]{:S(2)}) collective-permute-start(bf16[64,1152]{1,0:T(8,128)(2,1)S(1)} %get-tuple-element.3), channel_id=1, source_target_pairs={{0,224},{32,0},{64,32},{96,64},{128,96},{160,128},{192,160},{224,1... | collective-permute-start | bytes 442376 | tf_op jit(solution)/shard_map/ppermute | solution.py:14
  13.8 40.6 %all-to-all-start = ((bf16[16,64,1152]{2,1,0:T(8,128)(2,1)}), bf16[16,64,1152]{2,1,0:T(8,128)(2,1)S(1)}, u32[]{:S(2)}, u32[]{:S(2)}) async-start(bf16[16,64,1152]{2,1,0:T(8,128)(2,1)} %broadcast_in_dim.20), calls=%async_computation | async-start | bytes 4718592 | tf_op jit(solution)/shard_map/all_to_all | solution.py:61
  21.2 6.4 %collective-permute-start.2 = (bf16[64,1152]{1,0:T(8,128)(2,1)S(1)}, bf16[64,1152]{1,0:T(8,128)(2,1)S(1)}, u32[]{:S(2)}, u32[]{:S(2)}) collective-permute-start(bf16[64,1152]{1,0:T(8,128)(2,1)S(1)} %collective-permute-done), channel_id=1, source_target_pairs={{0,32},{32,64},{64,96},{96,128},{128,160},{160,192},{192,224},{224... | collective-permute-start | bytes 442376 | tf_op jit(solution)/shard_map/ppermute | solution.py:14
  21.3 6.3 %collective-permute-start.3 = (bf16[64,1152]{1,0:T(8,128)(2,1)S(1)}, bf16[64,1152]{1,0:T(8,128)(2,1)S(1)}, u32[]{:S(2)}, u32[]{:S(2)}) collective-permute-start(bf16[64,1152]{1,0:T(8,128)(2,1)S(1)} %collective-permute-done.1), channel_id=1, source_target_pairs={{0,224},{32,0},{64,32},{96,64},{128,96},{160,128},{192,160},{224,1... | collective-permute-start | bytes 442376 | tf_op jit(solution)/shard_map/ppermute | solution.py:14
  27.6 6.4 %collective-permute-start.4 = (bf16[64,1152]{1,0:T(8,128)(2,1)S(1)}, bf16[64,1152]{1,0:T(8,128)(2,1)S(1)}, u32[]{:S(2)}, u32[]{:S(2)}) collective-permute-start(bf16[64,1152]{1,0:T(8,128)(2,1)S(1)} %collective-permute-done.2), channel_id=1, source_target_pairs={{0,32},{32,64},{64,96},{96,128},{128,160},{160,192},{192,224},{224... | collective-permute-start | bytes 442376 | tf_op jit(solution)/shard_map/ppermute | solution.py:14
  27.6 6.4 %collective-permute-start.5 = (bf16[64,1152]{1,0:T(8,128)(2,1)S(1)}, bf16[64,1152]{1,0:T(8,128)(2,1)S(1)}, u32[]{:S(2)}, u32[]{:S(2)}) collective-permute-start(bf16[64,1152]{1,0:T(8,128)(2,1)S(1)} %collective-permute-done.3), channel_id=1, source_target_pairs={{0,224},{32,0},{64,32},{96,64},{128,96},{160,128},{192,160},{224,1... | collective-permute-start | bytes 442376 | tf_op jit(solution)/shard_map/ppermute | solution.py:14
  34.0 5.6 %collective-permute-start.6 = (bf16[32,1152]{1,0:T(8,128)(2,1)S(1)}, bf16[32,1152]{1,0:T(8,128)(2,1)S(1)}, u32[]{:S(2)}, u32[]{:S(2)}) collective-permute-start(bf16[32,1152]{1,0:T(8,128)(2,1)S(1)} %slice.70), channel_id=1, source_target_pairs={{0,32},{32,64},{64,96},{96,128},{128,160},{160,192},{192,224},{224... | collective-permute-start | bytes 221192 | tf_op jit(solution)/shard_map/ppermute | solution.py:14
  34.0 6.2 %collective-permute-start.7 = (bf16[32,1152]{1,0:T(8,128)(2,1)S(1)}, bf16[32,1152]{1,0:T(8,128)(2,1)S(1)}, u32[]{:S(2)}, u32[]{:S(2)}) collective-permute-start(bf16[32,1152]{1,0:T(8,128)(2,1)S(1)} %slice.71), channel_id=1, source_target_pairs={{0,224},{32,0},{64,32},{96,64},{128,96},{160,128},{192,160},{224,1... | collective-permute-start | bytes 221192 | tf_op jit(solution)/shard_map/ppermute | solution.py:14
  40.8 1.4 %copy-start.1 = (bf16[1024,1152]{1,0:T(8,128)(2,1)}, bf16[1024,1152]{1,0:T(8,128)(2,1)S(1)}, u32[]{:S(2)}) copy-start(bf16[1024,1152]{1,0:T(8,128)(2,1)S(1)} %get-tuple-element.25) | copy-start | bytes 7077892
  42.3 3.1 %collective-permute-start.8 = (bf16[512,1152]{1,0:T(8,128)(2,1)}, bf16[512,1152]{1,0:T(8,128)(2,1)S(1)}, u32[]{:S(2)}, u32[]{:S(2)}) collective-permute-start(bf16[512,1152]{1,0:T(8,128)(2,1)} %get-tuple-element.24), channel_id=1, source_target_pairs={{0,8},{8,0},{1,9},{9,1},{2,10},{10,2},{3,11},{11,3},{4,12},{12,4},... | collective-permute-start | bytes 3538952 | tf_op jit(solution)/shard_map/ppermute | solution.py:14
  63.8 5.9 %copy-start.2 = (bf16[1024,1152]{1,0:T(8,128)(2,1)S(1)}, bf16[1024,1152]{1,0:T(8,128)(2,1)}, u32[]{:S(2)}) copy-start(bf16[1024,1152]{1,0:T(8,128)(2,1)} %constant_dynamic-update-slice_fusion.9) | copy-start | bytes 7077892
  63.8 2.9 %collective-permute-start.9 = (bf16[512,1152]{1,0:T(8,128)(2,1)S(1)}, bf16[512,1152]{1,0:T(8,128)(2,1)S(1)}, u32[]{:S(2)}, u32[]{:S(2)}) collective-permute-start(bf16[512,1152]{1,0:T(8,128)(2,1)S(1)} %slice.97), channel_id=1, source_target_pairs={{0,8},{8,0},{1,9},{9,1},{2,10},{10,2},{3,11},{11,3},{4,12},{12,4},... | collective-permute-start | bytes 3538952 | tf_op jit(solution)/shard_map/ppermute | solution.py:14
  67.7 11.3 %collective-permute-start.10 = (bf16[32,1152]{1,0:T(8,128)(2,1)}, bf16[32,1152]{1,0:T(8,128)(2,1)}, u32[]{:S(2)}, u32[]{:S(2)}) collective-permute-start(bf16[32,1152]{1,0:T(8,128)(2,1)} %get-tuple-element.8), channel_id=1, source_target_pairs={{0,224},{32,0},{64,32},{96,64},{128,96},{160,128},{192,160},{224,1... | collective-permute-start | bytes 221192 | tf_op jit(solution)/shard_map/ppermute | solution.py:14
  68.7 10.2 %collective-permute-start.14 = (bf16[32,1152]{1,0:T(8,128)(2,1)}, bf16[32,1152]{1,0:T(8,128)(2,1)}, u32[]{:S(2)}, u32[]{:S(2)}) collective-permute-start(bf16[32,1152]{1,0:T(8,128)(2,1)} %get-tuple-element.9), channel_id=1, source_target_pairs={{0,32},{32,64},{64,96},{96,128},{128,160},{160,192},{192,224},{224... | collective-permute-start | bytes 221192 | tf_op jit(solution)/shard_map/ppermute | solution.py:14
  73.8 39.2 %all-to-all-start.1 = ((bf16[16,64,1152]{2,1,0:T(8,128)(2,1)}), bf16[16,64,1152]{2,1,0:T(8,128)(2,1)S(1)}, u32[]{:S(2)}, u32[]{:S(2)}) async-start(bf16[16,64,1152]{2,1,0:T(8,128)(2,1)} %bitcast.16), calls=%async_computation.1 | async-start | bytes 4718592 | tf_op jit(solution)/shard_map/all_to_all | solution.py:85
  78.9 27.1 %copy-start = (f32[64,1152]{1,0:T(8,128)S(1)}, f32[64,1152]{1,0:T(8,128)}, u32[]{:S(2)}) copy-start(f32[64,1152]{1,0:T(8,128)} %param.4) | copy-start | bytes 884740
  80.8 5.2 %collective-permute-start.11 = (bf16[64,1152]{1,0:T(8,128)(2,1)S(1)}, bf16[64,1152]{1,0:T(8,128)(2,1)S(1)}, u32[]{:S(2)}, u32[]{:S(2)}) collective-permute-start(bf16[64,1152]{1,0:T(8,128)(2,1)S(1)} %pad_maximum_fusion), channel_id=1, source_target_pairs={{0,224},{32,0},{64,32},{96,64},{128,96},{160,128},{192,160},{224,1... | collective-permute-start | bytes 442376 | tf_op jit(solution)/shard_map/ppermute | solution.py:14
  84.3 6.4 %collective-permute-start.15 = (bf16[64,1152]{1,0:T(8,128)(2,1)S(1)}, bf16[64,1152]{1,0:T(8,128)(2,1)S(1)}, u32[]{:S(2)}, u32[]{:S(2)}) collective-permute-start(bf16[64,1152]{1,0:T(8,128)(2,1)S(1)} %pad_maximum_fusion.1), channel_id=1, source_target_pairs={{0,32},{32,64},{64,96},{96,128},{128,160},{160,192},{192,224},{224... | collective-permute-start | bytes 442376 | tf_op jit(solution)/shard_map/ppermute | solution.py:14
  86.1 6.4 %collective-permute-start.12 = (bf16[64,1152]{1,0:T(8,128)(2,1)S(1)}, bf16[64,1152]{1,0:T(8,128)(2,1)S(1)}, u32[]{:S(2)}, u32[]{:S(2)}) collective-permute-start(bf16[64,1152]{1,0:T(8,128)(2,1)S(1)} %add_convert_fusion.3), channel_id=1, source_target_pairs={{0,224},{32,0},{64,32},{96,64},{128,96},{160,128},{192,160},{224,1... | collective-permute-start | bytes 442376 | tf_op jit(solution)/shard_map/ppermute | solution.py:14
  92.6 6.9 %collective-permute-start.16 = (bf16[64,1152]{1,0:T(8,128)(2,1)S(1)}, bf16[64,1152]{1,0:T(8,128)(2,1)S(1)}, u32[]{:S(2)}, u32[]{:S(2)}) collective-permute-start(bf16[64,1152]{1,0:T(8,128)(2,1)S(1)} %get-tuple-element.5), channel_id=1, source_target_pairs={{0,32},{32,64},{64,96},{96,128},{128,160},{160,192},{192,224},{224... | collective-permute-start | bytes 442376 | tf_op jit(solution)/shard_map/ppermute | solution.py:14
  92.7 6.9 %collective-permute-start.13 = (bf16[64,1152]{1,0:T(8,128)(2,1)S(1)}, bf16[64,1152]{1,0:T(8,128)(2,1)S(1)}, u32[]{:S(2)}, u32[]{:S(2)}) collective-permute-start(bf16[64,1152]{1,0:T(8,128)(2,1)S(1)} %get-tuple-element.4), channel_id=1, source_target_pairs={{0,224},{32,0},{64,32},{96,64},{128,96},{160,128},{192,160},{224,1... | collective-permute-start | bytes 442376 | tf_op jit(solution)/shard_map/ppermute | solution.py:14
  99.6 14.9 %copy-start.3 = (f32[64]{0:T(128)S(1)}, f32[64]{0:T(128)}, u32[]{:S(2)}) copy-start(f32[64]{0:T(128)} %get-tuple-element.28) | copy-start | bytes 772
  99.6 6.4 %collective-permute-start.17 = (bf16[64,1152]{1,0:T(8,128)(2,1)S(1)}, bf16[64,1152]{1,0:T(8,128)(2,1)S(1)}, u32[]{:S(2)}, u32[]{:S(2)}) collective-permute-start(bf16[64,1152]{1,0:T(8,128)(2,1)S(1)} %add_convert_fusion), channel_id=1, source_target_pairs={{0,32},{32,64},{64,96},{96,128},{128,160},{160,192},{192,224},{224... | collective-permute-start | bytes 442376 | tf_op jit(solution)/shard_map/ppermute | solution.py:14

commit v2 on v1

--- a/solution.py
+++ b/solution.py
@@ -1,12 +1,31 @@
 import jax
 import jax.numpy as jnp
 from jax import lax
+from jax.experimental import pallas as pl
+from jax.experimental.pallas import tpu as pltpu
 from jax.sharding import Mesh, PartitionSpec as P
 
 AXES = ("z", "yh", "c", "yl", "x")
-PLANE = ("yh", "yl", "x")
+PLANE = ("yh", "c", "yl", "x")
 BF16 = jnp.bfloat16
 F32 = jnp.float32
+
+
+VMEM = pl.BlockSpec(memory_space=pltpu.VMEM)
+
+
+def plane_groups():
+    at = lambda y, c, x: ((y // 2 * 2 + c) * 2 + y % 2) * 4 + x
+    along_x = [[[at(y, c, x) for x in range(4)] for y in range(4)] for c in range(2)]
+    along_y = [[[at(y, c, x) for y in range(4)] for x in range(4)] for c in range(2)]
+    return (along_x[0] + along_y[1], along_y[0] + along_x[1])
+
+
+FIRST, SECOND = plane_groups()
+
+
+def exchanged(blocks, groups):
+    return lax.all_to_all(blocks, PLANE, 0, 0, tiled=True, axis_index_groups=groups)
 
 
 def shifted(value, axis, by):
@@ -14,12 +33,31 @@
     return lax.ppermute(value, axis, [(i, (i + by) % length) for i in range(length)])
 
 
-def normalize(raw):
-    inv = lax.rsqrt(jnp.sum(raw * raw, axis=1, keepdims=True) + 1e-06)
-    return ((raw * inv).astype(BF16), inv)
+def normalize_kernel(img_ref, txt_ref, img_out, txt_out):
+    def norm(raw):
+        inv = lax.rsqrt(jnp.sum(raw * raw, axis=1, keepdims=True) + 1e-06)
+        return (raw * inv).astype(BF16)
+
+    txt = norm(txt_ref[...])
+    for i in range(txt_out.shape[0]):
+        txt_out[i] = txt
+    img_out[...] = norm(img_ref[...])
 
 
-def unnormalize(raw, inv, grad):
+def normalize(images, texts, copies):
+    return pl.pallas_call(
+        normalize_kernel,
+        out_shape=(
+            jax.ShapeDtypeStruct(images.shape, BF16),
+            jax.ShapeDtypeStruct((copies, *texts.shape), BF16),
+        ),
+        in_specs=[VMEM, VMEM],
+        out_specs=(VMEM, VMEM),
+    )(images, texts)
+
+
+def unnormalize(raw, grad):
+    inv = lax.rsqrt(jnp.sum(raw * raw, axis=1, keepdims=True) + 1e-06)
     return inv * grad - raw * (inv * inv * inv) * jnp.sum(raw * grad, axis=1, keepdims=True)
 
 
@@ -51,14 +89,14 @@
 
 def body(images, texts, logit_scale, logit_bias):
     rows, width = images.shape
-    plane = lax.axis_size(PLANE)
+    line = len(FIRST[0])
     scale = logit_scale[0]
     bias = logit_bias[0]
-    img_norm, img_inv = normalize(images)
-    txt_norm, txt_inv = normalize(texts)
+    img_norm, txt_copies = normalize(images, texts, line)
 
-    copies = jnp.broadcast_to(txt_norm[None], (plane, rows, width))
-    txt = lax.all_to_all(copies, PLANE, 0, 0, tiled=True).reshape(plane * rows, width)
+    txt = exchanged(txt_copies, FIRST).reshape(1, line * rows, width)
+    txt = jnp.broadcast_to(txt, (line, line * rows, width))
+    txt = exchanged(txt, SECOND).reshape(line * line * rows, width)
     mine = jnp.concatenate(ring_gather(img_norm), axis=0)
     theirs = shifted(mine, "c", 1)
     img = jnp.concatenate([mine, theirs], axis=0)
@@ -68,7 +106,9 @@
         * lax.dot_general(txt, img, (((1,), (1,)), ((), ())), preferred_element_type=F32)
         + bias
     )
-    place = lax.axis_index(PLANE) * rows
+    core, x = (lax.axis_index("c"), lax.axis_index("x"))
+    y = lax.axis_index(("yh", "yl"))
+    place = jnp.where(core == 0, y * line + x, x * line + y) * rows
     txt_at = lax.broadcasted_iota(jnp.int32, logits.shape, 0)
     img_at = lax.broadcasted_iota(jnp.int32, logits.shape, 1)
     sign = jnp.where((txt_at - place == img_at) & (img_at < rows), 1.0, -1.0).astype(F32)
@@ -82,10 +122,12 @@
     near = mine.shape[0]
     d_mine = d_img[:near] + shifted(d_img[near:].astype(BF16), "c", 1).astype(F32)
     d_mine = d_mine.astype(BF16)
-    parts = lax.all_to_all(d_txt.reshape(plane, rows, width), PLANE, 0, 0, tiled=True)
+    parts = exchanged(d_txt.reshape(line, line * rows, width), SECOND)
+    parts = jnp.sum(parts.astype(F32), axis=0).astype(BF16)
+    parts = exchanged(parts.reshape(line, rows, width), FIRST)
     img_dir = ring_scatter([d_mine[i * rows : (i + 1) * rows] for i in range(near // rows)])
     txt_dir = jnp.sum(parts.astype(F32), axis=0)
-    return (unnormalize(images, img_inv, img_dir), unnormalize(texts, txt_inv, txt_dir))
+    return (unnormalize(images, img_dir), unnormalize(texts, txt_dir))
 
 
 def solution(mesh):

time: 118 us -> 118 us (level)
  the two profiles are of different devices: /device:TPU:8 before, /device:TPU:112 now
where the time goes in v2:
time: 118 us; the launch traced here: 117 us
  starting transfers between devices  46.1 us (39%)
  waiting for transfers between devices  33.1 us (28%)
  matrix products  13.3 us (11%)
  local copies, waits for them, and re-layouts  10.7 us (9%)
  other arithmetic  10 us (8%)
  between operations  2.09 us (2%)
  Pallas kernels  2.04 us (2%)
    ppermute x18, starting transfers between devices, shifted(): lax.ppermute(value, axis, [(i, (i + by) % length) for i in range(length)])  24.8 us
    all_to_all x4, starting transfers between devices, exchanged(): lax.all_to_all(blocks, PLANE, 0, 0, tiled=True, axis_index_groups=groups)  21.3 us
    ppermute x18, waiting for transfers between devices, shifted(): lax.ppermute(value, axis, [(i, (i + by) % length) for i in range(length)])  19.9 us
    all_to_all x4, waiting for transfers between devices, exchanged(): lax.all_to_all(blocks, PLANE, 0, 0, tiled=True, axis_index_groups=groups)  13.2 us
    unnamed x14, local copies, waits for them, and re-layouts  6.48 us
    dot_general x1, matrix products, body(): lax.dot_general(txt, img, (((1,), (1,)), ((), ())), preferred_element_typ...  6.2 us
    dot_general x1, matrix products, body(): jnp.dot(weights, img, preferred_element_type=F32)  4.09 us
    dot_general x1, matrix products, body(): lax.dot_general(weights, txt, (((0,), (0,)), ((), ())), preferred_element...  3.02 us
  transfers between devices with their start and end apart: 22, of which 10 were waited for; matrix products, arithmetic and copies ran while one was open for 19% of the time, Pallas kernels for 0%

profile of v2, /device:TPU:112, one launch (start us, length us, event | category | flops | bytes accessed | tf_op | source)
XLA Modules:
  0.0 117.4 jit_solution(7196158754966677718)
XLA Ops:
  0.6 2.0 %shard_map.59 = (bf16[64,1152]{1,0:T(8,128)(2,1)}, bf16[4,64,1152]{2,1,0:T(8,128)(2,1)}) custom-call(f32[64,1152]{1,0:T(8,128)} %img_ref.1, f32[64,1152]{1,0:T(8,128)} %txt_ref.1), custom_call_target="tpu_custom_call" | custom-call | tf_op jit(solution)/shard_map/pallas_call | solution.py:48
  2.7 3.1 %collective-permute-start = (bf16[64,1152]{1,0:T(8,128)(2,1)}, bf16[64,1152]{1,0:T(8,128)(2,1)S(1)}, u32[]{:S(2)}, u32[]{:S(2)}) collective-permute-start(bf16[64,1152]{1,0:T(8,128)(2,1)} %get-tuple-element.5), channel_id=1, source_target_pairs={{0,32},{32,64},{64,96},{96,128},{128,160},{160,192},{192,224},{224... | collective-permute-start | bytes 442376 | tf_op jit(solution)/shard_map/ppermute | solution.py:33
  5.8 4.3 %all-to-all-start = ((bf16[4,64,1152]{2,1,0:T(8,128)(2,1)}), bf16[4,64,1152]{2,1,0:T(8,128)(2,1)S(1)}, u32[]{:S(2)}, u32[]{:S(2)}) async-start(bf16[4,64,1152]{2,1,0:T(8,128)(2,1)} %get-tuple-element.4), calls=%async_computation | async-start | bytes 1179648 | tf_op jit(solution)/shard_map/all_to_all | solution.py:28
  11.7 3.2 %collective-permute-start.2 = (bf16[64,1152]{1,0:T(8,128)(2,1)S(1)}, bf16[64,1152]{1,0:T(8,128)(2,1)S(1)}, u32[]{:S(2)}, u32[]{:S(2)}) collective-permute-start(bf16[64,1152]{1,0:T(8,128)(2,1)S(1)} %collective-permute-done), channel_id=1, source_target_pairs={{0,32},{32,64},{64,96},{96,128},{128,160},{160,192},{192,224},{224... | collective-permute-start | bytes 442376 | tf_op jit(solution)/shard_map/ppermute | solution.py:33
  17.6 3.7 %collective-permute-start.4 = (bf16[64,1152]{1,0:T(8,128)(2,1)S(1)}, bf16[64,1152]{1,0:T(8,128)(2,1)S(1)}, u32[]{:S(2)}, u32[]{:S(2)}) collective-permute-start(bf16[64,1152]{1,0:T(8,128)(2,1)S(1)} %collective-permute-done.2), channel_id=1, source_target_pairs={{0,32},{32,64},{64,96},{96,128},{128,160},{160,192},{192,224},{224... | collective-permute-start | bytes 442376 | tf_op jit(solution)/shard_map/ppermute | solution.py:33
  24.0 3.7 %collective-permute-start.6 = (bf16[32,1152]{1,0:T(8,128)(2,1)S(1)}, bf16[32,1152]{1,0:T(8,128)(2,1)S(1)}, u32[]{:S(2)}, u32[]{:S(2)}) collective-permute-start(bf16[32,1152]{1,0:T(8,128)(2,1)S(1)} %slice.70), channel_id=1, source_target_pairs={{0,32},{32,64},{64,96},{96,128},{128,160},{160,192},{192,224},{224... | collective-permute-start | bytes 221192 | tf_op jit(solution)/shard_map/ppermute | solution.py:33
  27.8 1.6 %broadcast_in_dim.22 = bf16[4,256,1152]{2,1,0:T(8,128)(2,1)} broadcast(bf16[256,1152]{1,0:T(8,128)(2,1)S(1)} %bitcast.19), dimensions={1,2} | broadcast | bytes 2949120 | tf_op jit(solution)/shard_map/broadcast_in_dim | solution.py:98
  29.4 4.8 %all-to-all-start.1 = ((bf16[4,256,1152]{2,1,0:T(8,128)(2,1)}), bf16[4,256,1152]{2,1,0:T(8,128)(2,1)S(1)}, u32[]{:S(2)}, u32[]{:S(2)}) async-start(bf16[4,256,1152]{2,1,0:T(8,128)(2,1)} %broadcast_in_dim.22), calls=%async_computation.1 | async-start | bytes 4718592 | tf_op jit(solution)/shard_map/all_to_all | solution.py:28
  38.3 1.7 %collective-permute-done.8 = bf16[512,1152]{1,0:T(8,128)(2,1)S(1)} collective-permute-done((bf16[512,1152]{1,0:T(8,128)(2,1)}, bf16[512,1152]{1,0:T(8,128)(2,1)S(1)}, u32[]{:S(2)}, u32[]{:S(2)}) %collective-permute-start.8) | collective-permute-done | bytes 1179680 | tf_op jit(solution)/shard_map/ppermute | solution.py:33
  41.2 7.9 %all-to-all-done.1 = bf16[4,256,1152]{2,1,0:T(8,128)(2,1)S(1)} async-done(((bf16[4,256,1152]{2,1,0:T(8,128)(2,1)}), bf16[4,256,1152]{2,1,0:T(8,128)(2,1)S(1)}, u32[]{:S(2)}, u32[]{:S(2)}) %all-to-all-start.1) | async-done | bytes 2359328 | tf_op jit(solution)/shard_map/all_to_all | solution.py:28
  49.1 6.2 %multiply_convert_fusion = bf16[1024,1024]{1,0:T(8,128)(2,1)S(1)} fusion(bf16[1024,1152]{1,0:T(8,128)(2,1)S(1)} %bitcast.16, bf16[1024,1152]{1,0:T(8,128)(2,1)} %constant_dynamic-update-slice_fusion.9, f32[]{:T(128)} %bitcast.15, f32[]{:T(128)} %bitcast.13, s32[1024]{0:T(1024)S(1)} %iota_subtract_fusion, pred[1024]{0:T(1024)(128)(4,1)S(1)} %iota_compare_fusion.1), kind=kOutput, calls=%fused_computation.2 | convolution fusion | flops 2428502016 | bytes 6820872 | tf_op jit(solution)/shard_map/dot_general | solution.py:106
  55.3 3.0 %convolution_multiply_fusion.1 = f32[1024,1152]{1,0:T(8,128)S(1)} fusion(bf16[1024,1024]{1,0:T(8,128)(2,1)S(1)} %multiply_convert_fusion, bf16[1024,1152]{1,0:T(8,128)(2,1)S(1)} %bitcast.17, f32[]{:T(128)} %bitcast.12), kind=kOutput, calls=%fused_computation.1 | convolution fusion | flops 2417098752 | bytes 9175044 | tf_op jit(solution)/shard_map/dot_general | solution.py:118
  58.6 2.8 %collective-permute-done.9 = bf16[512,1152]{1,0:T(8,128)(2,1)S(1)} collective-permute-done((bf16[512,1152]{1,0:T(8,128)(2,1)S(1)}, bf16[512,1152]{1,0:T(8,128)(2,1)S(1)}, u32[]{:S(2)}, u32[]{:S(2)}) %collective-permute-start.9) | collective-permute-done | bytes 1179680 | tf_op jit(solution)/shard_map/ppermute | solution.py:33
  62.3 3.2 %collective-permute-start.14 = (bf16[32,1152]{1,0:T(8,128)(2,1)}, bf16[32,1152]{1,0:T(8,128)(2,1)}, u32[]{:S(2)}, u32[]{:S(2)}) collective-permute-start(bf16[32,1152]{1,0:T(8,128)(2,1)} %get-tuple-element.15), channel_id=1, source_target_pairs={{0,32},{32,64},{64,96},{96,128},{128,160},{160,192},{192,224},{224... | collective-permute-start | bytes 221192 | tf_op jit(solution)/shard_map/ppermute | solution.py:33
  65.6 4.1 %fusion.1 = bf16[1024,1152]{1,0:T(8,128)(2,1)} fusion(bf16[1024,1024]{1,0:T(8,128)(2,1)S(1)} %multiply_convert_fusion, bf16[1024,1152]{1,0:T(8,128)(2,1)S(1)} %copy-done.2, f32[]{:T(128)} %bitcast.14), kind=kOutput, calls=%fused_computation.5 | convolution fusion | flops 2418278400 | bytes 6815748 | tf_op jit(solution)/shard_map/dot_general | solution.py:120
  69.7 6.6 %all-to-all-start.2 = ((bf16[4,256,1152]{2,1,0:T(8,128)(2,1)}), bf16[4,256,1152]{2,1,0:T(8,128)(2,1)S(1)}, u32[]{:S(2)}, u32[]{:S(2)}) async-start(bf16[4,256,1152]{2,1,0:T(8,128)(2,1)} %bitcast.18), calls=%async_computation.2 | async-start | bytes 4718592 | tf_op jit(solution)/shard_map/all_to_all | solution.py:28
  79.1 3.3 %collective-permute-start.15 = (bf16[64,1152]{1,0:T(8,128)(2,1)S(1)}, bf16[64,1152]{1,0:T(8,128)(2,1)S(1)}, u32[]{:S(2)}, u32[]{:S(2)}) collective-permute-start(bf16[64,1152]{1,0:T(8,128)(2,1)S(1)} %pad_maximum_fusion.1), channel_id=1, source_target_pairs={{0,32},{32,64},{64,96},{96,128},{128,160},{160,192},{192,224},{224... | collective-permute-start | bytes 442376 | tf_op jit(solution)/shard_map/ppermute | solution.py:33
  82.4 2.1 %collective-permute-done.11 = bf16[64,1152]{1,0:T(8,128)(2,1)S(1)} collective-permute-done((bf16[64,1152]{1,0:T(8,128)(2,1)S(1)}, bf16[64,1152]{1,0:T(8,128)(2,1)S(1)}, u32[]{:S(2)}, u32[]{:S(2)}) %collective-permute-start.11) | collective-permute-done | bytes 147488 | tf_op jit(solution)/shard_map/ppermute | solution.py:33
  85.1 5.9 %collective-permute-done.12 = bf16[64,1152]{1,0:T(8,128)(2,1)S(1)} collective-permute-done((bf16[64,1152]{1,0:T(8,128)(2,1)S(1)}, bf16[64,1152]{1,0:T(8,128)(2,1)S(1)}, u32[]{:S(2)}, u32[]{:S(2)}) %collective-permute-start.12) | collective-permute-done | bytes 147488 | tf_op jit(solution)/shard_map/ppermute | solution.py:33
  93.8 4.3 %collective-permute-done.16 = bf16[64,1152]{1,0:T(8,128)(2,1)S(1)} collective-permute-done((bf16[64,1152]{1,0:T(8,128)(2,1)S(1)}, bf16[64,1152]{1,0:T(8,128)(2,1)S(1)}, u32[]{:S(2)}, u32[]{:S(2)}) %collective-permute-start.16) | collective-permute-done | bytes 147488 | tf_op jit(solution)/shard_map/ppermute | solution.py:33
  98.7 2.2 %collective-permute-start.17 = (bf16[64,1152]{1,0:T(8,128)(2,1)}, bf16[64,1152]{1,0:T(8,128)(2,1)}, u32[]{:S(2)}, u32[]{:S(2)}) collective-permute-start(bf16[64,1152]{1,0:T(8,128)(2,1)} %add_convert_fusion), channel_id=1, source_target_pairs={{0,32},{32,64},{64,96},{96,128},{128,160},{160,192},{192,224},{224... | collective-permute-start | bytes 442376 | tf_op jit(solution)/shard_map/ppermute | solution.py:33
  102.2 5.6 %all-to-all-start.3 = ((bf16[4,64,1152]{2,1,0:T(8,128)(2,1)}), bf16[4,64,1152]{2,1,0:T(8,128)(2,1)S(1)}, u32[]{:S(2)}, u32[]{:S(2)}) async-start(bf16[4,64,1152]{2,1,0:T(8,128)(2,1)} %bitcast.20), calls=%async_computation.3 | async-start | bytes 1179648 | tf_op jit(solution)/shard_map/all_to_all | solution.py:28
  109.1 1.9 %multiply_subtract_fusion.1 = f32[64,1152]{1,0:T(8,128)} fusion(f32[64,1152]{1,0:T(8,128)} %img_ref.1, bf16[64,1152]{1,0:T(8,128)(2,1)} %collective-permute-done.17, bf16[64,1152]{1,0:T(8,128)(2,1)} %collective-permute-done.13, f32[64]{0:T(128)S(1)} %get-tuple-element.9, f32[64]{0:T(128)S(1)} %get-tuple-element.39, f32[64]{0:T(128)S(1)} %get-tuple-element.38, ...), kind=kLoop, calls=%fused_computation.13 | loop fusion | flops 663552 | bytes 1032960 | tf_op jit(solution)/shard_map/sub | solution.py:61
  111.1 5.2 %all-to-all-done.3 = bf16[4,64,1152]{2,1,0:T(8,128)(2,1)S(1)} async-done(((bf16[4,64,1152]{2,1,0:T(8,128)(2,1)}), bf16[4,64,1152]{2,1,0:T(8,128)(2,1)S(1)}, u32[]{:S(2)}, u32[]{:S(2)}) %all-to-all-start.3) | async-done | bytes 589856 | tf_op jit(solution)/shard_map/all_to_all | solution.py:28
  (62 shorter events, 22.7 us)
Async XLA Ops:
  2.7 9.0 %collective-permute-start = (bf16[64,1152]{1,0:T(8,128)(2,1)}, bf16[64,1152]{1,0:T(8,128)(2,1)S(1)}, u32[]{:S(2)}, u32[]{:S(2)}) collective-permute-start(bf16[64,1152]{1,0:T(8,128)(2,1)} %get-tuple-element.5), channel_id=1, source_target_pairs={{0,32},{32,64},{64,96},{96,128},{128,160},{160,192},{192,224},{224... | collective-permute-start | bytes 442376 | tf_op jit(solution)/shard_map/ppermute | solution.py:33
  5.8 9.1 %collective-permute-start.1 = (bf16[64,1152]{1,0:T(8,128)(2,1)}, bf16[64,1152]{1,0:T(8,128)(2,1)S(1)}, u32[]{:S(2)}, u32[]{:S(2)}) collective-permute-start(bf16[64,1152]{1,0:T(8,128)(2,1)} %get-tuple-element.5), channel_id=1, source_target_pairs={{0,224},{32,0},{64,32},{96,64},{128,96},{160,128},{192,160},{224,1... | collective-permute-start | bytes 442376 | tf_op jit(solution)/shard_map/ppermute | solution.py:33
  5.8 21.9 %all-to-all-start = ((bf16[4,64,1152]{2,1,0:T(8,128)(2,1)}), bf16[4,64,1152]{2,1,0:T(8,128)(2,1)S(1)}, u32[]{:S(2)}, u32[]{:S(2)}) async-start(bf16[4,64,1152]{2,1,0:T(8,128)(2,1)} %get-tuple-element.4), calls=%async_computation | async-start | bytes 1179648 | tf_op jit(solution)/shard_map/all_to_all | solution.py:28
  11.7 5.9 %collective-permute-start.2 = (bf16[64,1152]{1,0:T(8,128)(2,1)S(1)}, bf16[64,1152]{1,0:T(8,128)(2,1)S(1)}, u32[]{:S(2)}, u32[]{:S(2)}) collective-permute-start(bf16[64,1152]{1,0:T(8,128)(2,1)S(1)} %collective-permute-done), channel_id=1, source_target_pairs={{0,32},{32,64},{64,96},{96,128},{128,160},{160,192},{192,224},{224... | collective-permute-start | bytes 442376 | tf_op jit(solution)/shard_map/ppermute | solution.py:33
  14.9 6.4 %collective-permute-start.3 = (bf16[64,1152]{1,0:T(8,128)(2,1)S(1)}, bf16[64,1152]{1,0:T(8,128)(2,1)S(1)}, u32[]{:S(2)}, u32[]{:S(2)}) collective-permute-start(bf16[64,1152]{1,0:T(8,128)(2,1)S(1)} %collective-permute-done.1), channel_id=1, source_target_pairs={{0,224},{32,0},{64,32},{96,64},{128,96},{160,128},{192,160},{224,1... | collective-permute-start | bytes 442376 | tf_op jit(solution)/shard_map/ppermute | solution.py:33
  17.6 6.4 %collective-permute-start.4 = (bf16[64,1152]{1,0:T(8,128)(2,1)S(1)}, bf16[64,1152]{1,0:T(8,128)(2,1)S(1)}, u32[]{:S(2)}, u32[]{:S(2)}) collective-permute-start(bf16[64,1152]{1,0:T(8,128)(2,1)S(1)} %collective-permute-done.2), channel_id=1, source_target_pairs={{0,32},{32,64},{64,96},{96,128},{128,160},{160,192},{192,224},{224... | collective-permute-start | bytes 442376 | tf_op jit(solution)/shard_map/ppermute | solution.py:33
  21.3 6.4 %collective-permute-start.5 = (bf16[64,1152]{1,0:T(8,128)(2,1)S(1)}, bf16[64,1152]{1,0:T(8,128)(2,1)S(1)}, u32[]{:S(2)}, u32[]{:S(2)}) collective-permute-start(bf16[64,1152]{1,0:T(8,128)(2,1)S(1)} %collective-permute-done.3), channel_id=1, source_target_pairs={{0,224},{32,0},{64,32},{96,64},{128,96},{160,128},{192,160},{224,1... | collective-permute-start | bytes 442376 | tf_op jit(solution)/shard_map/ppermute | solution.py:33
  24.0 11.7 %collective-permute-start.6 = (bf16[32,1152]{1,0:T(8,128)(2,1)S(1)}, bf16[32,1152]{1,0:T(8,128)(2,1)S(1)}, u32[]{:S(2)}, u32[]{:S(2)}) collective-permute-start(bf16[32,1152]{1,0:T(8,128)(2,1)S(1)} %slice.70), channel_id=1, source_target_pairs={{0,32},{32,64},{64,96},{96,128},{128,160},{160,192},{192,224},{224... | collective-permute-start | bytes 221192 | tf_op jit(solution)/shard_map/ppermute | solution.py:33
  27.6 8.7 %collective-permute-start.7 = (bf16[32,1152]{1,0:T(8,128)(2,1)S(1)}, bf16[32,1152]{1,0:T(8,128)(2,1)S(1)}, u32[]{:S(2)}, u32[]{:S(2)}) collective-permute-start(bf16[32,1152]{1,0:T(8,128)(2,1)S(1)} %slice.71), channel_id=1, source_target_pairs={{0,224},{32,0},{64,32},{96,64},{128,96},{160,128},{192,160},{224,1... | collective-permute-start | bytes 221192 | tf_op jit(solution)/shard_map/ppermute | solution.py:33
  29.4 19.7 %all-to-all-start.1 = ((bf16[4,256,1152]{2,1,0:T(8,128)(2,1)}), bf16[4,256,1152]{2,1,0:T(8,128)(2,1)S(1)}, u32[]{:S(2)}, u32[]{:S(2)}) async-start(bf16[4,256,1152]{2,1,0:T(8,128)(2,1)} %broadcast_in_dim.22), calls=%async_computation.1 | async-start | bytes 4718592 | tf_op jit(solution)/shard_map/all_to_all | solution.py:28
  37.0 3.1 %collective-permute-start.8 = (bf16[512,1152]{1,0:T(8,128)(2,1)}, bf16[512,1152]{1,0:T(8,128)(2,1)S(1)}, u32[]{:S(2)}, u32[]{:S(2)}) collective-permute-start(bf16[512,1152]{1,0:T(8,128)(2,1)} %get-tuple-element.32), channel_id=1, source_target_pairs={{0,8},{8,0},{1,9},{9,1},{2,10},{10,2},{3,11},{11,3},{4,12},{12,4},... | collective-permute-start | bytes 3538952 | tf_op jit(solution)/shard_map/ppermute | solution.py:33
  58.5 7.1 %copy-start.2 = (bf16[1024,1152]{1,0:T(8,128)(2,1)S(1)}, bf16[1024,1152]{1,0:T(8,128)(2,1)}, u32[]{:S(2)}) copy-start(bf16[1024,1152]{1,0:T(8,128)(2,1)} %constant_dynamic-update-slice_fusion.9) | copy-start | bytes 7077892
  58.5 2.9 %collective-permute-start.9 = (bf16[512,1152]{1,0:T(8,128)(2,1)S(1)}, bf16[512,1152]{1,0:T(8,128)(2,1)S(1)}, u32[]{:S(2)}, u32[]{:S(2)}) collective-permute-start(bf16[512,1152]{1,0:T(8,128)(2,1)S(1)} %slice.97), channel_id=1, source_target_pairs={{0,8},{8,0},{1,9},{9,1},{2,10},{10,2},{3,11},{11,3},{4,12},{12,4},... | collective-permute-start | bytes 3538952 | tf_op jit(solution)/shard_map/ppermute | solution.py:33
  62.3 13.9 %collective-permute-start.10 = (bf16[32,1152]{1,0:T(8,128)(2,1)}, bf16[32,1152]{1,0:T(8,128)(2,1)}, u32[]{:S(2)}, u32[]{:S(2)}) collective-permute-start(bf16[32,1152]{1,0:T(8,128)(2,1)} %get-tuple-element.14), channel_id=1, source_target_pairs={{0,224},{32,0},{64,32},{96,64},{128,96},{160,128},{192,160},{224,1... | collective-permute-start | bytes 221192 | tf_op jit(solution)/shard_map/ppermute | solution.py:33
  62.3 13.9 %collective-permute-start.14 = (bf16[32,1152]{1,0:T(8,128)(2,1)}, bf16[32,1152]{1,0:T(8,128)(2,1)}, u32[]{:S(2)}, u32[]{:S(2)}) collective-permute-start(bf16[32,1152]{1,0:T(8,128)(2,1)} %get-tuple-element.15), channel_id=1, source_target_pairs={{0,32},{32,64},{64,96},{96,128},{128,160},{160,192},{192,224},{224... | collective-permute-start | bytes 221192 | tf_op jit(solution)/shard_map/ppermute | solution.py:33
  69.7 31.2 %all-to-all-start.2 = ((bf16[4,256,1152]{2,1,0:T(8,128)(2,1)}), bf16[4,256,1152]{2,1,0:T(8,128)(2,1)S(1)}, u32[]{:S(2)}, u32[]{:S(2)}) async-start(bf16[4,256,1152]{2,1,0:T(8,128)(2,1)} %bitcast.18), calls=%async_computation.2 | async-start | bytes 4718592 | tf_op jit(solution)/shard_map/all_to_all | solution.py:28
  78.1 6.4 %collective-permute-start.11 = (bf16[64,1152]{1,0:T(8,128)(2,1)S(1)}, bf16[64,1152]{1,0:T(8,128)(2,1)S(1)}, u32[]{:S(2)}, u32[]{:S(2)}) collective-permute-start(bf16[64,1152]{1,0:T(8,128)(2,1)S(1)} %pad_maximum_fusion), channel_id=1, source_target_pairs={{0,224},{32,0},{64,32},{96,64},{128,96},{160,128},{192,160},{224,1... | collective-permute-start | bytes 442376 | tf_op jit(solution)/shard_map/ppermute | solution.py:33
  79.1 6.0 %collective-permute-start.15 = (bf16[64,1152]{1,0:T(8,128)(2,1)S(1)}, bf16[64,1152]{1,0:T(8,128)(2,1)S(1)}, u32[]{:S(2)}, u32[]{:S(2)}) collective-permute-start(bf16[64,1152]{1,0:T(8,128)(2,1)S(1)} %pad_maximum_fusion.1), channel_id=1, source_target_pairs={{0,32},{32,64},{64,96},{96,128},{128,160},{160,192},{192,224},{224... | collective-permute-start | bytes 442376 | tf_op jit(solution)/shard_map/ppermute | solution.py:33
  84.6 6.4 %collective-permute-start.12 = (bf16[64,1152]{1,0:T(8,128)(2,1)S(1)}, bf16[64,1152]{1,0:T(8,128)(2,1)S(1)}, u32[]{:S(2)}, u32[]{:S(2)}) collective-permute-start(bf16[64,1152]{1,0:T(8,128)(2,1)S(1)} %add_convert_fusion.3), channel_id=1, source_target_pairs={{0,224},{32,0},{64,32},{96,64},{128,96},{160,128},{192,160},{224,1... | collective-permute-start | bytes 442376 | tf_op jit(solution)/shard_map/ppermute | solution.py:33
  91.8 6.3 %collective-permute-start.16 = (bf16[64,1152]{1,0:T(8,128)(2,1)S(1)}, bf16[64,1152]{1,0:T(8,128)(2,1)S(1)}, u32[]{:S(2)}, u32[]{:S(2)}) collective-permute-start(bf16[64,1152]{1,0:T(8,128)(2,1)S(1)} %get-tuple-element.11), channel_id=1, source_target_pairs={{0,32},{32,64},{64,96},{96,128},{128,160},{160,192},{192,224},{224... | collective-permute-start | bytes 442376 | tf_op jit(solution)/shard_map/ppermute | solution.py:33
  92.6 15.3 %collective-permute-start.13 = (bf16[64,1152]{1,0:T(8,128)(2,1)}, bf16[64,1152]{1,0:T(8,128)(2,1)}, u32[]{:S(2)}, u32[]{:S(2)}) collective-permute-start(bf16[64,1152]{1,0:T(8,128)(2,1)} %get-tuple-element.10), channel_id=1, source_target_pairs={{0,224},{32,0},{64,32},{96,64},{128,96},{160,128},{192,160},{224,1... | collective-permute-start | bytes 442376 | tf_op jit(solution)/shard_map/ppermute | solution.py:33
  98.7 9.1 %collective-permute-start.17 = (bf16[64,1152]{1,0:T(8,128)(2,1)}, bf16[64,1152]{1,0:T(8,128)(2,1)}, u32[]{:S(2)}, u32[]{:S(2)}) collective-permute-start(bf16[64,1152]{1,0:T(8,128)(2,1)} %add_convert_fusion), channel_id=1, source_target_pairs={{0,32},{32,64},{64,96},{96,128},{128,160},{160,192},{192,224},{224... | collective-permute-start | bytes 442376 | tf_op jit(solution)/shard_map/ppermute | solution.py:33
  102.2 14.1 %copy-start = (f32[64,1152]{1,0:T(8,128)S(1)}, f32[64,1152]{1,0:T(8,128)}, u32[]{:S(2)}) copy-start(f32[64,1152]{1,0:T(8,128)} %txt_ref.1) | copy-start | bytes 884740
  102.2 14.1 %all-to-all-start.3 = ((bf16[4,64,1152]{2,1,0:T(8,128)(2,1)}), bf16[4,64,1152]{2,1,0:T(8,128)(2,1)S(1)}, u32[]{:S(2)}, u32[]{:S(2)}) async-start(bf16[4,64,1152]{2,1,0:T(8,128)(2,1)} %bitcast.20), calls=%async_computation.3 | async-start | bytes 1179648 | tf_op jit(solution)/shard_map/all_to_all | solution.py:28
  (1 other events, 6.7 us)

commit v3 on v2

v3 whole, which is shorter than its diff:
```python
import functools

import jax
import jax.numpy as jnp
from jax import lax
from jax.experimental import pallas as pl
from jax.experimental.pallas import tpu as pltpu
from jax.sharding import Mesh, PartitionSpec as P

AXES = ("z", "yh", "c", "yl", "x")
PLANE = ("yh", "c", "yl", "x")
BF16 = jnp.bfloat16
F32 = jnp.float32
VMEM = pl.BlockSpec(memory_space=pltpu.VMEM)
SMEM = pl.BlockSpec(memory_space=pltpu.SMEM)
ROWS_TILE = 256


def plane_groups():
    at = lambda y, c, x: ((y // 2 * 2 + c) * 2 + y % 2) * 4 + x
    along_x = [[[at(y, c, x) for x in range(4)] for y in range(4)] for c in range(2)]
    along_y = [[[at(y, c, x) for y in range(4)] for x in range(4)] for c in range(2)]
    return (along_x[0] + along_y[1], along_y[0] + along_x[1])


FIRST, SECOND = plane_groups()


def exchanged(blocks, groups):
    return lax.all_to_all(blocks, PLANE, 0, 0, tiled=True, axis_index_groups=groups)


def shifted(value, axis, by):
    length = lax.axis_size(axis)
    return lax.ppermute(value, axis, [(i, (i + by) % length) for i in range(length)])


def shaped(shape, dtype):
    return jax.ShapeDtypeStruct(shape, dtype)


def local(kernel, outs, *args, scalars=0, flops=0, out_specs=None):
    specs = [SMEM] * scalars + [VMEM] * (len(args) - scalars)
    many = isinstance(outs, list)
    return pl.pallas_call(
        kernel,
        out_shape=outs,
        in_specs=specs,
        out_specs=out_specs or ([VMEM] * len(outs) if many else VMEM),
        compiler_params=pltpu.CompilerParams(vmem_limit_bytes=40 * 2**20),
        cost_estimate=pl.CostEstimate(
            flops=flops,
            bytes_accessed=sum(a.size * a.dtype.itemsize for a in args),
            transcendentals=0,
        ),
    )(*args)


def matmul(a, b, contract):
    return lax.dot_general(a, b, (contract, ((), ())), preferred_element_type=F32)


def inverse(raw):
    return lax.rsqrt(jnp.sum(raw * raw, axis=1, keepdims=True) + 1e-06)


def normalize_kernel(raw_ref, out_ref):
    raw = raw_ref[...]
    norm = (raw * inverse(raw)).astype(BF16)
    for i in range(out_ref.shape[0]):
        out_ref[i] = norm


def repeat_kernel(block_ref, out_ref):
    for i in range(out_ref.shape[0]):
        out_ref[i] = block_ref[...]


def join_kernel(*refs):
    *blocks, out_ref = refs
    rows = blocks[0].shape[0]
    for i, block in enumerate(blocks):
        out_ref[i * rows : (i + 1) * rows, :] = block[...]


def pair_kernel(rows, scale_ref, bias_ref, place_ref, img_ref, txt_ref, w_ref, d_ref):
    scale, bias = (scale_ref[0], bias_ref[0])
    for at in range(0, img_ref.shape[0], ROWS_TILE):
        tile = pl.ds(at, ROWS_TILE)
        logits = scale * matmul(img_ref[tile, :], txt_ref[...], ((1,), (1,))) + bias
        if at < rows:
            img_at = at + lax.broadcasted_iota(jnp.int32, logits.shape, 0)
            txt_at = lax.broadcasted_iota(jnp.int32, logits.shape, 1) - place_ref[0]
            sign = jnp.where((img_at == txt_at) & (img_at < rows), 1.0, -1.0).astype(F32)
            weights = -sign / (1.0 + jnp.exp(sign * logits))
        else:
            weights = 1.0 / (1.0 + jnp.exp(-logits))
        weights = weights.astype(BF16)
        w_ref[tile, :] = weights
        d_ref[tile, :] = (scale * matmul(weights, txt_ref[...], ((1,), (0,)))).astype(d_ref.dtype)


def text_kernel(scale_ref, w_mine_ref, w_theirs_ref, mine_ref, theirs_ref, d_ref):
    scale = scale_ref[0]
    for i in range(d_ref.shape[0]):
        cols = pl.ds(i * d_ref.shape[1], d_ref.shape[1])
        total = matmul(w_mine_ref[:, cols], mine_ref[...], ((0,), (0,)))
        total += matmul(w_theirs_ref[:, cols], theirs_ref[...], ((0,), (0,)))
        d_ref[i] = (scale * total).astype(BF16)


def split_kernel(mine_ref, theirs_ref, *outs):
    rows = outs[0].shape[0]
    for i, out in enumerate(outs):
        tile = pl.ds(i * rows, rows)
        out[...] = (mine_ref[tile, :] + theirs_ref[tile, :].astype(F32)).astype(out.dtype)


def add_kernel(a_ref, b_ref, out_ref):
    out_ref[...] = (a_ref[...].astype(F32) + b_ref[...].astype(F32)).astype(BF16)


def sum_kernel(parts_ref, out_ref):
    total = parts_ref[0].astype(F32)
    for i in range(1, parts_ref.shape[0]):
        total += parts_ref[i].astype(F32)
    rows = out_ref.shape[1]
    for i in range(out_ref.shape[0]):
        out_ref[i] = total[i * rows : (i + 1) * rows].astype(BF16)


def unnormalize(raw, grad):
    inv = inverse(raw)
    return inv * grad - raw * (inv * inv * inv) * jnp.sum(raw * grad, axis=1, keepdims=True)


def image_end_kernel(raw_ref, own_ref, up_ref, down_ref, out_ref):
    grad = own_ref[...] + up_ref[...].astype(F32) + down_ref[...].astype(F32)
    out_ref[...] = unnormalize(raw_ref[...], grad)


def text_end_kernel(raw_ref, parts_ref, out_ref):
    grad = parts_ref[0].astype(F32)
    for i in range(1, parts_ref.shape[0]):
        grad += parts_ref[i].astype(F32)
    out_ref[...] = unnormalize(raw_ref[...], grad)


def added(a, b):
    return local(add_kernel, shaped(a.shape, BF16), a, b)


def body(images, texts, scale, bias):
    rows, width = images.shape
    line = len(FIRST[0])
    ring = lax.axis_size("z")
    near, all_txt = (ring * rows, line * line * rows)
    txt_copies = local(normalize_kernel, shaped((line, rows, width), BF16), texts)
    img_norm = local(normalize_kernel, shaped((1, rows, width), BF16), images).reshape(rows, width)

    lines = exchanged(txt_copies, FIRST)
    up, down = (shifted(img_norm, "z", 1), shifted(img_norm, "z", -1))
    blocks = [img_norm, up, down]
    lines, up, down = lax.optimization_barrier((lines, up, down))
    copies = local(
        repeat_kernel,
        shaped((line, line * rows, width), BF16),
        lines.reshape(line * rows, width),
    )
    txt = exchanged(copies, SECOND).reshape(all_txt, width)
    for _ in range(2):
        up, down = (shifted(up, "z", 1), shifted(down, "z", -1))
        blocks += [up, down]
    blocks.append(shifted(up, "z", 1))
    mine = local(join_kernel, shaped((near, width), BF16), *blocks)
    theirs = shifted(mine, "c", 1)

    core, x = (lax.axis_index("c"), lax.axis_index("x"))
    y = lax.axis_index(("yh", "yl"))
    place = (jnp.where(core == 0, y * line + x, x * line + y) * rows).reshape(1)
    flops = 4 * near * all_txt * width
    pair = lambda paired, images_of, kind: local(
        functools.partial(pair_kernel, paired),
        [shaped((near, all_txt), BF16), shaped((near, width), kind)],
        scale, bias, place, images_of, txt,
        scalars=3, flops=flops,
    )
    w_mine, d_mine = pair(rows, mine, F32)
    w_theirs, d_theirs = pair(0, theirs, BF16)
    back = shifted(d_theirs, "c", 1)
    d_txt = local(
        text_kernel,
        shaped((line, line * rows, width), BF16),
        scale, w_mine, w_theirs, mine, theirs,
        scalars=1, flops=flops,
    )

    parts = exchanged(d_txt, SECOND)
    kinds = [F32] + [BF16] * (ring - 1)
    own, m1, p1, m2, p2, m3, p3, far = local(
        split_kernel, [shaped((rows, width), kind) for kind in kinds], d_mine, back
    )
    up, down = (shifted(far, "z", -1), shifted(p3, "z", 1))
    up, down = (shifted(added(m3, up), "z", -1), shifted(added(p2, down), "z", 1))
    up = shifted(added(m2, up), "z", -1)
    sums = local(sum_kernel, shaped((line, rows, width), BF16), parts)
    sums, up, down = lax.optimization_barrier((sums, up, down))
    ends = exchanged(sums, FIRST)
    up, down = (shifted(added(m1, up), "z", -1), shifted(added(p1, down), "z", 1))

    whole = pl.BlockSpec((rows, width), lambda: (0, 0))
    img_out = local(
        image_end_kernel, shaped((rows, width), F32), images, own, up, down, out_specs=whole
    )
    txt_out = local(text_end_kernel, shaped((rows, width), F32), texts, ends, out_specs=whole)
    return (img_out, txt_out)


def solution(mesh):
    fine = Mesh(mesh.devices.reshape(8, 2, 2, 2, 4), AXES)
    rows = P(AXES, None)
    return jax.shard_map(
        body,
        mesh=fine,
        in_specs=(rows, rows, P(), P()),
        out_specs=(rows, rows),
        check_vma=False,
    )
```

time: 118 us -> 109 us (0.924)
  the two profiles are of different devices: /device:TPU:112 before, /device:TPU:8 now
where the time goes in v3:
time: 109 us
  starting transfers between devices  42.7 us (39%)
  waiting for transfers between devices  34.1 us (31%)
  Pallas kernels  18.9 us (17%)
  local copies, waits for them, and re-layouts  10.9 us (10%)
  between operations  2.08 us (2%)
    ppermute x16, waiting for transfers between devices, shifted(): lax.ppermute(value, axis, [(i, (i + by) % length) for i in range(length)])  33.3 us
    ppermute x16, starting transfers between devices, shifted(): lax.ppermute(value, axis, [(i, (i + by) % length) for i in range(length)])  23.9 us
    pallas_call x16, Pallas kernels, local(): pl.pallas_call(kernel, out_shape=outs, in_specs=specs, out_specs=out_spec...  18.9 us
    all_to_all x4, starting transfers between devices, exchanged(): lax.all_to_all(blocks, PLANE, 0, 0, tiled=True, axis_index_groups=groups)  18.7 us
    unnamed x30, local copies, waits for them, and re-layouts  10.9 us
  transfers between devices with their start and end apart: 20, of which 11 were waited for; matrix products, arithmetic and copies ran while one was open for 0% of the time, Pallas kernels for 6%

profile of v3, /device:TPU:8, one launch (start us, length us, event | category | flops | bytes accessed | tf_op | source)
XLA Modules:
  0.0 108.6 jit_solution(1004919713256501525)
XLA Ops:
  2.5 4.3 %all-to-all-start = ((bf16[4,64,1152]{2,1,0:T(8,128)(2,1)}), bf16[4,64,1152]{2,1,0:T(8,128)(2,1)S(1)}, u32[]{:S(2)}, u32[]{:S(2)}) async-start(bf16[4,64,1152]{2,1,0:T(8,128)(2,1)} %shard_map.60), calls=%async_computation | async-start | bytes 1179648 | tf_op jit(solution)/shard_map/all_to_all | solution.py:30
  7.9 5.9 %collective-permute-start.1 = (bf16[64,1152]{1,0:T(8,128)(2,1)S(1)}, bf16[64,1152]{1,0:T(8,128)(2,1)S(1)}, u32[]{:S(2)}, u32[]{:S(2)}) collective-permute-start(bf16[64,1152]{1,0:T(8,128)(2,1)S(1)} %bitcast.7), channel_id=1, source_target_pairs={{0,224},{32,0},{64,32},{96,64},{128,96},{160,128},{192,160},{224,1... | collective-permute-start | bytes 442376 | tf_op jit(solution)/shard_map/ppermute | solution.py:35
  14.5 2.5 %collective-permute-done.1.refs_2_ = bf16[64,1152]{1,0:T(8,128)(2,1)S(1)} collective-permute-done((bf16[64,1152]{1,0:T(8,128)(2,1)S(1)}, bf16[64,1152]{1,0:T(8,128)(2,1)S(1)}, u32[]{:S(2)}, u32[]{:S(2)}) %collective-permute-start.1) | collective-permute-done | bytes 147488 | tf_op jit(solution)/shard_map/ppermute | solution.py:35
  17.0 3.4 %collective-permute-done.refs_1_ = bf16[64,1152]{1,0:T(8,128)(2,1)S(1)} collective-permute-done((bf16[64,1152]{1,0:T(8,128)(2,1)S(1)}, bf16[64,1152]{1,0:T(8,128)(2,1)S(1)}, u32[]{:S(2)}, u32[]{:S(2)}) %collective-permute-start) | collective-permute-done | bytes 147488 | tf_op jit(solution)/shard_map/ppermute | solution.py:35
  22.0 4.8 %all-to-all-start.1 = ((bf16[4,256,1152]{2,1,0:T(8,128)(2,1)}), bf16[4,256,1152]{2,1,0:T(8,128)(2,1)S(1)}, u32[]{:S(2)}, u32[]{:S(2)}) async-start(bf16[4,256,1152]{2,1,0:T(8,128)(2,1)} %shard_map.62), calls=%async_computation.1 | async-start | bytes 4718592 | tf_op jit(solution)/shard_map/all_to_all | solution.py:30
  26.8 3.2 %collective-permute-start.3 = (bf16[64,1152]{1,0:T(8,128)(2,1)S(1)}, bf16[64,1152]{1,0:T(8,128)(2,1)S(1)}, u32[]{:S(2)}, u32[]{:S(2)}) collective-permute-start(bf16[64,1152]{1,0:T(8,128)(2,1)S(1)} %collective-permute-done.1.refs_2_), channel_id=1, source_target_pairs={{0,224},{32,0},{64,32},{96,64},{128,96},{160,128},{192,160},{224,1... | collective-permute-start | bytes 442376 | tf_op jit(solution)/shard_map/ppermute | solution.py:35
  30.1 3.1 %collective-permute-done.2.refs_3_ = bf16[64,1152]{1,0:T(8,128)(2,1)S(1)} collective-permute-done((bf16[64,1152]{1,0:T(8,128)(2,1)S(1)}, bf16[64,1152]{1,0:T(8,128)(2,1)S(1)}, u32[]{:S(2)}, u32[]{:S(2)}) %collective-permute-start.2) | collective-permute-done | bytes 147488 | tf_op jit(solution)/shard_map/ppermute | solution.py:35
  33.2 3.2 %collective-permute-start.5 = (bf16[64,1152]{1,0:T(8,128)(2,1)S(1)}, bf16[64,1152]{1,0:T(8,128)(2,1)S(1)}, u32[]{:S(2)}, u32[]{:S(2)}) collective-permute-start(bf16[64,1152]{1,0:T(8,128)(2,1)S(1)} %collective-permute-done.3.refs_4_), channel_id=1, source_target_pairs={{0,224},{32,0},{64,32},{96,64},{128,96},{160,128},{192,160},{224,1... | collective-permute-start | bytes 442376 | tf_op jit(solution)/shard_map/ppermute | solution.py:35
  36.4 4.0 %collective-permute-done.4.refs_5_ = bf16[64,1152]{1,0:T(8,128)(2,1)S(1)} collective-permute-done((bf16[64,1152]{1,0:T(8,128)(2,1)S(1)}, bf16[64,1152]{1,0:T(8,128)(2,1)S(1)}, u32[]{:S(2)}, u32[]{:S(2)}) %collective-permute-start.4) | collective-permute-done | bytes 147488 | tf_op jit(solution)/shard_map/ppermute | solution.py:35
  40.4 6.3 %collective-permute-done.6.refs_7_ = bf16[64,1152]{1,0:T(8,128)(2,1)S(1)} collective-permute-done((bf16[64,1152]{1,0:T(8,128)(2,1)S(1)}, bf16[64,1152]{1,0:T(8,128)(2,1)S(1)}, u32[]{:S(2)}, u32[]{:S(2)}) %collective-permute-start.6) | collective-permute-done | bytes 147488 | tf_op jit(solution)/shard_map/ppermute | solution.py:35
  51.2 3.1 %shard_map.63 = (bf16[512,1024]{1,0:T(8,128)(2,1)S(1)}, f32[512,1152]{1,0:T(8,128)S(1)}) custom-call(f32[1]{0:T(128)S(6)} %copy.6.scale_ref, f32[1]{0:T(128)S(6)} %copy.7.bias_ref, s32[1]{0:T(128)} %bitcast.place_ref, bf16[512,1152]{1,0:T(8,128)(2,1)S(1)} %shard_map.61.img_ref.mine_ref, bf16[1024,1152]{1,0:T(8,128)(2,1)S(1)} %bitcast.4), custom_call_target="tpu_custom_call" | custom-call | flops 2415919104 | bytes 3538956 | tf_op jit(solution)/shard_map/pallas_call | solution.py:45
  55.7 4.3 %shard_map.64 = (bf16[512,1024]{1,0:T(8,128)(2,1)S(1)}, bf16[512,1152]{1,0:T(8,128)(2,1)S(1)}) custom-call(f32[1]{0:T(128)S(6)} %copy.6.scale_ref, f32[1]{0:T(128)S(6)} %copy.7.bias_ref, s32[1]{0:T(128)} %bitcast.place_ref, bf16[512,1152]{1,0:T(8,128)(2,1)} %collective-permute-done.7.img_ref.theirs_ref, bf16[1024,1152]{1,0:T(8,128)(2,1)S(1)} %bitcast.5), custom_call_target="tpu_custom_call" | custom-call | flops 2415919104 | bytes 3538956 | tf_op jit(solution)/shard_map/pallas_call | solution.py:45
  61.1 4.2 %shard_map.66 = bf16[4,256,1152]{2,1,0:T(8,128)(2,1)S(1)} custom-call(f32[1]{0:T(128)S(6)} %copy.6.scale_ref, bf16[512,1024]{1,0:T(8,128)(2,1)S(1)} %get-tuple-element.27.w_mine_ref, bf16[512,1024]{1,0:T(8,128)(2,1)S(1)} %get-tuple-element.28.w_theirs_ref, bf16[512,1152]{1,0:T(8,128)(2,1)S(1)} %shard_map.61.img_ref.mine_ref, ...), custom_call_target="tpu_custom_call" | custom-call | flops 2415919104 | bytes 4456452 | tf_op jit(solution)/shard_map/pallas_call | solution.py:45
  66.7 5.1 %all-to-all-start.2 = ((bf16[4,256,1152]{2,1,0:T(8,128)(2,1)}), bf16[4,256,1152]{2,1,0:T(8,128)(2,1)S(1)}, u32[]{:S(2)}, u32[]{:S(2)}) async-start(bf16[4,256,1152]{2,1,0:T(8,128)(2,1)} %copy-done), calls=%async_computation.2 | async-start | bytes 4718592 | tf_op jit(solution)/shard_map/all_to_all | solution.py:30
  72.1 2.6 %collective-permute-done.8.theirs_ref = bf16[512,1152]{1,0:T(8,128)(2,1)S(1)} collective-permute-done((bf16[512,1152]{1,0:T(8,128)(2,1)S(1)}, bf16[512,1152]{1,0:T(8,128)(2,1)S(1)}, u32[]{:S(2)}, u32[]{:S(2)}) %collective-permute-start.8) | collective-permute-done | bytes 1179680 | tf_op jit(solution)/shard_map/ppermute | solution.py:35
  74.6 1.7 %copy-done.2 = f32[512,1152]{1,0:T(8,128)S(1)} copy-done((f32[512,1152]{1,0:T(8,128)S(1)}, f32[512,1152]{1,0:T(8,128)}, u32[]{:S(2)}) %copy-start.2) | copy-done | bytes 2359320
  76.6 2.0 %collective-permute-start.12 = (bf16[64,1152]{1,0:T(8,128)(2,1)S(1)}, bf16[64,1152]{1,0:T(8,128)(2,1)S(1)}, u32[]{:S(2)}, u32[]{:S(2)}) collective-permute-start(bf16[64,1152]{1,0:T(8,128)(2,1)S(1)} %get-tuple-element.33), channel_id=1, source_target_pairs={{0,32},{32,64},{64,96},{96,128},{128,160},{160,192},{192,224},{224... | collective-permute-start | bytes 442376 | tf_op jit(solution)/shard_map/ppermute | solution.py:35
  78.6 4.0 %collective-permute-done.9.b_ref = bf16[64,1152]{1,0:T(8,128)(2,1)S(1)} collective-permute-done((bf16[64,1152]{1,0:T(8,128)(2,1)S(1)}, bf16[64,1152]{1,0:T(8,128)(2,1)S(1)}, u32[]{:S(2)}, u32[]{:S(2)}) %collective-permute-start.9) | collective-permute-done | bytes 147488 | tf_op jit(solution)/shard_map/ppermute | solution.py:35
  85.5 2.5 %collective-permute-done.10.b_ref = bf16[64,1152]{1,0:T(8,128)(2,1)S(1)} collective-permute-done((bf16[64,1152]{1,0:T(8,128)(2,1)S(1)}, bf16[64,1152]{1,0:T(8,128)(2,1)S(1)}, u32[]{:S(2)}, u32[]{:S(2)}) %collective-permute-start.10) | collective-permute-done | bytes 147488 | tf_op jit(solution)/shard_map/ppermute | solution.py:35
  88.6 3.0 %collective-permute-start.11 = (bf16[64,1152]{1,0:T(8,128)(2,1)}, bf16[64,1152]{1,0:T(8,128)(2,1)S(1)}, u32[]{:S(2)}, u32[]{:S(2)}) collective-permute-start(bf16[64,1152]{1,0:T(8,128)(2,1)} %shard_map.69), channel_id=1, source_target_pairs={{0,224},{32,0},{64,32},{96,64},{128,96},{160,128},{192,160},{224,1... | collective-permute-start | bytes 442376 | tf_op jit(solution)/shard_map/ppermute | solution.py:35
  92.8 1.9 %collective-permute-done.11.b_ref = bf16[64,1152]{1,0:T(8,128)(2,1)S(1)} collective-permute-done((bf16[64,1152]{1,0:T(8,128)(2,1)}, bf16[64,1152]{1,0:T(8,128)(2,1)S(1)}, u32[]{:S(2)}, u32[]{:S(2)}) %collective-permute-start.11) | collective-permute-done | bytes 147488 | tf_op jit(solution)/shard_map/ppermute | solution.py:35
  94.7 4.6 %all-to-all-start.3 = ((bf16[4,64,1152]{2,1,0:T(8,128)(2,1)}), bf16[4,64,1152]{2,1,0:T(8,128)(2,1)S(1)}, u32[]{:S(2)}, u32[]{:S(2)}) async-start(bf16[4,64,1152]{2,1,0:T(8,128)(2,1)} %shard_map.67), calls=%async_computation.3 | async-start | bytes 1179648 | tf_op jit(solution)/shard_map/all_to_all | solution.py:30
  99.4 3.6 %collective-permute-start.14 = (bf16[64,1152]{1,0:T(8,128)(2,1)S(1)}, bf16[64,1152]{1,0:T(8,128)(2,1)S(1)}, u32[]{:S(2)}, u32[]{:S(2)}) collective-permute-start(bf16[64,1152]{1,0:T(8,128)(2,1)S(1)} %shard_map.71), channel_id=1, source_target_pairs={{0,224},{32,0},{64,32},{96,64},{128,96},{160,128},{192,160},{224,1... | collective-permute-start | bytes 442376 | tf_op jit(solution)/shard_map/ppermute | solution.py:35
  103.1 3.0 %collective-permute-done.15.down_ref = bf16[64,1152]{1,0:T(8,128)(2,1)S(1)} collective-permute-done((bf16[64,1152]{1,0:T(8,128)(2,1)S(1)}, bf16[64,1152]{1,0:T(8,128)(2,1)S(1)}, u32[]{:S(2)}, u32[]{:S(2)}) %collective-permute-start.15) | collective-permute-done | bytes 147488 | tf_op jit(solution)/shard_map/ppermute | solution.py:35
  (62 shorter events, 20.1 us)
Async XLA Ops:
  2.5 17.9 %all-to-all-start = ((bf16[4,64,1152]{2,1,0:T(8,128)(2,1)}), bf16[4,64,1152]{2,1,0:T(8,128)(2,1)S(1)}, u32[]{:S(2)}, u32[]{:S(2)}) async-start(bf16[4,64,1152]{2,1,0:T(8,128)(2,1)} %shard_map.60), calls=%async_computation | async-start | bytes 1179648 | tf_op jit(solution)/shard_map/all_to_all | solution.py:30
  7.9 9.1 %collective-permute-start.1 = (bf16[64,1152]{1,0:T(8,128)(2,1)S(1)}, bf16[64,1152]{1,0:T(8,128)(2,1)S(1)}, u32[]{:S(2)}, u32[]{:S(2)}) collective-permute-start(bf16[64,1152]{1,0:T(8,128)(2,1)S(1)} %bitcast.7), channel_id=1, source_target_pairs={{0,224},{32,0},{64,32},{96,64},{128,96},{160,128},{192,160},{224,1... | collective-permute-start | bytes 442376 | tf_op jit(solution)/shard_map/ppermute | solution.py:35
  13.8 6.6 %collective-permute-start = (bf16[64,1152]{1,0:T(8,128)(2,1)S(1)}, bf16[64,1152]{1,0:T(8,128)(2,1)S(1)}, u32[]{:S(2)}, u32[]{:S(2)}) collective-permute-start(bf16[64,1152]{1,0:T(8,128)(2,1)S(1)} %bitcast.8), channel_id=1, source_target_pairs={{0,32},{32,64},{64,96},{96,128},{128,160},{160,192},{192,224},{224... | collective-permute-start | bytes 442376 | tf_op jit(solution)/shard_map/ppermute | solution.py:35
  17.0 9.8 %copy-start.9 = (bf16[64,1152]{1,0:T(8,128)(2,1)}, bf16[64,1152]{1,0:T(8,128)(2,1)S(1)}, u32[]{:S(2)}) copy-start(bf16[64,1152]{1,0:T(8,128)(2,1)S(1)} %collective-permute-done.1.refs_2_) | copy-start | bytes 442372
  20.4 6.4 %copy-start.11 = (bf16[64,1152]{1,0:T(8,128)(2,1)}, bf16[64,1152]{1,0:T(8,128)(2,1)S(1)}, u32[]{:S(2)}) copy-start(bf16[64,1152]{1,0:T(8,128)(2,1)S(1)} %collective-permute-done.refs_1_) | copy-start | bytes 442372
  22.0 29.2 %all-to-all-start.1 = ((bf16[4,256,1152]{2,1,0:T(8,128)(2,1)}), bf16[4,256,1152]{2,1,0:T(8,128)(2,1)S(1)}, u32[]{:S(2)}, u32[]{:S(2)}) async-start(bf16[4,256,1152]{2,1,0:T(8,128)(2,1)} %shard_map.62), calls=%async_computation.1 | async-start | bytes 4718592 | tf_op jit(solution)/shard_map/all_to_all | solution.py:30
  26.8 6.4 %collective-permute-start.2 = (bf16[64,1152]{1,0:T(8,128)(2,1)S(1)}, bf16[64,1152]{1,0:T(8,128)(2,1)S(1)}, u32[]{:S(2)}, u32[]{:S(2)}) collective-permute-start(bf16[64,1152]{1,0:T(8,128)(2,1)S(1)} %collective-permute-done.refs_1_), channel_id=1, source_target_pairs={{0,32},{32,64},{64,96},{96,128},{128,160},{160,192},{192,224},{224... | collective-permute-start | bytes 442376 | tf_op jit(solution)/shard_map/ppermute | solution.py:35
  26.8 6.4 %collective-permute-start.3 = (bf16[64,1152]{1,0:T(8,128)(2,1)S(1)}, bf16[64,1152]{1,0:T(8,128)(2,1)S(1)}, u32[]{:S(2)}, u32[]{:S(2)}) collective-permute-start(bf16[64,1152]{1,0:T(8,128)(2,1)S(1)} %collective-permute-done.1.refs_2_), channel_id=1, source_target_pairs={{0,224},{32,0},{64,32},{96,64},{128,96},{160,128},{192,160},{224,1... | collective-permute-start | bytes 442376 | tf_op jit(solution)/shard_map/ppermute | solution.py:35
  33.2 7.3 %collective-permute-start.4 = (bf16[64,1152]{1,0:T(8,128)(2,1)S(1)}, bf16[64,1152]{1,0:T(8,128)(2,1)S(1)}, u32[]{:S(2)}, u32[]{:S(2)}) collective-permute-start(bf16[64,1152]{1,0:T(8,128)(2,1)S(1)} %collective-permute-done.2.refs_3_), channel_id=1, source_target_pairs={{0,32},{32,64},{64,96},{96,128},{128,160},{160,192},{192,224},{224... | collective-permute-start | bytes 442376 | tf_op jit(solution)/shard_map/ppermute | solution.py:35
  33.2 7.3 %collective-permute-start.5 = (bf16[64,1152]{1,0:T(8,128)(2,1)S(1)}, bf16[64,1152]{1,0:T(8,128)(2,1)S(1)}, u32[]{:S(2)}, u32[]{:S(2)}) collective-permute-start(bf16[64,1152]{1,0:T(8,128)(2,1)S(1)} %collective-permute-done.3.refs_4_), channel_id=1, source_target_pairs={{0,224},{32,0},{64,32},{96,64},{128,96},{160,128},{192,160},{224,1... | collective-permute-start | bytes 442376 | tf_op jit(solution)/shard_map/ppermute | solution.py:35
  40.4 6.4 %collective-permute-start.6 = (bf16[64,1152]{1,0:T(8,128)(2,1)S(1)}, bf16[64,1152]{1,0:T(8,128)(2,1)S(1)}, u32[]{:S(2)}, u32[]{:S(2)}) collective-permute-start(bf16[64,1152]{1,0:T(8,128)(2,1)S(1)} %collective-permute-done.4.refs_5_), channel_id=1, source_target_pairs={{0,32},{32,64},{64,96},{96,128},{128,160},{160,192},{192,224},{224... | collective-permute-start | bytes 442376 | tf_op jit(solution)/shard_map/ppermute | solution.py:35
  49.6 6.1 %collective-permute-start.7 = (bf16[512,1152]{1,0:T(8,128)(2,1)S(1)}, bf16[512,1152]{1,0:T(8,128)(2,1)}, u32[]{:S(2)}, u32[]{:S(2)}) collective-permute-start(bf16[512,1152]{1,0:T(8,128)(2,1)S(1)} %shard_map.61.img_ref.mine_ref), channel_id=1, source_target_pairs={{0,8},{8,0},{1,9},{9,1},{2,10},{10,2},{3,11},{11,3},{4,12},{12,4},... | collective-permute-start | bytes 3538952 | tf_op jit(solution)/shard_map/ppermute | solution.py:35
  66.7 24.9 %all-to-all-start.2 = ((bf16[4,256,1152]{2,1,0:T(8,128)(2,1)}), bf16[4,256,1152]{2,1,0:T(8,128)(2,1)S(1)}, u32[]{:S(2)}, u32[]{:S(2)}) async-start(bf16[4,256,1152]{2,1,0:T(8,128)(2,1)} %copy-done), calls=%async_computation.2 | async-start | bytes 4718592 | tf_op jit(solution)/shard_map/all_to_all | solution.py:30
  71.8 2.8 %collective-permute-start.8 = (bf16[512,1152]{1,0:T(8,128)(2,1)S(1)}, bf16[512,1152]{1,0:T(8,128)(2,1)S(1)}, u32[]{:S(2)}, u32[]{:S(2)}) collective-permute-start(bf16[512,1152]{1,0:T(8,128)(2,1)S(1)} %copy-done.14), channel_id=1, source_target_pairs={{0,8},{8,0},{1,9},{9,1},{2,10},{10,2},{3,11},{11,3},{4,12},{12,4},... | collective-permute-start | bytes 3538952 | tf_op jit(solution)/shard_map/ppermute | solution.py:35
  76.5 6.1 %collective-permute-start.9 = (bf16[64,1152]{1,0:T(8,128)(2,1)S(1)}, bf16[64,1152]{1,0:T(8,128)(2,1)S(1)}, u32[]{:S(2)}, u32[]{:S(2)}) collective-permute-start(bf16[64,1152]{1,0:T(8,128)(2,1)S(1)} %get-tuple-element.31), channel_id=1, source_target_pairs={{0,224},{32,0},{64,32},{96,64},{128,96},{160,128},{192,160},{224,1... | collective-permute-start | bytes 442376 | tf_op jit(solution)/shard_map/ppermute | solution.py:35
  76.6 7.6 %collective-permute-start.12 = (bf16[64,1152]{1,0:T(8,128)(2,1)S(1)}, bf16[64,1152]{1,0:T(8,128)(2,1)S(1)}, u32[]{:S(2)}, u32[]{:S(2)}) collective-permute-start(bf16[64,1152]{1,0:T(8,128)(2,1)S(1)} %get-tuple-element.33), channel_id=1, source_target_pairs={{0,32},{32,64},{64,96},{96,128},{128,160},{160,192},{192,224},{224... | collective-permute-start | bytes 442376 | tf_op jit(solution)/shard_map/ppermute | solution.py:35
  82.7 5.3 %collective-permute-start.10 = (bf16[64,1152]{1,0:T(8,128)(2,1)S(1)}, bf16[64,1152]{1,0:T(8,128)(2,1)S(1)}, u32[]{:S(2)}, u32[]{:S(2)}) collective-permute-start(bf16[64,1152]{1,0:T(8,128)(2,1)S(1)} %shard_map.68), channel_id=1, source_target_pairs={{0,224},{32,0},{64,32},{96,64},{128,96},{160,128},{192,160},{224,1... | collective-permute-start | bytes 442376 | tf_op jit(solution)/shard_map/ppermute | solution.py:35
  84.9 7.9 %collective-permute-start.13 = (bf16[64,1152]{1,0:T(8,128)(2,1)}, bf16[64,1152]{1,0:T(8,128)(2,1)S(1)}, u32[]{:S(2)}, u32[]{:S(2)}) collective-permute-start(bf16[64,1152]{1,0:T(8,128)(2,1)} %shard_map.70), channel_id=1, source_target_pairs={{0,32},{32,64},{64,96},{96,128},{128,160},{160,192},{192,224},{224... | collective-permute-start | bytes 442376 | tf_op jit(solution)/shard_map/ppermute | solution.py:35
  88.6 17.4 %copy-start.6 = (f32[64,1152]{1,0:T(8,128)S(1)}, f32[64,1152]{1,0:T(8,128)}, u32[]{:S(2)}) copy-start(f32[64,1152]{1,0:T(8,128)} %raw_ref.6) | copy-start | bytes 884740
  88.6 6.0 %collective-permute-start.11 = (bf16[64,1152]{1,0:T(8,128)(2,1)}, bf16[64,1152]{1,0:T(8,128)(2,1)S(1)}, u32[]{:S(2)}, u32[]{:S(2)}) collective-permute-start(bf16[64,1152]{1,0:T(8,128)(2,1)} %shard_map.69), channel_id=1, source_target_pairs={{0,224},{32,0},{64,32},{96,64},{128,96},{160,128},{192,160},{224,1... | collective-permute-start | bytes 442376 | tf_op jit(solution)/shard_map/ppermute | solution.py:35
  92.8 14.9 %copy-start.4 = (f32[64,1152]{1,0:T(8,128)S(1)}, f32[64,1152]{1,0:T(8,128)}, u32[]{:S(2)}) copy-start(f32[64,1152]{1,0:T(8,128)} %raw_ref.7) | copy-start | bytes 884740
  94.7 13.0 %all-to-all-start.3 = ((bf16[4,64,1152]{2,1,0:T(8,128)(2,1)}), bf16[4,64,1152]{2,1,0:T(8,128)(2,1)S(1)}, u32[]{:S(2)}, u32[]{:S(2)}) async-start(bf16[4,64,1152]{2,1,0:T(8,128)(2,1)} %shard_map.67), calls=%async_computation.3 | async-start | bytes 1179648 | tf_op jit(solution)/shard_map/all_to_all | solution.py:30
  99.3 6.8 %collective-permute-start.15 = (bf16[64,1152]{1,0:T(8,128)(2,1)S(1)}, bf16[64,1152]{1,0:T(8,128)(2,1)S(1)}, u32[]{:S(2)}, u32[]{:S(2)}) collective-permute-start(bf16[64,1152]{1,0:T(8,128)(2,1)S(1)} %shard_map.72), channel_id=1, source_target_pairs={{0,32},{32,64},{64,96},{96,128},{128,160},{160,192},{192,224},{224... | collective-permute-start | bytes 442376 | tf_op jit(solution)/shard_map/ppermute | solution.py:35
  99.4 6.6 %collective-permute-start.14 = (bf16[64,1152]{1,0:T(8,128)(2,1)S(1)}, bf16[64,1152]{1,0:T(8,128)(2,1)S(1)}, u32[]{:S(2)}, u32[]{:S(2)}) collective-permute-start(bf16[64,1152]{1,0:T(8,128)(2,1)S(1)} %shard_map.71), channel_id=1, source_target_pairs={{0,224},{32,0},{64,32},{96,64},{128,96},{160,128},{192,160},{224,1... | collective-permute-start | bytes 442376 | tf_op jit(solution)/shard_map/ppermute | solution.py:35
  (11 other events, 16.0 us)

commit v4 on v3

v4 whole, which is shorter than its diff:
```python
import functools

import jax
import jax.numpy as jnp
from jax import lax
from jax.experimental import pallas as pl
from jax.experimental.pallas import tpu as pltpu
from jax.sharding import Mesh, PartitionSpec as P

AXES = ("z", "yh", "c", "yl", "x")
PLANE = ("yh", "c", "yl", "x")
BF16 = jnp.bfloat16
F32 = jnp.float32
VMEM = pl.BlockSpec(memory_space=pltpu.VMEM)
ANY = pl.BlockSpec(memory_space=pl.ANY)
HBM = pl.BlockSpec(memory_space=pltpu.HBM)
SMEM = pl.BlockSpec(memory_space=pltpu.SMEM)
ROWS_TILE = 256


def plane_groups():
    at = lambda y, c, x: ((y // 2 * 2 + c) * 2 + y % 2) * 4 + x
    along_x = [[[at(y, c, x) for x in range(4)] for y in range(4)] for c in range(2)]
    along_y = [[[at(y, c, x) for y in range(4)] for x in range(4)] for c in range(2)]
    return (along_x[0] + along_y[1], along_y[0] + along_x[1])


FIRST, SECOND = plane_groups()


def exchanged(blocks, groups):
    return lax.all_to_all(blocks, PLANE, 0, 0, tiled=True, axis_index_groups=groups)


def shifted(value, axis, by):
    length = lax.axis_size(axis)
    return lax.ppermute(value, axis, [(i, (i + by) % length) for i in range(length)])


def shaped(shape, dtype):
    return jax.ShapeDtypeStruct(shape, dtype)


def local(kernel, outs, *args, ins=None, out_specs=None, scratch=(), flops=0, aliases=None):
    many = isinstance(outs, list)
    ins = ins or [VMEM] * len(args)
    out_specs = out_specs or ([VMEM] * len(outs) if many else VMEM)
    placed = lambda out, spec: pltpu.HBM(out.shape, out.dtype) if spec is HBM else out
    outs = list(map(placed, outs, out_specs)) if many else placed(outs, out_specs)
    args = [
        pltpu.with_memory_space_constraint(arg, pltpu.HBM) if spec is HBM else arg
        for arg, spec in zip(args, ins)
    ]
    return pl.pallas_call(
        kernel,
        out_shape=outs,
        in_specs=ins,
        out_specs=out_specs,
        scratch_shapes=list(scratch),
        input_output_aliases=aliases or {},
        compiler_params=pltpu.CompilerParams(vmem_limit_bytes=16 * 2**20),
        cost_estimate=pl.CostEstimate(
            flops=flops,
            bytes_accessed=sum(a.size * a.dtype.itemsize for a in args),
            transcendentals=0,
        ),
    )(*args)


def matmul(a, b, contract):
    return lax.dot_general(a, b, (contract, ((), ())), preferred_element_type=F32)


def inverse(raw):
    return lax.rsqrt(jnp.sum(raw * raw, axis=1, keepdims=True) + 1e-06)


def copied(copies):
    for copy in copies:
        copy.start()
    for copy in copies:
        copy.wait()


def normalize_kernel(img_in, txt_in, img_out, txt_out, raw, img_buf, txt_buf, sems):
    reads = [
        pltpu.make_async_copy(a, raw.at[i], sems.at[0, i]) for i, a in enumerate((img_in, txt_in))
    ]
    for read in reads:
        read.start()
    reads[1].wait()
    txt = raw[1]
    txt_buf[...] = (txt * inverse(txt)).astype(BF16)
    writes = [
        pltpu.make_async_copy(txt_buf, txt_out.at[i], sems.at[1, i])
        for i in range(txt_out.shape[0])
    ]
    for write in writes:
        write.start()
    reads[0].wait()
    img = raw[0]
    img_buf[...] = (img * inverse(img)).astype(BF16)
    writes.append(pltpu.make_async_copy(img_buf, img_out, sems.at[0, 2]))
    writes[-1].start()
    for write in writes:
        write.wait()


def repeat_kernel(block_ref, out_ref, sems):
    copied(
        [pltpu.make_async_copy(block_ref, out_ref.at[i], sems.at[i]) for i in range(out_ref.shape[0])]
    )


def join_kernel(first, *refs):
    *blocks, out_ref, sems = refs
    rows = out_ref.shape[0] // sems.shape[0]
    at = lambda i: out_ref.at[pl.ds((first + i) * rows, rows), :]
    blocks = blocks[1:] if first else blocks
    copied([pltpu.make_async_copy(block, at(i), sems.at[i]) for i, block in enumerate(blocks)])


def weights_of(img_ref, txt_ref, tile, scale, bias, paired=0, place=None):
    at, size = tile
    logits = scale * matmul(img_ref[pl.ds(at, size), :], txt_ref[...], ((1,), (1,))) + bias
    if at >= paired:
        return (1.0 / (1.0 + jnp.exp(-logits))).astype(BF16)
    img_at = at + lax.broadcasted_iota(jnp.int32, logits.shape, 0)
    txt_at = lax.broadcasted_iota(jnp.int32, logits.shape, 1) - place
    sign = jnp.where((img_at == txt_at) & (img_at < paired), 1.0, -1.0).astype(F32)
    return (-sign / (1.0 + jnp.exp(sign * logits))).astype(BF16)


def tiles(rows):
    return [(at, ROWS_TILE) for at in range(0, rows, ROWS_TILE)]


def leave(copies, buffer, out, tile, sems):
    part = (pl.ds(*tile), slice(None))
    copies.append(pltpu.make_async_copy(buffer.at[part], out.at[part], sems.at[len(copies)]))
    copies[-1].start()


def mine_kernel(
    paired, scale_ref, bias_ref, place_ref, img_ref, txt_ref, w_ref, d_out, d_buf, sems
):
    scale, copies = (scale_ref[0], [])
    for tile in tiles(img_ref.shape[0]):
        weights = weights_of(img_ref, txt_ref, tile, scale, bias_ref[0], paired, place_ref[0])
        w_ref[pl.ds(*tile), :] = weights
        d_buf[pl.ds(*tile), :] = scale * matmul(weights, txt_ref[...], ((1,), (0,)))
        leave(copies, d_buf, d_out, tile, sems)
    for copy in copies:
        copy.wait()


def theirs_kernel(scale_ref, bias_ref, _, img_ref, txt_ref, w_ref, d_ref):
    scale = scale_ref[0]
    for tile in tiles(img_ref.shape[0]):
        weights = weights_of(img_ref, txt_ref, tile, scale, bias_ref[0])
        w_ref[pl.ds(*tile), :] = weights
        d_ref[pl.ds(*tile), :] = (scale * matmul(weights, txt_ref[...], ((1,), (0,)))).astype(BF16)


def text_kernel(scale_ref, w_mine_ref, w_theirs_ref, mine_ref, theirs_ref, d_out, d_buf, sems):
    scale, copies = (scale_ref[0], [])
    for tile in tiles(d_buf.shape[0]):
        total = matmul(w_mine_ref[:, pl.ds(*tile)], mine_ref[...], ((0,), (0,)))
        total += matmul(w_theirs_ref[:, pl.ds(*tile)], theirs_ref[...], ((0,), (0,)))
        d_buf[pl.ds(*tile), :] = (scale * total).astype(BF16)
        leave(copies, d_buf, d_out, tile, sems)
    for copy in copies:
        copy.wait()


def split_kernel(late, mine_in, theirs_in, *refs):
    *outs, mine, theirs, own_buf, late_buf, sems = refs
    rows = outs[0].shape[0]
    arriving, leaving = ([], [])
    for i in reversed(range(len(outs))):
        tile = (pl.ds(i * rows, rows), slice(None))
        pair = [
            pltpu.make_async_copy(mine_in.at[tile], mine.at[tile], sems.at[0, i]),
            pltpu.make_async_copy(theirs_in.at[tile], theirs.at[tile], sems.at[1, i]),
        ]
        for copy in pair:
            copy.start()
        arriving.append((i, tile, pair))
    for i, tile, pair in arriving:
        for copy in pair:
            copy.wait()
        out = outs[i]
        buffer = out if i >= late else late_buf.at[i - 1] if i else own_buf
        buffer[...] = (mine[tile] + theirs[tile].astype(F32)).astype(out.dtype)
        if i < late:
            leaving.append(pltpu.make_async_copy(buffer, out, sems.at[2, i]))
            leaving[-1].start()
    for copy in leaving:
        copy.wait()


def add_kernel(a_ref, b_ref, out_ref):
    out_ref[...] = (a_ref[...].astype(F32) + b_ref[...].astype(F32)).astype(BF16)


def sum_kernel(parts_ref, out_ref, buffer, sem):
    total = parts_ref[0].astype(F32)
    for i in range(1, parts_ref.shape[0]):
        total += parts_ref[i].astype(F32)
    rows = out_ref.shape[1]
    for i in range(out_ref.shape[0]):
        buffer[i] = total[i * rows : (i + 1) * rows].astype(BF16)
    copied([pltpu.make_async_copy(buffer, out_ref, sem)])


def unnormalize(raw, grad):
    inv = inverse(raw)
    return inv * grad - raw * (inv * inv * inv) * jnp.sum(raw * grad, axis=1, keepdims=True)


def image_end_kernel(raw_ref, own_ref, up_ref, down_ref, out_ref):
    grad = own_ref[...] + up_ref[...].astype(F32) + down_ref[...].astype(F32)
    out_ref[...] = unnormalize(raw_ref[...], grad)


def text_end_kernel(raw_ref, parts_ref, out_ref):
    grad = parts_ref[0].astype(F32)
    for i in range(1, parts_ref.shape[0]):
        grad += parts_ref[i].astype(F32)
    out_ref[...] = unnormalize(raw_ref[...], grad)


def added(a, b):
    return local(add_kernel, shaped(a.shape, BF16), a, b)


def body(images, texts, scale, bias):
    rows, width = images.shape
    line, ring = (len(FIRST[0]), lax.axis_size("z"))
    near, all_txt = (ring * rows, line * line * rows)
    copies_of = lambda *shape: pltpu.SemaphoreType.DMA(shape)

    img_norm, txt_copies = local(
        normalize_kernel,
        [shaped((rows, width), BF16), shaped((line, rows, width), BF16)],
        images, texts,
        ins=[HBM, HBM],
        out_specs=[HBM, HBM],
        scratch=[pltpu.VMEM((2, rows, width), F32)]
        + [pltpu.VMEM((rows, width), BF16)] * 2
        + [copies_of(2, line)],
    )
    lines = exchanged(txt_copies, FIRST).reshape(line * rows, width)
    up, down = (shifted(img_norm, "z", 1), shifted(img_norm, "z", -1))
    blocks = [img_norm, up, down]
    lines, up, down = lax.optimization_barrier((lines, up, down))
    up, down = (shifted(up, "z", 1), shifted(down, "z", -1))
    blocks += [up, down]
    copies = local(
        repeat_kernel,
        shaped((line, line * rows, width), BF16),
        lines,
        ins=[ANY],
        out_specs=HBM,
        scratch=[copies_of(line)],
    )
    txt = exchanged(copies, SECOND).reshape(all_txt, width)
    up, down = (shifted(up, "z", 1), shifted(down, "z", -1))
    blocks += [up, down]
    join = lambda first, ins, *args: local(
        functools.partial(join_kernel, first),
        shaped((near, width), BF16),
        *args,
        ins=ins,
        scratch=[copies_of(ring)],
        aliases={0: 0} if first else {},
    )
    mine = join(0, [HBM] * 3 + [ANY] * 4, *blocks)
    far = shifted(up, "z", 1)
    mine = join(ring - 1, [VMEM, ANY], mine, far)
    theirs = shifted(mine, "c", 1)

    core, x = (lax.axis_index("c"), lax.axis_index("x"))
    y = lax.axis_index(("yh", "yl"))
    place = (jnp.where(core == 0, y * line + x, x * line + y) * rows).reshape(1)
    flops = 2 * near * all_txt * width
    w_shape = shaped((near, all_txt), BF16)
    w_mine, d_mine = local(
        functools.partial(mine_kernel, rows),
        [w_shape, shaped((near, width), F32)],
        scale, bias, place, mine, txt,
        ins=[SMEM] * 3 + [VMEM] * 2,
        out_specs=[VMEM, HBM],
        scratch=[pltpu.VMEM((near, width), F32), copies_of(near // ROWS_TILE)],
        flops=2 * flops,
    )
    w_theirs, d_theirs = local(
        theirs_kernel,
        [w_shape, shaped((near, width), BF16)],
        scale, bias, w_mine, theirs, txt,
        ins=[SMEM] * 2 + [ANY] + [VMEM] * 2,
        flops=2 * flops,
    )
    back = shifted(d_theirs, "c", 1)
    d_txt = local(
        text_kernel,
        shaped((all_txt, width), BF16),
        scale, w_mine, w_theirs, mine, theirs,
        ins=[SMEM] + [VMEM] * 4,
        out_specs=HBM,
        scratch=[pltpu.VMEM((all_txt, width), BF16), copies_of(all_txt // ROWS_TILE)],
        flops=2 * flops,
    )

    d_txt, back = lax.optimization_barrier((d_txt, back))
    parts = exchanged(d_txt.reshape(line, line * rows, width), SECOND)
    kinds = [F32] + [BF16] * (ring - 1)
    late = 3
    own, m1, p1, m2, p2, m3, p3, far = local(
        functools.partial(split_kernel, late),
        [shaped((rows, width), kind) for kind in kinds],
        d_mine, back,
        ins=[HBM, HBM],
        out_specs=[HBM] * late + [VMEM] * (ring - late),
        scratch=[
            pltpu.VMEM((near, width), F32),
            pltpu.VMEM((near, width), BF16),
            pltpu.VMEM((rows, width), F32),
            pltpu.VMEM((late - 1, rows, width), BF16),
            copies_of(3, ring),
        ],
    )
    up, down = (shifted(far, "z", -1), shifted(p3, "z", 1))
    up, down = (shifted(added(m3, up), "z", -1), shifted(added(p2, down), "z", 1))
    up = shifted(added(m2, up), "z", -1)
    sums = local(
        sum_kernel,
        shaped((line, rows, width), BF16),
        parts,
        out_specs=HBM,
        scratch=[pltpu.VMEM((line, rows, width), BF16), copies_of()],
    )
    sums, up, down = lax.optimization_barrier((sums, up, down))
    ends = exchanged(sums, FIRST)
    up, down = (shifted(added(m1, up), "z", -1), shifted(added(p1, down), "z", 1))

    whole = pl.BlockSpec((rows, width), lambda: (0, 0))
    img_out = local(
        image_end_kernel, shaped((rows, width), F32), images, own, up, down, out_specs=whole
    )
    txt_out = local(text_end_kernel, shaped((rows, width), F32), texts, ends, out_specs=whole)
    return (img_out, txt_out)


def solution(mesh):
    fine = Mesh(mesh.devices.reshape(8, 2, 2, 2, 4), AXES)
    rows = P(AXES, None)
    return jax.shard_map(
        body,
        mesh=fine,
        in_specs=(rows, rows, P(), P()),
        out_specs=(rows, rows),
        check_vma=False,
    )
```

time: 109 us -> 105 us (0.963)
  local copies, waits for them, and re-layouts: 10.9 us -> 1.06 us
  Pallas kernels: 18.9 us -> 25.9 us
  waiting for transfers between devices: 34.1 us -> 31.3 us
  starting transfers between devices: 42.7 us -> 43.9 us
    unnamed x30 -> x16, local copies, waits for them, and re-layouts: 10.9 us -> 1.06 us
    pallas_call x16, Pallas kernels: 18.9 us -> 25.9 us  [local(): pl.pallas_call(kernel, out_shape=outs, in_specs=ins, out_specs=out_specs,...]
    ppermute x16, waiting for transfers between devices: 33.3 us -> 31.3 us  [shifted(): lax.ppermute(value, axis, [(i, (i + by) % length) for i in range(length)])]
    ppermute x16, starting transfers between devices: 23.9 us -> 25.4 us  [shifted(): lax.ppermute(value, axis, [(i, (i + by) % length) for i in range(length)])]
  transfers between devices with their start and end apart: 20 -> 20, of which waited for: 11 -> 9; matrix products, arithmetic and copies ran while one was open for 0% -> 0% of each run, Pallas kernels for 6% -> 16%
where the time goes in v4:
time: 105 us; the launch traced here: 104 us
  starting transfers between devices  43.9 us (42%)
  waiting for transfers between devices  31.3 us (30%)
  Pallas kernels  25.9 us (25%)
  between operations  2.13 us (2%)
  local copies, waits for them, and re-layouts  1.06 us (1%)
    ppermute x16, waiting for transfers between devices, shifted(): lax.ppermute(value, axis, [(i, (i + by) % length) for i in range(length)])  31.3 us
    pallas_call x16, Pallas kernels, local(): pl.pallas_call(kernel, out_shape=outs, in_specs=ins, out_specs=out_specs,...  25.9 us
    ppermute x16, starting transfers between devices, shifted(): lax.ppermute(value, axis, [(i, (i + by) % length) for i in range(length)])  25.4 us
    all_to_all x4, starting transfers between devices, exchanged(): lax.all_to_all(blocks, PLANE, 0, 0, tiled=True, axis_index_groups=groups)  18.6 us
  transfers between devices with their start and end apart: 20, of which 9 were waited for; matrix products, arithmetic and copies ran while one was open for 0% of the time, Pallas kernels for 16%

profile of v4, /device:TPU:8, one launch (start us, length us, event | category | flops | bytes accessed | tf_op | source)
XLA Modules:
  0.0 104.3 jit_solution(6331478389733056367)
XLA Ops:
  0.6 2.1 %shard_map.59 = (bf16[64,1152]{1,0:T(8,128)(2,1)}, bf16[4,64,1152]{2,1,0:T(8,128)(2,1)}) custom-call(f32[64,1152]{1,0:T(8,128)} %raw_ref.2, f32[64,1152]{1,0:T(8,128)} %raw_ref.3), custom_call_target="tpu_custom_call" | custom-call | bytes 589824 | tf_op jit(solution)/shard_map/pallas_call | solution.py:54
  2.7 4.3 %all-to-all-start = ((bf16[4,64,1152]{2,1,0:T(8,128)(2,1)}), bf16[4,64,1152]{2,1,0:T(8,128)(2,1)S(1)}, u32[]{:S(2)}, u32[]{:S(2)}) async-start(bf16[4,64,1152]{2,1,0:T(8,128)(2,1)} %get-tuple-element.25), calls=%async_computation | async-start | bytes 1179648 | tf_op jit(solution)/shard_map/all_to_all | solution.py:32
  7.0 1.9 %collective-permute-start = (bf16[64,1152]{1,0:T(8,128)(2,1)}, bf16[64,1152]{1,0:T(8,128)(2,1)S(1)}, u32[]{:S(2)}, u32[]{:S(2)}) collective-permute-start(bf16[64,1152]{1,0:T(8,128)(2,1)} %get-tuple-element.24.refs_0_), channel_id=1, source_target_pairs={{0,32},{32,64},{64,96},{96,128},{128,160},{160,192},{192,224},{224... | collective-permute-start | bytes 442376 | tf_op jit(solution)/shard_map/ppermute | solution.py:37
  8.9 3.9 %collective-permute-start.1 = (bf16[64,1152]{1,0:T(8,128)(2,1)}, bf16[64,1152]{1,0:T(8,128)(2,1)S(1)}, u32[]{:S(2)}, u32[]{:S(2)}) collective-permute-start(bf16[64,1152]{1,0:T(8,128)(2,1)} %get-tuple-element.24.refs_0_), channel_id=1, source_target_pairs={{0,224},{32,0},{64,32},{96,64},{128,96},{160,128},{192,160},{224,1... | collective-permute-start | bytes 442376 | tf_op jit(solution)/shard_map/ppermute | solution.py:37
  12.9 4.1 %collective-permute-done.refs_1_ = bf16[64,1152]{1,0:T(8,128)(2,1)S(1)} collective-permute-done((bf16[64,1152]{1,0:T(8,128)(2,1)}, bf16[64,1152]{1,0:T(8,128)(2,1)S(1)}, u32[]{:S(2)}, u32[]{:S(2)}) %collective-permute-start) | collective-permute-done | bytes 147488 | tf_op jit(solution)/shard_map/ppermute | solution.py:37
  18.5 4.8 %all-to-all-start.1 = ((bf16[4,256,1152]{2,1,0:T(8,128)(2,1)}), bf16[4,256,1152]{2,1,0:T(8,128)(2,1)S(1)}, u32[]{:S(2)}, u32[]{:S(2)}) async-start(bf16[4,256,1152]{2,1,0:T(8,128)(2,1)} %shard_map.62), calls=%async_computation.1 | async-start | bytes 4718592 | tf_op jit(solution)/shard_map/all_to_all | solution.py:32
  23.8 4.0 %collective-permute-start.3 = (bf16[64,1152]{1,0:T(8,128)(2,1)S(1)}, bf16[64,1152]{1,0:T(8,128)(2,1)S(1)}, u32[]{:S(2)}, u32[]{:S(2)}) collective-permute-start(bf16[64,1152]{1,0:T(8,128)(2,1)S(1)} %collective-permute-done.1.refs_2_), channel_id=1, source_target_pairs={{0,224},{32,0},{64,32},{96,64},{128,96},{160,128},{192,160},{224,1... | collective-permute-start | bytes 442376 | tf_op jit(solution)/shard_map/ppermute | solution.py:37
  27.8 3.1 %collective-permute-done.2.refs_3_ = bf16[64,1152]{1,0:T(8,128)(2,1)S(1)} collective-permute-done((bf16[64,1152]{1,0:T(8,128)(2,1)S(1)}, bf16[64,1152]{1,0:T(8,128)(2,1)S(1)}, u32[]{:S(2)}, u32[]{:S(2)}) %collective-permute-start.2) | collective-permute-done | bytes 147488 | tf_op jit(solution)/shard_map/ppermute | solution.py:37
  30.9 3.6 %collective-permute-start.5 = (bf16[64,1152]{1,0:T(8,128)(2,1)S(1)}, bf16[64,1152]{1,0:T(8,128)(2,1)S(1)}, u32[]{:S(2)}, u32[]{:S(2)}) collective-permute-start(bf16[64,1152]{1,0:T(8,128)(2,1)S(1)} %collective-permute-done.3.refs_4_), channel_id=1, source_target_pairs={{0,224},{32,0},{64,32},{96,64},{128,96},{160,128},{192,160},{224,1... | collective-permute-start | bytes 442376 | tf_op jit(solution)/shard_map/ppermute | solution.py:37
  34.5 4.5 %collective-permute-done.4.refs_5_ = bf16[64,1152]{1,0:T(8,128)(2,1)S(1)} collective-permute-done((bf16[64,1152]{1,0:T(8,128)(2,1)S(1)}, bf16[64,1152]{1,0:T(8,128)(2,1)S(1)}, u32[]{:S(2)}, u32[]{:S(2)}) %collective-permute-start.4) | collective-permute-done | bytes 147488 | tf_op jit(solution)/shard_map/ppermute | solution.py:37
  40.2 5.2 %collective-permute-done.6.refs_1_ = bf16[64,1152]{1,0:T(8,128)(2,1)S(1)} collective-permute-done((bf16[64,1152]{1,0:T(8,128)(2,1)S(1)}, bf16[64,1152]{1,0:T(8,128)(2,1)S(1)}, u32[]{:S(2)}, u32[]{:S(2)}) %collective-permute-start.6) | collective-permute-done | bytes 147488 | tf_op jit(solution)/shard_map/ppermute | solution.py:37
  47.1 4.1 %shard_map.63 = (bf16[512,1024]{1,0:T(8,128)(2,1)S(1)}, f32[512,1152]{1,0:T(8,128)}) custom-call(f32[1]{0:T(128)S(6)} %copy.8.scale_ref, f32[1]{0:T(128)S(6)} %copy.9.bias_ref, s32[1]{0:T(128)} %bitcast.place_ref, bf16[512,1152]{1,0:T(8,128)(2,1)S(1)} %shard_map.61.img_ref.mine_ref, bf16[1024,1152]{1,0:T(8,128)(2,1)S(1)} %bitcast.4), custom_call_target="tpu_custom_call" | custom-call | flops 2415919104 | bytes 3538956 | tf_op jit(solution)/shard_map/pallas_call | solution.py:54
  51.2 4.3 %shard_map.64 = (bf16[512,1024]{1,0:T(8,128)(2,1)S(1)}, bf16[512,1152]{1,0:T(8,128)(2,1)S(1)}) custom-call(f32[1]{0:T(128)S(6)} %copy.8.scale_ref, f32[1]{0:T(128)S(6)} %copy.9.bias_ref, bf16[512,1024]{1,0:T(8,128)(2,1)S(1)} %get-tuple-element.30._.w_mine_ref, bf16[512,1152]{1,0:T(8,128)(2,1)} %collective-permute-done.7.img_ref.theirs_ref, ...), custom_call_target="tpu_custom_call" | custom-call | flops 2415919104 | bytes 4587528 | tf_op jit(solution)/shard_map/pallas_call | solution.py:54
  56.3 5.0 %shard_map.65 = bf16[1024,1152]{1,0:T(8,128)(2,1)} custom-call(f32[1]{0:T(128)S(6)} %copy.8.scale_ref, bf16[512,1024]{1,0:T(8,128)(2,1)S(1)} %get-tuple-element.30._.w_mine_ref, bf16[512,1024]{1,0:T(8,128)(2,1)S(1)} %get-tuple-element.31.w_theirs_ref, bf16[512,1152]{1,0:T(8,128)(2,1)S(1)} %shard_map.61.img_ref.mine_ref, ...), custom_call_target="tpu_custom_call" | custom-call | flops 2415919104 | bytes 4456452 | tf_op jit(solution)/shard_map/pallas_call | solution.py:54
  62.4 4.6 %all-to-all-start.2 = ((bf16[4,256,1152]{2,1,0:T(8,128)(2,1)}), bf16[4,256,1152]{2,1,0:T(8,128)(2,1)S(1)}, u32[]{:S(2)}, u32[]{:S(2)}) async-start(bf16[4,256,1152]{2,1,0:T(8,128)(2,1)} %bitcast.7), calls=%async_computation.2 | async-start | bytes 4718592 | tf_op jit(solution)/shard_map/all_to_all | solution.py:32
  67.0 2.9 %shard_map.66 = (f32[64,1152]{1,0:T(8,128)}, bf16[64,1152]{1,0:T(8,128)(2,1)}, bf16[64,1152]{1,0:T(8,128)(2,1)}, bf16[64,1152]{1,0:T(8,128)(2,1)S(1)}, bf16[64,1...) custom-call(f32[512,1152]{1,0:T(8,128)} %get-tuple-element.29.mine_i, ...), custom_call_target="tpu_custom_call" | custom-call | bytes 3538944 | tf_op jit(solution)/shard_map/pallas_call | solution.py:54
  70.0 2.0 %collective-permute-start.12 = (bf16[64,1152]{1,0:T(8,128)(2,1)S(1)}, bf16[64,1152]{1,0:T(8,128)(2,1)S(1)}, u32[]{:S(2)}, u32[]{:S(2)}) collective-permute-start(bf16[64,1152]{1,0:T(8,128)(2,1)S(1)} %get-tuple-element.41), channel_id=1, source_target_pairs={{0,32},{32,64},{64,96},{96,128},{128,160},{160,192},{192,224},{224... | collective-permute-start | bytes 442376 | tf_op jit(solution)/shard_map/ppermute | solution.py:37
  72.0 3.1 %collective-permute-done.9.b_ref = bf16[64,1152]{1,0:T(8,128)(2,1)S(1)} collective-permute-done((bf16[64,1152]{1,0:T(8,128)(2,1)S(1)}, bf16[64,1152]{1,0:T(8,128)(2,1)S(1)}, u32[]{:S(2)}, u32[]{:S(2)}) %collective-permute-start.9) | collective-permute-done | bytes 147488 | tf_op jit(solution)/shard_map/ppermute | solution.py:37
  77.4 3.0 %collective-permute-done.10.b_ref = bf16[64,1152]{1,0:T(8,128)(2,1)S(1)} collective-permute-done((bf16[64,1152]{1,0:T(8,128)(2,1)S(1)}, bf16[64,1152]{1,0:T(8,128)(2,1)S(1)}, u32[]{:S(2)}, u32[]{:S(2)}) %collective-permute-start.10) | collective-permute-done | bytes 147488 | tf_op jit(solution)/shard_map/ppermute | solution.py:37
  81.1 2.4 %collective-permute-start.11 = (bf16[64,1152]{1,0:T(8,128)(2,1)}, bf16[64,1152]{1,0:T(8,128)(2,1)}, u32[]{:S(2)}, u32[]{:S(2)}) collective-permute-start(bf16[64,1152]{1,0:T(8,128)(2,1)} %shard_map.69), channel_id=1, source_target_pairs={{0,224},{32,0},{64,32},{96,64},{128,96},{160,128},{192,160},{224,1... | collective-permute-start | bytes 442376 | tf_op jit(solution)/shard_map/ppermute | solution.py:37
  86.5 4.8 %all-to-all-start.3 = ((bf16[4,64,1152]{2,1,0:T(8,128)(2,1)}), bf16[4,64,1152]{2,1,0:T(8,128)(2,1)S(1)}, u32[]{:S(2)}, u32[]{:S(2)}) async-start(bf16[4,64,1152]{2,1,0:T(8,128)(2,1)} %shard_map.67), calls=%async_computation.3 | async-start | bytes 1179648 | tf_op jit(solution)/shard_map/all_to_all | solution.py:32
  92.3 3.8 %collective-permute-start.14 = (bf16[64,1152]{1,0:T(8,128)(2,1)S(1)}, bf16[64,1152]{1,0:T(8,128)(2,1)S(1)}, u32[]{:S(2)}, u32[]{:S(2)}) collective-permute-start(bf16[64,1152]{1,0:T(8,128)(2,1)S(1)} %shard_map.71), channel_id=1, source_target_pairs={{0,224},{32,0},{64,32},{96,64},{128,96},{160,128},{192,160},{224,1... | collective-permute-start | bytes 442376 | tf_op jit(solution)/shard_map/ppermute | solution.py:37
  96.2 2.5 %collective-permute-done.14.up_ref = bf16[64,1152]{1,0:T(8,128)(2,1)S(1)} collective-permute-done((bf16[64,1152]{1,0:T(8,128)(2,1)S(1)}, bf16[64,1152]{1,0:T(8,128)(2,1)S(1)}, u32[]{:S(2)}, u32[]{:S(2)}) %collective-permute-start.14) | collective-permute-done | bytes 147488 | tf_op jit(solution)/shard_map/ppermute | solution.py:37
  98.7 3.8 %collective-permute-done.15.down_ref = bf16[64,1152]{1,0:T(8,128)(2,1)S(1)} collective-permute-done((bf16[64,1152]{1,0:T(8,128)(2,1)S(1)}, bf16[64,1152]{1,0:T(8,128)(2,1)S(1)}, u32[]{:S(2)}, u32[]{:S(2)}) %collective-permute-start.15) | collective-permute-done | bytes 147488 | tf_op jit(solution)/shard_map/ppermute | solution.py:37
  (48 shorter events, 14.1 us)
Async XLA Ops:
  2.7 14.3 %all-to-all-start = ((bf16[4,64,1152]{2,1,0:T(8,128)(2,1)}), bf16[4,64,1152]{2,1,0:T(8,128)(2,1)S(1)}, u32[]{:S(2)}, u32[]{:S(2)}) async-start(bf16[4,64,1152]{2,1,0:T(8,128)(2,1)} %get-tuple-element.25), calls=%async_computation | async-start | bytes 1179648 | tf_op jit(solution)/shard_map/all_to_all | solution.py:32
  7.0 10.0 %collective-permute-start = (bf16[64,1152]{1,0:T(8,128)(2,1)}, bf16[64,1152]{1,0:T(8,128)(2,1)S(1)}, u32[]{:S(2)}, u32[]{:S(2)}) collective-permute-start(bf16[64,1152]{1,0:T(8,128)(2,1)} %get-tuple-element.24.refs_0_), channel_id=1, source_target_pairs={{0,32},{32,64},{64,96},{96,128},{128,160},{160,192},{192,224},{224... | collective-permute-start | bytes 442376 | tf_op jit(solution)/shard_map/ppermute | solution.py:37
  8.9 8.1 %collective-permute-start.1 = (bf16[64,1152]{1,0:T(8,128)(2,1)}, bf16[64,1152]{1,0:T(8,128)(2,1)S(1)}, u32[]{:S(2)}, u32[]{:S(2)}) collective-permute-start(bf16[64,1152]{1,0:T(8,128)(2,1)} %get-tuple-element.24.refs_0_), channel_id=1, source_target_pairs={{0,224},{32,0},{64,32},{96,64},{128,96},{160,128},{192,160},{224,1... | collective-permute-start | bytes 442376 | tf_op jit(solution)/shard_map/ppermute | solution.py:37
  18.5 28.5 %all-to-all-start.1 = ((bf16[4,256,1152]{2,1,0:T(8,128)(2,1)}), bf16[4,256,1152]{2,1,0:T(8,128)(2,1)S(1)}, u32[]{:S(2)}, u32[]{:S(2)}) async-start(bf16[4,256,1152]{2,1,0:T(8,128)(2,1)} %shard_map.62), calls=%async_computation.1 | async-start | bytes 4718592 | tf_op jit(solution)/shard_map/all_to_all | solution.py:32
  23.3 7.5 %collective-permute-start.2 = (bf16[64,1152]{1,0:T(8,128)(2,1)S(1)}, bf16[64,1152]{1,0:T(8,128)(2,1)S(1)}, u32[]{:S(2)}, u32[]{:S(2)}) collective-permute-start(bf16[64,1152]{1,0:T(8,128)(2,1)S(1)} %collective-permute-done.refs_1_), channel_id=1, source_target_pairs={{0,32},{32,64},{64,96},{96,128},{128,160},{160,192},{192,224},{224... | collective-permute-start | bytes 442376 | tf_op jit(solution)/shard_map/ppermute | solution.py:37
  23.8 7.1 %collective-permute-start.3 = (bf16[64,1152]{1,0:T(8,128)(2,1)S(1)}, bf16[64,1152]{1,0:T(8,128)(2,1)S(1)}, u32[]{:S(2)}, u32[]{:S(2)}) collective-permute-start(bf16[64,1152]{1,0:T(8,128)(2,1)S(1)} %collective-permute-done.1.refs_2_), channel_id=1, source_target_pairs={{0,224},{32,0},{64,32},{96,64},{128,96},{160,128},{192,160},{224,1... | collective-permute-start | bytes 442376 | tf_op jit(solution)/shard_map/ppermute | solution.py:37
  30.9 8.2 %collective-permute-start.4 = (bf16[64,1152]{1,0:T(8,128)(2,1)S(1)}, bf16[64,1152]{1,0:T(8,128)(2,1)S(1)}, u32[]{:S(2)}, u32[]{:S(2)}) collective-permute-start(bf16[64,1152]{1,0:T(8,128)(2,1)S(1)} %collective-permute-done.2.refs_3_), channel_id=1, source_target_pairs={{0,32},{32,64},{64,96},{96,128},{128,160},{160,192},{192,224},{224... | collective-permute-start | bytes 442376 | tf_op jit(solution)/shard_map/ppermute | solution.py:37
  30.9 8.2 %collective-permute-start.5 = (bf16[64,1152]{1,0:T(8,128)(2,1)S(1)}, bf16[64,1152]{1,0:T(8,128)(2,1)S(1)}, u32[]{:S(2)}, u32[]{:S(2)}) collective-permute-start(bf16[64,1152]{1,0:T(8,128)(2,1)S(1)} %collective-permute-done.3.refs_4_), channel_id=1, source_target_pairs={{0,224},{32,0},{64,32},{96,64},{128,96},{160,128},{192,160},{224,1... | collective-permute-start | bytes 442376 | tf_op jit(solution)/shard_map/ppermute | solution.py:37
  39.0 6.4 %collective-permute-start.6 = (bf16[64,1152]{1,0:T(8,128)(2,1)S(1)}, bf16[64,1152]{1,0:T(8,128)(2,1)S(1)}, u32[]{:S(2)}, u32[]{:S(2)}) collective-permute-start(bf16[64,1152]{1,0:T(8,128)(2,1)S(1)} %collective-permute-done.4.refs_5_), channel_id=1, source_target_pairs={{0,32},{32,64},{64,96},{96,128},{128,160},{160,192},{192,224},{224... | collective-permute-start | bytes 442376 | tf_op jit(solution)/shard_map/ppermute | solution.py:37
  45.6 5.5 %collective-permute-start.7 = (bf16[512,1152]{1,0:T(8,128)(2,1)S(1)}, bf16[512,1152]{1,0:T(8,128)(2,1)}, u32[]{:S(2)}, u32[]{:S(2)}) collective-permute-start(bf16[512,1152]{1,0:T(8,128)(2,1)S(1)} %shard_map.61.img_ref.mine_ref), channel_id=1, source_target_pairs={{0,8},{8,0},{1,9},{9,1},{2,10},{10,2},{3,11},{11,3},{4,12},{12,4},... | collective-permute-start | bytes 3538952 | tf_op jit(solution)/shard_map/ppermute | solution.py:37
  55.5 5.8 %collective-permute-start.8 = (bf16[512,1152]{1,0:T(8,128)(2,1)S(1)}, bf16[512,1152]{1,0:T(8,128)(2,1)S(1)}, u32[]{:S(2)}, u32[]{:S(2)}) collective-permute-start(bf16[512,1152]{1,0:T(8,128)(2,1)S(1)} %get-tuple-element.32), channel_id=1, source_target_pairs={{0,8},{8,0},{1,9},{9,1},{2,10},{10,2},{3,11},{11,3},{4,12},{12,4},... | collective-permute-start | bytes 3538952 | tf_op jit(solution)/shard_map/ppermute | solution.py:37
  62.4 21.1 %all-to-all-start.2 = ((bf16[4,256,1152]{2,1,0:T(8,128)(2,1)}), bf16[4,256,1152]{2,1,0:T(8,128)(2,1)S(1)}, u32[]{:S(2)}, u32[]{:S(2)}) async-start(bf16[4,256,1152]{2,1,0:T(8,128)(2,1)} %bitcast.7), calls=%async_computation.2 | async-start | bytes 4718592 | tf_op jit(solution)/shard_map/all_to_all | solution.py:32
  69.9 5.2 %collective-permute-start.9 = (bf16[64,1152]{1,0:T(8,128)(2,1)S(1)}, bf16[64,1152]{1,0:T(8,128)(2,1)S(1)}, u32[]{:S(2)}, u32[]{:S(2)}) collective-permute-start(bf16[64,1152]{1,0:T(8,128)(2,1)S(1)} %get-tuple-element.39), channel_id=1, source_target_pairs={{0,224},{32,0},{64,32},{96,64},{128,96},{160,128},{192,160},{224,1... | collective-permute-start | bytes 442376 | tf_op jit(solution)/shard_map/ppermute | solution.py:37
  70.0 6.5 %collective-permute-start.12 = (bf16[64,1152]{1,0:T(8,128)(2,1)S(1)}, bf16[64,1152]{1,0:T(8,128)(2,1)S(1)}, u32[]{:S(2)}, u32[]{:S(2)}) collective-permute-start(bf16[64,1152]{1,0:T(8,128)(2,1)S(1)} %get-tuple-element.41), channel_id=1, source_target_pairs={{0,32},{32,64},{64,96},{96,128},{128,160},{160,192},{192,224},{224... | collective-permute-start | bytes 442376 | tf_op jit(solution)/shard_map/ppermute | solution.py:37
  75.1 5.2 %collective-permute-start.10 = (bf16[64,1152]{1,0:T(8,128)(2,1)S(1)}, bf16[64,1152]{1,0:T(8,128)(2,1)S(1)}, u32[]{:S(2)}, u32[]{:S(2)}) collective-permute-start(bf16[64,1152]{1,0:T(8,128)(2,1)S(1)} %shard_map.68), channel_id=1, source_target_pairs={{0,224},{32,0},{64,32},{96,64},{128,96},{160,128},{192,160},{224,1... | collective-permute-start | bytes 442376 | tf_op jit(solution)/shard_map/ppermute | solution.py:37
  76.5 8.1 %collective-permute-start.13 = (bf16[64,1152]{1,0:T(8,128)(2,1)S(1)}, bf16[64,1152]{1,0:T(8,128)(2,1)S(1)}, u32[]{:S(2)}, u32[]{:S(2)}) collective-permute-start(bf16[64,1152]{1,0:T(8,128)(2,1)S(1)} %shard_map.70), channel_id=1, source_target_pairs={{0,32},{32,64},{64,96},{96,128},{128,160},{160,192},{192,224},{224... | collective-permute-start | bytes 442376 | tf_op jit(solution)/shard_map/ppermute | solution.py:37
  81.1 15.0 %copy-start.3 = (bf16[64,1152]{1,0:T(8,128)(2,1)S(1)}, bf16[64,1152]{1,0:T(8,128)(2,1)}, u32[]{:S(2)}) copy-start(bf16[64,1152]{1,0:T(8,128)(2,1)} %get-tuple-element.43.a_ref) | copy-start | bytes 442372
  81.1 21.5 %copy-start = (f32[64,1152]{1,0:T(8,128)S(1)}, f32[64,1152]{1,0:T(8,128)}, u32[]{:S(2)}) copy-start(f32[64,1152]{1,0:T(8,128)} %raw_ref.2) | copy-start | bytes 884740
  81.1 21.5 %copy-start.2 = (f32[64,1152]{1,0:T(8,128)S(1)}, f32[64,1152]{1,0:T(8,128)}, u32[]{:S(2)}) copy-start(f32[64,1152]{1,0:T(8,128)} %get-tuple-element.34.own_ref) | copy-start | bytes 884740
  81.1 5.5 %collective-permute-start.11 = (bf16[64,1152]{1,0:T(8,128)(2,1)}, bf16[64,1152]{1,0:T(8,128)(2,1)}, u32[]{:S(2)}, u32[]{:S(2)}) collective-permute-start(bf16[64,1152]{1,0:T(8,128)(2,1)} %shard_map.69), channel_id=1, source_target_pairs={{0,224},{32,0},{64,32},{96,64},{128,96},{160,128},{192,160},{224,1... | collective-permute-start | bytes 442376 | tf_op jit(solution)/shard_map/ppermute | solution.py:37
  84.6 18.8 %copy-start.1 = (f32[64,1152]{1,0:T(8,128)S(1)}, f32[64,1152]{1,0:T(8,128)}, u32[]{:S(2)}) copy-start(f32[64,1152]{1,0:T(8,128)} %raw_ref.3) | copy-start | bytes 884740
  86.5 16.9 %all-to-all-start.3 = ((bf16[4,64,1152]{2,1,0:T(8,128)(2,1)}), bf16[4,64,1152]{2,1,0:T(8,128)(2,1)S(1)}, u32[]{:S(2)}, u32[]{:S(2)}) async-start(bf16[4,64,1152]{2,1,0:T(8,128)(2,1)} %shard_map.67), calls=%async_computation.3 | async-start | bytes 1179648 | tf_op jit(solution)/shard_map/all_to_all | solution.py:32
  92.3 6.4 %collective-permute-start.14 = (bf16[64,1152]{1,0:T(8,128)(2,1)S(1)}, bf16[64,1152]{1,0:T(8,128)(2,1)S(1)}, u32[]{:S(2)}, u32[]{:S(2)}) collective-permute-start(bf16[64,1152]{1,0:T(8,128)(2,1)S(1)} %shard_map.71), channel_id=1, source_target_pairs={{0,224},{32,0},{64,32},{96,64},{128,96},{160,128},{192,160},{224,1... | collective-permute-start | bytes 442376 | tf_op jit(solution)/shard_map/ppermute | solution.py:37
  96.1 6.4 %collective-permute-start.15 = (bf16[64,1152]{1,0:T(8,128)(2,1)S(1)}, bf16[64,1152]{1,0:T(8,128)(2,1)S(1)}, u32[]{:S(2)}, u32[]{:S(2)}) collective-permute-start(bf16[64,1152]{1,0:T(8,128)(2,1)S(1)} %shard_map.72), channel_id=1, source_target_pairs={{0,32},{32,64},{64,96},{96,128},{128,160},{160,192},{192,224},{224... | collective-permute-start | bytes 442376 | tf_op jit(solution)/shard_map/ppermute | solution.py:37
  (4 other events, 29.0 us)

commit v5 on v1

v5 whole, which is shorter than its diff:
```python
import functools

import jax
import jax.numpy as jnp
from jax import lax
from jax.experimental import pallas as pl
from jax.experimental.pallas import tpu as pltpu
from jax.sharding import Mesh, PartitionSpec as P

AXES = ("z", "yh", "c", "yl", "x")
PLANE = ("yh", "c", "yl", "x")
SIDE = 4
BF16 = jnp.bfloat16
F32 = jnp.float32
VMEM = pl.BlockSpec(memory_space=pltpu.VMEM)
SMEM = pl.BlockSpec(memory_space=pltpu.SMEM)
TILE = 256


def shifted(value, axis, by):
    length = lax.axis_size(axis)
    return lax.ppermute(value, axis, [(i, (i + by) % length) for i in range(length)])


def crossed(value, first, by):
    at = lambda y, c, x: ((y // 2 * 2 + c) * 2 + y % 2) * SIDE + x
    pairs = []
    for c in range(2):
        along_x = (c == 0) == first
        for y in range(SIDE):
            for x in range(SIDE):
                to = (y, c, (x + by) % SIDE) if along_x else ((y + by) % SIDE, c, x)
                pairs.append((at(y, c, x), at(*to)))
    return lax.ppermute(value, PLANE, pairs)


def shaped(shape, dtype):
    return jax.ShapeDtypeStruct(shape, dtype)


def local(kernel, outs, *args, scalars=0, out_specs=None, flops=0):
    many = isinstance(outs, list)
    return pl.pallas_call(
        kernel,
        out_shape=outs,
        in_specs=[SMEM] * scalars + [VMEM] * (len(args) - scalars),
        out_specs=out_specs or ([VMEM] * len(outs) if many else VMEM),
        compiler_params=pltpu.CompilerParams(vmem_limit_bytes=16 * 2**20),
        cost_estimate=pl.CostEstimate(
            flops=flops,
            bytes_accessed=sum(a.size * a.dtype.itemsize for a in args),
            transcendentals=0,
        ),
    )(*args)


def matmul(a, b, contract):
    return lax.dot_general(a, b, (contract, ((), ())), preferred_element_type=F32)


def inverse(raw):
    return lax.rsqrt(jnp.sum(raw * raw, axis=1, keepdims=True) + 1e-06)


def normalize_kernel(img_ref, txt_ref, img_out, txt_out):
    for raw, out in ((txt_ref, txt_out), (img_ref, img_out)):
        out[...] = (raw[...] * inverse(raw[...])).astype(BF16)


def join_kernel(*refs):
    *blocks, out_ref = refs
    at = 0
    for block in blocks:
        out_ref[pl.ds(at, block.shape[0]), :] = block[...]
        at += block.shape[0]


def weights_of(images, texts, scale, bias, paired):
    logits = scale * matmul(images, texts, ((1,), (1,))) + bias
    if not paired:
        return (1.0 / (1.0 + jnp.exp(-logits))).astype(BF16)
    img_at = lax.broadcasted_iota(jnp.int32, logits.shape, 0)
    txt_at = lax.broadcasted_iota(jnp.int32, logits.shape, 1)
    sign = jnp.where((img_at == txt_at) & (img_at < paired), 1.0, -1.0).astype(F32)
    return (-sign / (1.0 + jnp.exp(sign * logits))).astype(BF16)


def image_kernel(paired, scale_ref, bias_ref, txt_ref, *refs):
    *blocks, w_ref, d_ref, img_ref = refs
    scale = scale_ref[0]
    for i, block in enumerate(blocks):
        tile = pl.ds(i * block.shape[0], block.shape[0])
        images = block[...]
        img_ref[tile, :] = images
        weights = weights_of(images, txt_ref[...], scale, bias_ref[0], 0 if i else paired)
        w_ref[tile, :] = weights
        d_ref[tile, :] = (scale * matmul(weights, txt_ref[...], ((1,), (0,)))).astype(d_ref.dtype)


def text_kernel(places, scale_ref, w_mine_ref, w_theirs_ref, mine_ref, theirs_ref, *outs):
    for place, out in zip(places, outs):
        cols = pl.ds(place * TILE, TILE)
        total = matmul(w_mine_ref[:, cols], mine_ref[...], ((0,), (0,)))
        total += matmul(w_theirs_ref[:, cols], theirs_ref[...], ((0,), (0,)))
        out[...] = (scale_ref[0] * total).astype(out.dtype)


def split_kernel(count, *refs):
    arrays, outs = (refs[:count], refs[count:])
    rows = outs[0].shape[0]
    for i in reversed(range(len(outs))):
        tile = pl.ds(i * rows, rows)
        total = arrays[0][tile, :].astype(F32)
        for array in arrays[1:]:
            total += array[tile, :].astype(F32)
        outs[i][...] = total.astype(outs[i].dtype)


def add_kernel(a_ref, b_ref, out_ref):
    out_ref[...] = (a_ref[...].astype(F32) + b_ref[...].astype(F32)).astype(BF16)


def end_kernel(raw_ref, *refs):
    *parts, out_ref = refs
    raw, grad = (raw_ref[...], parts[0][...].astype(F32))
    for part in parts[1:]:
        grad += part[...].astype(F32)
    inv = inverse(raw)
    across = jnp.sum(raw * grad, axis=1, keepdims=True)
    out_ref[...] = inv * grad - raw * (inv * inv * inv) * across


def added(a, b):
    return local(add_kernel, shaped(a.shape, BF16), a, b)


def body(images, texts, scale, bias):
    rows, width = images.shape
    line, half, all_txt = (SIDE * rows, 8 * rows, SIDE * SIDE * rows)
    block = shaped((rows, width), BF16)
    join = lambda *parts: local(
        join_kernel, shaped((sum(part.shape[0] for part in parts), width), BF16), *parts
    )
    img, txt = local(normalize_kernel, [block, block], images, texts)

    ahead, behind, across = [crossed(txt, True, by) for by in (1, -1, 2)]
    up1, down1, far = (shifted(img, "z", 1), shifted(img, "z", -1), shifted(img, "z", 4))
    texts0 = join(txt, ahead, behind, across)
    texts1, texts2, texts3 = [crossed(texts0, False, by) for by in (1, -1, 2)]
    up2, down2 = (shifted(up1, "z", 1), shifted(down1, "z", -1))
    mine_a = join(img, up1, down1, far)
    theirs_a = shifted(mine_a, "c", 1)
    up3, down3 = (shifted(up2, "z", 1), shifted(down2, "z", -1))
    mine_b = join(up2, down2, up3, down3)
    theirs_b = shifted(mine_b, "c", 1)
    txt_all = join(texts0, texts1, texts2, texts3)

    flops = 2 * half * all_txt * width
    halves = lambda paired, kind, *parts: local(
        functools.partial(image_kernel, paired),
        [shaped((half, all_txt), BF16), shaped((half, width), kind), shaped((half, width), BF16)],
        scale, bias, txt_all, *parts,
        scalars=2, flops=2 * flops,
    )
    w_mine, d_mine, mine = halves(rows, F32, mine_a, mine_b)
    w_theirs, d_theirs, theirs = halves(0, BF16, theirs_a, theirs_b)
    back = shifted(d_theirs, "c", 1)
    gradients = lambda places, kind: local(
        functools.partial(text_kernel, places),
        [shaped((line, width), kind) for _ in places],
        scale, w_mine, w_theirs, mine, theirs,
        scalars=1, flops=2 * flops * len(places) // SIDE,
    )
    d_texts3, d_texts1, d_texts2 = gradients((3, 1, 2), BF16)
    d_texts0 = gradients((0,), F32)[0]

    back3, back1, back2 = (
        crossed(d_texts3, False, 2),
        crossed(d_texts1, False, -1),
        crossed(d_texts2, False, 1),
    )
    kinds = [F32] + [BF16] * 7
    own, m1, p1, d_far, m2, p2, m3, p3 = local(
        functools.partial(split_kernel, 2),
        [shaped((rows, width), kind) for kind in kinds],
        d_mine, back,
    )
    up, down = (shifted(m3, "z", -1), shifted(p3, "z", 1))
    d_far = shifted(d_far, "z", 4)
    up, down = (shifted(added(m2, up), "z", -1), shifted(added(p2, down), "z", 1))
    up, down = (shifted(added(m1, up), "z", -1), shifted(added(p1, down), "z", 1))
    txt_own, d_ahead, d_behind, d_across = local(
        functools.partial(split_kernel, 4),
        [shaped((rows, width), kind) for kind in kinds[:SIDE]],
        d_texts0, back1, back2, back3,
    )
    d_ahead, d_behind, d_across = (
        crossed(d_ahead, True, -1),
        crossed(d_behind, True, 1),
        crossed(d_across, True, 2),
    )

    whole = pl.BlockSpec((rows, width), lambda: (0, 0))
    end = lambda raw, *parts: local(
        end_kernel, shaped((rows, width), F32), raw, *parts, out_specs=whole
    )
    return (end(images, own, up, down, d_far), end(texts, txt_own, d_ahead, d_behind, d_across))


def solution(mesh):
    fine = Mesh(mesh.devices.reshape(8, 2, 2, 2, 4), AXES)
    rows = P(AXES, None)
    return jax.shard_map(
        body,
        mesh=fine,
        in_specs=(rows, rows, P(), P()),
        out_specs=(rows, rows),
        check_vma=False,
    )
```

time: 118 us -> 93.5 us (0.79)
  other arithmetic: 13.5 us -> 0 us
  matrix products: 13.3 us -> 0 us
  Pallas kernels: 0 us -> 12 us
  local copies, waits for them, and re-layouts: 10.5 us -> 1.93 us
    ppermute x0 -> x12, waiting for transfers between devices: none -> 22.2 us  [crossed(): return lax.ppermute(value, PLANE, pairs)]
    ppermute x0 -> x12, starting transfers between devices: none -> 14.8 us  [crossed(): return lax.ppermute(value, PLANE, pairs)]
    all_to_all x2 -> x0, waiting for transfers between devices: 14 us -> none  [the longest x1 7.96 us: body(): lax.all_to_all(copies, PLANE, 0, 0, tiled=True).reshape(plane * rows, width)]
    dot_general x3 -> x0, matrix products: 13.3 us -> none  [the longest x1 6.22 us: body(): lax.dot_general(txt, img, (((1,), (1,)), ((), ())), preferred_element_typ...]
    all_to_all x2 -> x0, starting transfers between devices: 12.5 us -> none  [the longest x1 7.39 us: body(): lax.all_to_all(copies, PLANE, 0, 0, tiled=True).reshape(plane * rows, width)]
    pallas_call x0 -> x17, Pallas kernels: none -> 12 us  [local(): pl.pallas_call(kernel, out_shape=outs, in_specs=[SMEM] * scalars + [VMEM]...]
    ppermute x18 -> x17, waiting for transfers between devices: 22.1 us -> 12.8 us  [shifted(): lax.ppermute(value, axis, [(i, (i + by) % length) for i in range(length)])]
    unnamed x16 -> x8, local copies, waits for them, and re-layouts: 6.19 us -> 1.93 us
  transfers between devices with their start and end apart: 20 -> 29, of which waited for: 12 -> 13; matrix products, arithmetic and copies ran while one was open for 17% -> 0% of each run, Pallas kernels for 0% -> 9%
where the time goes in v5:
time: 93.5 us; the launch traced here: 92.1 us
  starting transfers between devices  41 us (44%)
  waiting for transfers between devices  35 us (37%)
  Pallas kernels  12 us (13%)
  between operations  2.16 us (2%)
  local copies, waits for them, and re-layouts  1.93 us (2%)
    ppermute x17, starting transfers between devices, shifted(): lax.ppermute(value, axis, [(i, (i + by) % length) for i in range(length)])  26.2 us
    ppermute x12, waiting for transfers between devices, crossed(): return lax.ppermute(value, PLANE, pairs)  22.2 us
    ppermute x12, starting transfers between devices, crossed(): return lax.ppermute(value, PLANE, pairs)  14.8 us
    ppermute x17, waiting for transfers between devices, shifted(): lax.ppermute(value, axis, [(i, (i + by) % length) for i in range(length)])  12.8 us
    pallas_call x17, Pallas kernels, local(): pl.pallas_call(kernel, out_shape=outs, in_specs=[SMEM] * scalars + [VMEM]...  12 us
    unnamed x8, local copies, waits for them, and re-layouts  1.93 us
  transfers between devices with their start and end apart: 29, of which 13 were waited for; matrix products, arithmetic and copies ran while one was open for 0% of the time, Pallas kernels for 9%

profile of v5, /device:TPU:8, one launch (start us, length us, event | category | flops | bytes accessed | tf_op | source)
XLA Modules:
  0.0 92.1 jit_solution(17961297835463483763)
XLA Ops:
  2.7 5.9 %collective-permute-start.7 = (bf16[64,1152]{1,0:T(8,128)(2,1)S(1)}, bf16[64,1152]{1,0:T(8,128)(2,1)S(1)}, u32[]{:S(2)}, u32[]{:S(2)}) collective-permute-start(bf16[64,1152]{1,0:T(8,128)(2,1)S(1)} %get-tuple-element.26.refs_0_), channel_id=1, source_target_pairs={{0,224},{32,0},{64,32},{96,64},{128,96},{160,128},{192,160},{224,1... | collective-permute-start | bytes 442376 | tf_op jit(solution)/shard_map/ppermute | solution.py:22
  8.6 3.0 %collective-permute-start.2 = (bf16[64,1152]{1,0:T(8,128)(2,1)S(1)}, bf16[64,1152]{1,0:T(8,128)(2,1)S(1)}, u32[]{:S(2)}, u32[]{:S(2)}) collective-permute-start(bf16[64,1152]{1,0:T(8,128)(2,1)S(1)} %get-tuple-element.25.refs_0_), channel_id=1, source_target_pairs={{0,2},{1,3},{2,0},{3,1},{4,6},{5,7},{6,4},{7,5},{16,18},{17,19},{1... | collective-permute-start | bytes 442376 | tf_op jit(solution)/shard_map/ppermute | solution.py:34
  11.7 3.7 %collective-permute-start.10 = (bf16[64,1152]{1,0:T(8,128)(2,1)S(1)}, bf16[64,1152]{1,0:T(8,128)(2,1)S(1)}, u32[]{:S(2)}, u32[]{:S(2)}) collective-permute-start(bf16[64,1152]{1,0:T(8,128)(2,1)S(1)} %collective-permute-done.7.refs_2_), channel_id=1, source_target_pairs={{0,224},{32,0},{64,32},{96,64},{128,96},{160,128},{192,160},{224,1... | collective-permute-start | bytes 442376 | tf_op jit(solution)/shard_map/ppermute | solution.py:22
  15.4 2.8 %collective-permute-start.1 = (bf16[64,1152]{1,0:T(8,128)(2,1)S(1)}, bf16[64,1152]{1,0:T(8,128)(2,1)S(1)}, u32[]{:S(2)}, u32[]{:S(2)}) collective-permute-start(bf16[64,1152]{1,0:T(8,128)(2,1)S(1)} %get-tuple-element.25.refs_0_), channel_id=1, source_target_pairs={{0,3},{1,0},{2,1},{3,2},{4,7},{5,4},{6,5},{7,6},{16,19},{17,16},{1... | collective-permute-start | bytes 442376 | tf_op jit(solution)/shard_map/ppermute | solution.py:34
  18.2 2.1 %collective-permute-start.8 = (bf16[64,1152]{1,0:T(8,128)(2,1)S(1)}, bf16[64,1152]{1,0:T(8,128)(2,1)S(1)}, u32[]{:S(2)}, u32[]{:S(2)}) collective-permute-start(bf16[64,1152]{1,0:T(8,128)(2,1)S(1)} %get-tuple-element.26.refs_0_), channel_id=1, source_target_pairs={{0,128},{32,160},{64,192},{96,224},{128,0},{160,32},{192,64},{224,... | collective-permute-start | bytes 442376 | tf_op jit(solution)/shard_map/ppermute | solution.py:22
  20.3 2.7 %collective-permute-start.12 = (bf16[64,1152]{1,0:T(8,128)(2,1)S(1)}, bf16[64,1152]{1,0:T(8,128)(2,1)S(1)}, u32[]{:S(2)}, u32[]{:S(2)}) collective-permute-start(bf16[64,1152]{1,0:T(8,128)(2,1)S(1)} %collective-permute-done.10.refs_1_), channel_id=1, source_target_pairs={{0,224},{32,0},{64,32},{96,64},{128,96},{160,128},{192,160},{224,1... | collective-permute-start | bytes 442376 | tf_op jit(solution)/shard_map/ppermute | solution.py:22
  23.1 4.0 %collective-permute-done.9.refs_0_ = bf16[64,1152]{1,0:T(8,128)(2,1)S(1)} collective-permute-done((bf16[64,1152]{1,0:T(8,128)(2,1)S(1)}, bf16[64,1152]{1,0:T(8,128)(2,1)S(1)}, u32[]{:S(2)}, u32[]{:S(2)}) %collective-permute-start.9) | collective-permute-done | bytes 147488 | tf_op jit(solution)/shard_map/ppermute | solution.py:22
  27.1 4.1 %collective-permute-done.refs_1_ = bf16[64,1152]{1,0:T(8,128)(2,1)S(1)} collective-permute-done((bf16[64,1152]{1,0:T(8,128)(2,1)S(1)}, bf16[64,1152]{1,0:T(8,128)(2,1)S(1)}, u32[]{:S(2)}, u32[]{:S(2)}) %collective-permute-start) | collective-permute-done | bytes 147488 | tf_op jit(solution)/shard_map/ppermute | solution.py:34
  31.3 3.6 %collective-permute-start.4 = (bf16[256,1152]{1,0:T(8,128)(2,1)S(1)}, bf16[256,1152]{1,0:T(8,128)(2,1)S(1)}, u32[]{:S(2)}, u32[]{:S(2)}) collective-permute-start(bf16[256,1152]{1,0:T(8,128)(2,1)S(1)} %shard_map.60.refs_0_), channel_id=1, source_target_pairs={{0,20},{1,21},{2,22},{3,23},{4,0},{5,1},{6,2},{7,3},{16,4},{17,5},... | collective-permute-start | bytes 1769480 | tf_op jit(solution)/shard_map/ppermute | solution.py:34
  37.2 5.6 %collective-permute-done.5.refs_3_ = bf16[256,1152]{1,0:T(8,128)(2,1)S(1)} collective-permute-done((bf16[256,1152]{1,0:T(8,128)(2,1)S(1)}, bf16[256,1152]{1,0:T(8,128)(2,1)S(1)}, u32[]{:S(2)}, u32[]{:S(2)}) %collective-permute-start.5) | collective-permute-done | bytes 589856 | tf_op jit(solution)/shard_map/ppermute | solution.py:34
  42.8 4.8 %collective-permute-done.4.refs_2_ = bf16[256,1152]{1,0:T(8,128)(2,1)S(1)} collective-permute-done((bf16[256,1152]{1,0:T(8,128)(2,1)S(1)}, bf16[256,1152]{1,0:T(8,128)(2,1)S(1)}, u32[]{:S(2)}, u32[]{:S(2)}) %collective-permute-start.4) | collective-permute-done | bytes 589856 | tf_op jit(solution)/shard_map/ppermute | solution.py:34
  47.6 1.6 %collective-permute-done.3.refs_1_ = bf16[256,1152]{1,0:T(8,128)(2,1)S(1)} collective-permute-done((bf16[256,1152]{1,0:T(8,128)(2,1)S(1)}, bf16[256,1152]{1,0:T(8,128)(2,1)S(1)}, u32[]{:S(2)}, u32[]{:S(2)}) %collective-permute-start.3) | collective-permute-done | bytes 589856 | tf_op jit(solution)/shard_map/ppermute | solution.py:34
  49.4 3.1 %shard_map.65 = (bf16[512,1024]{1,0:T(8,128)(2,1)S(1)}, bf16[512,1152]{1,0:T(8,128)(2,1)S(1)}, bf16[512,1152]{1,0:T(8,128)(2,1)S(1)}) custom-call(f32[1]{0:T(128)S(6)} %copy.6.scale_ref, f32[1]{0:T(128)S(6)} %copy.7.bias_ref, bf16[1024,1152]{1,0:T(8,128)(2,1)S(1)} %shard_map.61.txt_ref, bf16[256,1152]{1,0:T(8,128)(2,1)S(1)} %collective-permute-done.13.refs_0_, ...), custom_call_target="tpu_custom_call" | custom-call | flops 2415919104 | bytes 3538952 | tf_op jit(solution)/shard_map/pallas_call | solution.py:43
  52.5 3.0 %shard_map.64 = (bf16[512,1024]{1,0:T(8,128)(2,1)S(1)}, f32[512,1152]{1,0:T(8,128)S(1)}, bf16[512,1152]{1,0:T(8,128)(2,1)S(1)}) custom-call(f32[1]{0:T(128)S(6)} %copy.6.scale_ref, f32[1]{0:T(128)S(6)} %copy.7.bias_ref, bf16[1024,1152]{1,0:T(8,128)(2,1)S(1)} %shard_map.61.txt_ref, bf16[256,1152]{1,0:T(8,128)(2,1)S(1)} %shard_map.62.refs_0_, ...), custom_call_target="tpu_custom_call" | custom-call | flops 2415919104 | bytes 3538952 | tf_op jit(solution)/shard_map/pallas_call | solution.py:43
  55.6 2.2 %shard_map.73 = (bf16[256,1152]{1,0:T(8,128)(2,1)S(1)}, bf16[256,1152]{1,0:T(8,128)(2,1)S(1)}, bf16[256,1152]{1,0:T(8,128)(2,1)S(1)}) custom-call(f32[1]{0:T(128)S(6)} %copy.6.scale_ref, bf16[512,1024]{1,0:T(8,128)(2,1)S(1)} %get-tuple-element.37.w_mine_ref, bf16[512,1024]{1,0:T(8,128)(2,1)S(1)} %get-tuple-element.38.w_theirs_ref, ...), custom_call_target="tpu_custom_call" | custom-call | flops 1811939328 | bytes 4456452 | tf_op jit(solution)/shard_map/pallas_call | solution.py:43
  57.9 2.0 %collective-permute-start.24 = (bf16[256,1152]{1,0:T(8,128)(2,1)S(1)}, bf16[256,1152]{1,0:T(8,128)(2,1)S(1)}, u32[]{:S(2)}, u32[]{:S(2)}) collective-permute-start(bf16[256,1152]{1,0:T(8,128)(2,1)S(1)} %get-tuple-element.42), channel_id=1, source_target_pairs={{0,4},{1,5},{2,6},{3,7},{4,16},{5,17},{6,18},{7,19},{16,20},{17,21... | collective-permute-start | bytes 1769480 | tf_op jit(solution)/shard_map/ppermute | solution.py:34
  61.2 3.6 %collective-permute-start.16 = (bf16[64,1152]{1,0:T(8,128)(2,1)S(1)}, bf16[64,1152]{1,0:T(8,128)(2,1)S(1)}, u32[]{:S(2)}, u32[]{:S(2)}) collective-permute-start(bf16[64,1152]{1,0:T(8,128)(2,1)S(1)} %get-tuple-element.32), channel_id=1, source_target_pairs={{0,224},{32,0},{64,32},{96,64},{128,96},{160,128},{192,160},{224,1... | collective-permute-start | bytes 442376 | tf_op jit(solution)/shard_map/ppermute | solution.py:22
  65.7 1.8 %collective-permute-done.16.b_ref = bf16[64,1152]{1,0:T(8,128)(2,1)S(1)} collective-permute-done((bf16[64,1152]{1,0:T(8,128)(2,1)S(1)}, bf16[64,1152]{1,0:T(8,128)(2,1)S(1)}, u32[]{:S(2)}, u32[]{:S(2)}) %collective-permute-start.16) | collective-permute-done | bytes 147488 | tf_op jit(solution)/shard_map/ppermute | solution.py:22
  67.5 4.0 %collective-permute-start.17 = (bf16[64,1152]{1,0:T(8,128)(2,1)S(1)}, bf16[64,1152]{1,0:T(8,128)(2,1)S(1)}, u32[]{:S(2)}, u32[]{:S(2)}) collective-permute-start(bf16[64,1152]{1,0:T(8,128)(2,1)S(1)} %shard_map.67), channel_id=1, source_target_pairs={{0,224},{32,0},{64,32},{96,64},{128,96},{160,128},{192,160},{224,1... | collective-permute-start | bytes 442376 | tf_op jit(solution)/shard_map/ppermute | solution.py:22
  71.6 2.1 %collective-permute-done.24.refs_2_ = bf16[256,1152]{1,0:T(8,128)(2,1)S(1)} collective-permute-done((bf16[256,1152]{1,0:T(8,128)(2,1)S(1)}, bf16[256,1152]{1,0:T(8,128)(2,1)S(1)}, u32[]{:S(2)}, u32[]{:S(2)}) %collective-permute-start.24) | collective-permute-done | bytes 589856 | tf_op jit(solution)/shard_map/ppermute | solution.py:34
  75.3 2.0 %collective-permute-start.27 = (bf16[64,1152]{1,0:T(8,128)(2,1)S(1)}, bf16[64,1152]{1,0:T(8,128)(2,1)S(1)}, u32[]{:S(2)}, u32[]{:S(2)}) collective-permute-start(bf16[64,1152]{1,0:T(8,128)(2,1)S(1)} %get-tuple-element.46), channel_id=1, source_target_pairs={{0,1},{1,2},{2,3},{3,0},{4,5},{5,6},{6,7},{7,4},{16,17},{17,18},{1... | collective-permute-start | bytes 442376 | tf_op jit(solution)/shard_map/ppermute | solution.py:34
  78.0 3.0 %collective-permute-start.18 = (bf16[64,1152]{1,0:T(8,128)(2,1)S(1)}, bf16[64,1152]{1,0:T(8,128)(2,1)S(1)}, u32[]{:S(2)}, u32[]{:S(2)}) collective-permute-start(bf16[64,1152]{1,0:T(8,128)(2,1)S(1)} %shard_map.68), channel_id=1, source_target_pairs={{0,224},{32,0},{64,32},{96,64},{128,96},{160,128},{192,160},{224,1... | collective-permute-start | bytes 442376 | tf_op jit(solution)/shard_map/ppermute | solution.py:22
  81.8 2.2 %collective-permute-done.28.refs_3_ = bf16[64,1152]{1,0:T(8,128)(2,1)S(1)} collective-permute-done((bf16[64,1152]{1,0:T(8,128)(2,1)S(1)}, bf16[64,1152]{1,0:T(8,128)(2,1)S(1)}, u32[]{:S(2)}, u32[]{:S(2)}) %collective-permute-start.28) | collective-permute-done | bytes 147488 | tf_op jit(solution)/shard_map/ppermute | solution.py:34
  84.9 6.3 %collective-permute-done.22.refs_3_ = bf16[64,1152]{1,0:T(8,128)(2,1)S(1)} collective-permute-done((bf16[64,1152]{1,0:T(8,128)(2,1)S(1)}, bf16[64,1152]{1,0:T(8,128)(2,1)S(1)}, u32[]{:S(2)}, u32[]{:S(2)}) %collective-permute-start.22) | collective-permute-done | bytes 147488 | tf_op jit(solution)/shard_map/ppermute | solution.py:22
  (59 shorter events, 10.6 us)
Async XLA Ops:
  2.7 9.0 %collective-permute-start.7 = (bf16[64,1152]{1,0:T(8,128)(2,1)S(1)}, bf16[64,1152]{1,0:T(8,128)(2,1)S(1)}, u32[]{:S(2)}, u32[]{:S(2)}) collective-permute-start(bf16[64,1152]{1,0:T(8,128)(2,1)S(1)} %get-tuple-element.26.refs_0_), channel_id=1, source_target_pairs={{0,224},{32,0},{64,32},{96,64},{128,96},{160,128},{192,160},{224,1... | collective-permute-start | bytes 442376 | tf_op jit(solution)/shard_map/ppermute | solution.py:22
  8.6 6.8 %collective-permute-start.6 = (bf16[64,1152]{1,0:T(8,128)(2,1)S(1)}, bf16[64,1152]{1,0:T(8,128)(2,1)S(1)}, u32[]{:S(2)}, u32[]{:S(2)}) collective-permute-start(bf16[64,1152]{1,0:T(8,128)(2,1)S(1)} %get-tuple-element.26.refs_0_), channel_id=1, source_target_pairs={{0,32},{32,64},{64,96},{96,128},{128,160},{160,192},{192,224},{224... | collective-permute-start | bytes 442376 | tf_op jit(solution)/shard_map/ppermute | solution.py:22
  8.6 9.6 %collective-permute-start.2 = (bf16[64,1152]{1,0:T(8,128)(2,1)S(1)}, bf16[64,1152]{1,0:T(8,128)(2,1)S(1)}, u32[]{:S(2)}, u32[]{:S(2)}) collective-permute-start(bf16[64,1152]{1,0:T(8,128)(2,1)S(1)} %get-tuple-element.25.refs_0_), channel_id=1, source_target_pairs={{0,2},{1,3},{2,0},{3,1},{4,6},{5,7},{6,4},{7,5},{16,18},{17,19},{1... | collective-permute-start | bytes 442376 | tf_op jit(solution)/shard_map/ppermute | solution.py:34
  11.7 8.6 %collective-permute-start.10 = (bf16[64,1152]{1,0:T(8,128)(2,1)S(1)}, bf16[64,1152]{1,0:T(8,128)(2,1)S(1)}, u32[]{:S(2)}, u32[]{:S(2)}) collective-permute-start(bf16[64,1152]{1,0:T(8,128)(2,1)S(1)} %collective-permute-done.7.refs_2_), channel_id=1, source_target_pairs={{0,224},{32,0},{64,32},{96,64},{128,96},{160,128},{192,160},{224,1... | collective-permute-start | bytes 442376 | tf_op jit(solution)/shard_map/ppermute | solution.py:22
  15.4 11.7 %collective-permute-start.9 = (bf16[64,1152]{1,0:T(8,128)(2,1)S(1)}, bf16[64,1152]{1,0:T(8,128)(2,1)S(1)}, u32[]{:S(2)}, u32[]{:S(2)}) collective-permute-start(bf16[64,1152]{1,0:T(8,128)(2,1)S(1)} %collective-permute-done.6.refs_1_), channel_id=1, source_target_pairs={{0,32},{32,64},{64,96},{96,128},{128,160},{160,192},{192,224},{224... | collective-permute-start | bytes 442376 | tf_op jit(solution)/shard_map/ppermute | solution.py:22
  15.4 11.7 %collective-permute-start.1 = (bf16[64,1152]{1,0:T(8,128)(2,1)S(1)}, bf16[64,1152]{1,0:T(8,128)(2,1)S(1)}, u32[]{:S(2)}, u32[]{:S(2)}) collective-permute-start(bf16[64,1152]{1,0:T(8,128)(2,1)S(1)} %get-tuple-element.25.refs_0_), channel_id=1, source_target_pairs={{0,3},{1,0},{2,1},{3,2},{4,7},{5,4},{6,5},{7,6},{16,19},{17,16},{1... | collective-permute-start | bytes 442376 | tf_op jit(solution)/shard_map/ppermute | solution.py:34
  18.2 13.0 %collective-permute-start = (bf16[64,1152]{1,0:T(8,128)(2,1)S(1)}, bf16[64,1152]{1,0:T(8,128)(2,1)S(1)}, u32[]{:S(2)}, u32[]{:S(2)}) collective-permute-start(bf16[64,1152]{1,0:T(8,128)(2,1)S(1)} %get-tuple-element.25.refs_0_), channel_id=1, source_target_pairs={{0,1},{1,2},{2,3},{3,0},{4,5},{5,6},{6,7},{7,4},{16,17},{17,18},{1... | collective-permute-start | bytes 442376 | tf_op jit(solution)/shard_map/ppermute | solution.py:34
  18.2 16.8 %collective-permute-start.8 = (bf16[64,1152]{1,0:T(8,128)(2,1)S(1)}, bf16[64,1152]{1,0:T(8,128)(2,1)S(1)}, u32[]{:S(2)}, u32[]{:S(2)}) collective-permute-start(bf16[64,1152]{1,0:T(8,128)(2,1)S(1)} %get-tuple-element.26.refs_0_), channel_id=1, source_target_pairs={{0,128},{32,160},{64,192},{96,224},{128,0},{160,32},{192,64},{224,... | collective-permute-start | bytes 442376 | tf_op jit(solution)/shard_map/ppermute | solution.py:22
  20.3 14.7 %collective-permute-start.12 = (bf16[64,1152]{1,0:T(8,128)(2,1)S(1)}, bf16[64,1152]{1,0:T(8,128)(2,1)S(1)}, u32[]{:S(2)}, u32[]{:S(2)}) collective-permute-start(bf16[64,1152]{1,0:T(8,128)(2,1)S(1)} %collective-permute-done.10.refs_1_), channel_id=1, source_target_pairs={{0,224},{32,0},{64,32},{96,64},{128,96},{160,128},{192,160},{224,1... | collective-permute-start | bytes 442376 | tf_op jit(solution)/shard_map/ppermute | solution.py:22
  27.1 8.0 %collective-permute-start.11 = (bf16[64,1152]{1,0:T(8,128)(2,1)S(1)}, bf16[64,1152]{1,0:T(8,128)(2,1)S(1)}, u32[]{:S(2)}, u32[]{:S(2)}) collective-permute-start(bf16[64,1152]{1,0:T(8,128)(2,1)S(1)} %collective-permute-done.9.refs_0_), channel_id=1, source_target_pairs={{0,32},{32,64},{64,96},{96,128},{128,160},{160,192},{192,224},{224... | collective-permute-start | bytes 442376 | tf_op jit(solution)/shard_map/ppermute | solution.py:22
  31.2 11.6 %collective-permute-start.5 = (bf16[256,1152]{1,0:T(8,128)(2,1)S(1)}, bf16[256,1152]{1,0:T(8,128)(2,1)S(1)}, u32[]{:S(2)}, u32[]{:S(2)}) collective-permute-start(bf16[256,1152]{1,0:T(8,128)(2,1)S(1)} %shard_map.60.refs_0_), channel_id=1, source_target_pairs={{0,16},{1,17},{2,18},{3,19},{4,20},{5,21},{6,22},{7,23},{16,0},{17... | collective-permute-start | bytes 1769480 | tf_op jit(solution)/shard_map/ppermute | solution.py:34
  31.3 16.3 %collective-permute-start.4 = (bf16[256,1152]{1,0:T(8,128)(2,1)S(1)}, bf16[256,1152]{1,0:T(8,128)(2,1)S(1)}, u32[]{:S(2)}, u32[]{:S(2)}) collective-permute-start(bf16[256,1152]{1,0:T(8,128)(2,1)S(1)} %shard_map.60.refs_0_), channel_id=1, source_target_pairs={{0,20},{1,21},{2,22},{3,23},{4,0},{5,1},{6,2},{7,3},{16,4},{17,5},... | collective-permute-start | bytes 1769480 | tf_op jit(solution)/shard_map/ppermute | solution.py:34
  35.0 14.2 %collective-permute-start.3 = (bf16[256,1152]{1,0:T(8,128)(2,1)S(1)}, bf16[256,1152]{1,0:T(8,128)(2,1)S(1)}, u32[]{:S(2)}, u32[]{:S(2)}) collective-permute-start(bf16[256,1152]{1,0:T(8,128)(2,1)S(1)} %shard_map.60.refs_0_), channel_id=1, source_target_pairs={{0,4},{1,5},{2,6},{3,7},{4,16},{5,17},{6,18},{7,19},{16,20},{17,21... | collective-permute-start | bytes 1769480 | tf_op jit(solution)/shard_map/ppermute | solution.py:34
  35.0 14.3 %collective-permute-start.13 = (bf16[256,1152]{1,0:T(8,128)(2,1)S(1)}, bf16[256,1152]{1,0:T(8,128)(2,1)S(1)}, u32[]{:S(2)}, u32[]{:S(2)}) collective-permute-start(bf16[256,1152]{1,0:T(8,128)(2,1)S(1)} %shard_map.62.refs_0_), channel_id=1, source_target_pairs={{0,8},{8,0},{1,9},{9,1},{2,10},{10,2},{3,11},{11,3},{4,12},{12,4},... | collective-permute-start | bytes 1769480 | tf_op jit(solution)/shard_map/ppermute | solution.py:22
  35.2 14.2 %collective-permute-start.14 = (bf16[256,1152]{1,0:T(8,128)(2,1)S(1)}, bf16[256,1152]{1,0:T(8,128)(2,1)S(1)}, u32[]{:S(2)}, u32[]{:S(2)}) collective-permute-start(bf16[256,1152]{1,0:T(8,128)(2,1)S(1)} %shard_map.63.refs_1_), channel_id=1, source_target_pairs={{0,8},{8,0},{1,9},{9,1},{2,10},{10,2},{3,11},{11,3},{4,12},{12,4},... | collective-permute-start | bytes 1769480 | tf_op jit(solution)/shard_map/ppermute | solution.py:22
  52.4 8.6 %collective-permute-start.15 = (bf16[512,1152]{1,0:T(8,128)(2,1)S(1)}, bf16[512,1152]{1,0:T(8,128)(2,1)S(1)}, u32[]{:S(2)}, u32[]{:S(2)}) collective-permute-start(bf16[512,1152]{1,0:T(8,128)(2,1)S(1)} %get-tuple-element.28), channel_id=1, source_target_pairs={{0,8},{8,0},{1,9},{9,1},{2,10},{10,2},{3,11},{11,3},{4,12},{12,4},... | collective-permute-start | bytes 3538952 | tf_op jit(solution)/shard_map/ppermute | solution.py:22
  57.8 13.8 %collective-permute-start.23 = (bf16[256,1152]{1,0:T(8,128)(2,1)S(1)}, bf16[256,1152]{1,0:T(8,128)(2,1)S(1)}, u32[]{:S(2)}, u32[]{:S(2)}) collective-permute-start(bf16[256,1152]{1,0:T(8,128)(2,1)S(1)} %get-tuple-element.41), channel_id=1, source_target_pairs={{0,20},{1,21},{2,22},{3,23},{4,0},{5,1},{6,2},{7,3},{16,4},{17,5},... | collective-permute-start | bytes 1769480 | tf_op jit(solution)/shard_map/ppermute | solution.py:34
  57.9 15.8 %collective-permute-start.24 = (bf16[256,1152]{1,0:T(8,128)(2,1)S(1)}, bf16[256,1152]{1,0:T(8,128)(2,1)S(1)}, u32[]{:S(2)}, u32[]{:S(2)}) collective-permute-start(bf16[256,1152]{1,0:T(8,128)(2,1)S(1)} %get-tuple-element.42), channel_id=1, source_target_pairs={{0,4},{1,5},{2,6},{3,7},{4,16},{5,17},{6,18},{7,19},{16,20},{17,21... | collective-permute-start | bytes 1769480 | tf_op jit(solution)/shard_map/ppermute | solution.py:34
  59.9 15.0 %collective-permute-start.25 = (bf16[256,1152]{1,0:T(8,128)(2,1)S(1)}, bf16[256,1152]{1,0:T(8,128)(2,1)S(1)}, u32[]{:S(2)}, u32[]{:S(2)}) collective-permute-start(bf16[256,1152]{1,0:T(8,128)(2,1)S(1)} %get-tuple-element.43), channel_id=1, source_target_pairs={{0,16},{1,17},{2,18},{3,19},{4,20},{5,21},{6,22},{7,23},{16,0},{17... | collective-permute-start | bytes 1769480 | tf_op jit(solution)/shard_map/ppermute | solution.py:34
  64.8 6.7 %collective-permute-start.19 = (bf16[64,1152]{1,0:T(8,128)(2,1)S(1)}, bf16[64,1152]{1,0:T(8,128)(2,1)S(1)}, u32[]{:S(2)}, u32[]{:S(2)}) collective-permute-start(bf16[64,1152]{1,0:T(8,128)(2,1)S(1)} %get-tuple-element.35), channel_id=1, source_target_pairs={{0,32},{32,64},{64,96},{96,128},{128,160},{160,192},{192,224},{224... | collective-permute-start | bytes 442376 | tf_op jit(solution)/shard_map/ppermute | solution.py:22
  67.5 9.8 %collective-permute-start.17 = (bf16[64,1152]{1,0:T(8,128)(2,1)S(1)}, bf16[64,1152]{1,0:T(8,128)(2,1)S(1)}, u32[]{:S(2)}, u32[]{:S(2)}) collective-permute-start(bf16[64,1152]{1,0:T(8,128)(2,1)S(1)} %shard_map.67), channel_id=1, source_target_pairs={{0,224},{32,0},{64,32},{96,64},{128,96},{160,128},{192,160},{224,1... | collective-permute-start | bytes 442376 | tf_op jit(solution)/shard_map/ppermute | solution.py:22
  77.3 13.8 %collective-permute-start.22 = (bf16[64,1152]{1,0:T(8,128)(2,1)S(1)}, bf16[64,1152]{1,0:T(8,128)(2,1)S(1)}, u32[]{:S(2)}, u32[]{:S(2)}) collective-permute-start(bf16[64,1152]{1,0:T(8,128)(2,1)S(1)} %get-tuple-element.36), channel_id=1, source_target_pairs={{0,128},{32,160},{64,192},{96,224},{128,0},{160,32},{192,64},{224,... | collective-permute-start | bytes 442376 | tf_op jit(solution)/shard_map/ppermute | solution.py:22
  78.0 13.2 %collective-permute-start.18 = (bf16[64,1152]{1,0:T(8,128)(2,1)S(1)}, bf16[64,1152]{1,0:T(8,128)(2,1)S(1)}, u32[]{:S(2)}, u32[]{:S(2)}) collective-permute-start(bf16[64,1152]{1,0:T(8,128)(2,1)S(1)} %shard_map.68), channel_id=1, source_target_pairs={{0,224},{32,0},{64,32},{96,64},{128,96},{160,128},{192,160},{224,1... | collective-permute-start | bytes 442376 | tf_op jit(solution)/shard_map/ppermute | solution.py:22
  81.1 10.1 %collective-permute-start.21 = (bf16[64,1152]{1,0:T(8,128)(2,1)S(1)}, bf16[64,1152]{1,0:T(8,128)(2,1)S(1)}, u32[]{:S(2)}, u32[]{:S(2)}) collective-permute-start(bf16[64,1152]{1,0:T(8,128)(2,1)S(1)} %shard_map.70), channel_id=1, source_target_pairs={{0,32},{32,64},{64,96},{96,128},{128,160},{160,192},{192,224},{224... | collective-permute-start | bytes 442376 | tf_op jit(solution)/shard_map/ppermute | solution.py:22
  (9 other events, 62.0 us)

commit v6 on v5

v6 whole, which is shorter than its diff:
```python
import functools

import jax
import jax.numpy as jnp
from jax import lax
from jax.experimental import pallas as pl
from jax.experimental.pallas import tpu as pltpu
from jax.sharding import Mesh, PartitionSpec as P

AXES = ("z", "yh", "c", "yl", "x")
PLANE = ("yh", "c", "yl", "x")
SIDE = 4
BF16 = jnp.bfloat16
F32 = jnp.float32
VMEM = pl.BlockSpec(memory_space=pltpu.VMEM)
HBM = pl.BlockSpec(memory_space=pltpu.HBM)
SMEM = pl.BlockSpec(memory_space=pltpu.SMEM)
TILE = 256


def shifted(value, axis, by):
    length = lax.axis_size(axis)
    return lax.ppermute(value, axis, [(i, (i + by) % length) for i in range(length)])


def crossed(value, first, by):
    at = lambda y, c, x: ((y // 2 * 2 + c) * 2 + y % 2) * SIDE + x
    pairs = []
    for c in range(2):
        along_x = (c == 0) == first
        for y in range(SIDE):
            for x in range(SIDE):
                to = (y, c, (x + by) % SIDE) if along_x else ((y + by) % SIDE, c, x)
                pairs.append((at(y, c, x), at(*to)))
    return lax.ppermute(value, PLANE, pairs)


def fanned(value, by):
    length = lax.axis_size("z")
    pairs = [
        (z * 2 + c, (z + (by if c == 0 else -by)) % length * 2 + c)
        for z in range(length)
        for c in range(2)
    ]
    return lax.ppermute(value, ("z", "c"), pairs)


def shaped(shape, dtype):
    return jax.ShapeDtypeStruct(shape, dtype)


def local(kernel, outs, *args, scalars=0, out_specs=None, flops=0, scratch=(), place=VMEM):
    many = isinstance(outs, list)
    if place is HBM:
        args = [pltpu.with_memory_space_constraint(arg, pltpu.HBM) for arg in args]
    return pl.pallas_call(
        kernel,
        out_shape=outs,
        in_specs=[SMEM] * scalars + [place] * (len(args) - scalars),
        out_specs=out_specs or ([VMEM] * len(outs) if many else VMEM),
        scratch_shapes=list(scratch),
        compiler_params=pltpu.CompilerParams(vmem_limit_bytes=16 * 2**20),
        cost_estimate=pl.CostEstimate(
            flops=flops,
            bytes_accessed=sum(a.size * a.dtype.itemsize for a in args),
            transcendentals=0,
        ),
    )(*args)


def matmul(a, b, contract):
    return lax.dot_general(a, b, (contract, ((), ())), preferred_element_type=F32)


def inverse(raw):
    return lax.rsqrt(jnp.sum(raw * raw, axis=1, keepdims=True) + 1e-06)


def normalize_kernel(img_in, txt_in, img_out, txt_out, raw, sems):
    reads = [pltpu.make_async_copy(a, raw.at[i], sems.at[i]) for i, a in enumerate((txt_in, img_in))]
    for read in reads:
        read.start()
    for i, out in enumerate((txt_out, img_out)):
        reads[i].wait()
        out[...] = (raw[i] * inverse(raw[i])).astype(BF16)


def join_kernel(*refs):
    *blocks, out_ref = refs
    at = 0
    for block in blocks:
        out_ref[pl.ds(at, block.shape[0]), :] = block[...]
        at += block.shape[0]


def weights_of(images, texts, scale, bias, paired):
    logits = scale * matmul(images, texts, ((1,), (1,))) + bias
    if not paired:
        return (1.0 / (1.0 + jnp.exp(-logits))).astype(BF16)
    img_at = lax.broadcasted_iota(jnp.int32, logits.shape, 0)
    txt_at = lax.broadcasted_iota(jnp.int32, logits.shape, 1)
    sign = jnp.where((img_at == txt_at) & (img_at < paired), 1.0, -1.0).astype(F32)
    return (-sign / (1.0 + jnp.exp(sign * logits))).astype(BF16)


def image_kernel(paired, pieces, groups, scale_ref, bias_ref, *refs):
    texts, images = (refs[:pieces], refs[pieces : pieces + groups])
    before = refs[pieces + groups : -2 * groups]
    weights_out, grads_out = (refs[-2 * groups : -groups], refs[-groups:])
    scale = scale_ref[0]
    for i in range(groups):
        total = None
        for j, text in enumerate(texts):
            pair = 0 if i or j else paired
            weights = weights_of(images[i][...], text[...], scale, bias_ref[0], pair)
            weights_out[i][:, pl.ds(j * TILE, TILE)] = weights
            part = matmul(weights, text[...], ((1,), (0,)))
            total = part if total is None else total + part
        total = scale * total
        if before:
            total += before[i][...]
        grads_out[i][...] = total.astype(grads_out[i].dtype)


def text_kernel(places, scale_ref, *refs):
    images, weights, outs = (refs[:4], refs[4 : -len(places)], refs[-len(places) :])
    for place, out in zip(places, outs):
        total = None
        for image, (array, at) in zip(images, place):
            w = weights[array][:, pl.ds(at * TILE, TILE)]
            part = matmul(w, image[...], ((0,), (0,)))
            total = part if total is None else total + part
        out[...] = (scale_ref[0] * total).astype(out.dtype)


def split_kernel(count, *refs):
    arrays, outs = (refs[:count], refs[count:])
    at = 0
    for out in outs:
        tile = pl.ds(at, out.shape[0])
        total = arrays[0][tile, :].astype(F32)
        for array in arrays[1:]:
            total += array[tile, :].astype(F32)
        out[...] = total.astype(out.dtype)
        at += out.shape[0]


def add_kernel(a_ref, b_ref, out_ref):
    out_ref[...] = (a_ref[...].astype(F32) + b_ref[...].astype(F32)).astype(BF16)


def ring_add_kernel(own_ref, sib_ref, far_ref, out_ref):
    rows = own_ref.shape[0]
    total = own_ref[...].astype(F32) + far_ref[...].astype(F32)
    out_ref[pl.ds(0, rows), :] = total.astype(BF16)
    out_ref[pl.ds(rows, rows), :] = sib_ref[...]


def end_kernel(raw_ref, *refs):
    *parts, out_ref = refs
    raw, grad = (raw_ref[...], parts[0][...].astype(F32))
    for part in parts[1:]:
        grad += part[...].astype(F32)
    inv = inverse(raw)
    across = jnp.sum(raw * grad, axis=1, keepdims=True)
    out_ref[...] = inv * grad - raw * (inv * inv * inv) * across


def added(a, b):
    return local(add_kernel, shaped(a.shape, BF16), a, b)


def body(images, texts, scale, bias):
    rows, width = images.shape
    line, half = (SIDE * rows, 8 * rows)
    block = shaped((rows, width), BF16)
    join = lambda *parts: local(
        join_kernel, shaped((sum(part.shape[0] for part in parts), width), BF16), *parts
    )
    img, txt = local(
        normalize_kernel,
        [block, block],
        images, texts,
        place=HBM,
        scratch=[pltpu.VMEM((2, rows, width), F32), pltpu.SemaphoreType.DMA((2,))],
    )

    def image_part(paired, pieces, groups, before, kinds):
        size = groups[0].shape[0]
        outs = [shaped((size, len(pieces) * line), BF16) for _ in groups]
        results = local(
            functools.partial(image_kernel, paired, len(pieces), len(groups)),
            outs + [shaped((size, width), kind) for kind in kinds],
            scale, bias, *pieces, *groups, *before,
            scalars=2, flops=4 * size * len(groups) * line * len(pieces) * width,
        )
        return results[: len(groups)], results[len(groups) :]

    ahead, behind, across = [crossed(txt, True, by) for by in (1, -1, 2)]
    texts0 = join(txt, ahead, behind, across)
    sib = shifted(img, "c", 1)
    keep_1 = join(img, sib)
    z1 = fanned(keep_1, 1)
    texts0, z1 = lax.optimization_barrier((texts0, z1))
    texts1, texts2, texts3 = [crossed(texts0, False, by) for by in (1, -1, 2)]
    others = (texts3, texts1, texts2)
    z1_sib = shifted(z1, "c", 1)
    z2 = fanned(z1, 1)
    z2, z1_sib = lax.optimization_barrier((z2, z1_sib))
    keep_a, send_a = (join(img, z1), join(sib, z1_sib))
    w_a0, d_a0 = image_part(rows, (texts0,), (keep_a, send_a), (), (F32, F32))
    z3 = fanned(z2, 1)
    z3, *d_a0 = lax.optimization_barrier((z3, *d_a0))
    far = fanned(z3[:rows], 1)
    w_a, (dk_a, ds_a) = image_part(0, others, (keep_a, send_a), d_a0, (F32, BF16))
    far, ds_a = lax.optimization_barrier((far, ds_a))
    keep_b = join(z2, z3, far)
    send_b = shifted(keep_b, "c", 1)

    w_sb, (ds_b,) = image_part(0, (texts0, *others), (send_b,), (), (BF16,))
    back_b, back_a = (shifted(ds_b, "c", 1), shifted(ds_a, "c", 1))
    w_kb, (dk_b,) = image_part(0, (texts0, *others), (keep_b,), (), (F32,))

    def text_part(places, kind):
        return local(
            functools.partial(text_kernel, places),
            [shaped((line, width), kind) for _ in places],
            scale, keep_a, send_a, send_b, keep_b, *w_a0, *w_a, *w_sb, *w_kb,
            scalars=1, flops=2 * len(places) * line * 16 * rows * width,
        )

    d_texts3, d_texts1, d_texts2 = text_part(
        [[(2, i), (3, i), (4, i + 1), (5, i + 1)] for i in range(3)], BF16
    )
    d_texts0 = text_part([[(0, 0), (1, 0), (4, 0), (5, 0)]], F32)[0]

    z2_sum, z3_own, z3_sib, far_sum = local(
        functools.partial(split_kernel, 2),
        [shaped((2 * rows, width), BF16), block, block, block],
        dk_b, back_b,
    )
    own, z1_sum = local(
        functools.partial(split_kernel, 2),
        [shaped((rows, width), F32), shaped((2 * rows, width), BF16)],
        dk_a, back_a,
    )
    far_back = fanned(far_sum, -1)
    far_back, d_texts3, d_texts1, d_texts2 = lax.optimization_barrier((far_back, d_texts3, d_texts1, d_texts2))
    back3, back1, back2 = (
        crossed(d_texts3, False, 2),
        crossed(d_texts1, False, -1),
        crossed(d_texts2, False, 1),
    )
    kinds = [F32] + [BF16] * 3
    returned = local(
        ring_add_kernel, shaped((2 * rows, width), BF16), z3_own, z3_sib, far_back
    )
    returned = fanned(returned, -1)
    returned = fanned(added(z2_sum, returned), -1)
    returned = fanned(added(z1_sum, returned), -1)
    other = shifted(returned[rows:], "c", 1)
    txt_own, d_ahead, d_behind, d_across = local(
        functools.partial(split_kernel, 4),
        [shaped((rows, width), kind) for kind in kinds],
        d_texts0, back1, back2, back3,
    )
    d_ahead, d_behind, d_across = (
        crossed(d_ahead, True, -1),
        crossed(d_behind, True, 1),
        crossed(d_across, True, 2),
    )

    whole = pl.BlockSpec((rows, width), lambda: (0, 0))
    end = lambda raw, *parts: local(
        end_kernel, shaped((rows, width), F32), raw, *parts, out_specs=whole
    )
    return (end(images, own, returned[:rows], other), end(texts, txt_own, d_ahead, d_behind, d_across))


def solution(mesh):
    fine = Mesh(mesh.devices.reshape(8, 2, 2, 2, 4), AXES)
    rows = P(AXES, None)
    return jax.shard_map(
        body,
        mesh=fine,
        in_specs=(rows, rows, P(), P()),
        out_specs=(rows, rows),
        check_vma=False,
    )
```

time: 93.5 us -> 87.4 us (0.935)
  the two profiles are of different devices: /device:TPU:8 before, /device:TPU:6 now
where the time goes in v6:
time: 87.4 us; the launch traced here: 87.3 us
  starting transfers between devices  35 us (40%)
  waiting for transfers between devices  32.4 us (37%)
  Pallas kernels  17.8 us (20%)
  between operations  2.13 us (2%)
    pallas_call x20, Pallas kernels, local(): pl.pallas_call(kernel, out_shape=outs, in_specs=[SMEM] * scalars + [place...  17.8 us
    ppermute x8, waiting for transfers between devices, fanned(): return lax.ppermute(value, ('z', 'c'), pairs)  16.2 us
    ppermute x8, starting transfers between devices, fanned(): return lax.ppermute(value, ('z', 'c'), pairs)  15.4 us
    ppermute x12, starting transfers between devices, crossed(): return lax.ppermute(value, PLANE, pairs)  14.7 us
    ppermute x12, waiting for transfers between devices, crossed(): return lax.ppermute(value, PLANE, pairs)  12.6 us
    ppermute x6, starting transfers between devices, shifted(): lax.ppermute(value, axis, [(i, (i + by) % length) for i in range(length)])  4.88 us
    ppermute x6, waiting for transfers between devices, shifted(): lax.ppermute(value, axis, [(i, (i + by) % length) for i in range(length)])  3.57 us
  transfers between devices with their start and end apart: 26, of which 15 were waited for; matrix products, arithmetic and copies ran while one was open for 0% of the time, Pallas kernels for 15%

profile of v6, /device:TPU:6, one launch (start us, length us, event | category | flops | bytes accessed | tf_op | source)
XLA Modules:
  0.0 87.3 jit_solution(6194215628313710048)
XLA Ops:
  3.3 2.0 %collective-permute-start.4 = (bf16[128,1152]{1,0:T(8,128)(2,1)S(1)}, bf16[128,1152]{1,0:T(8,128)(2,1)S(1)}, u32[]{:S(2)}, u32[]{:S(2)}) collective-permute-start(bf16[128,1152]{1,0:T(8,128)(2,1)S(1)} %shard_map.61), channel_id=1, source_target_pairs={{0,32},{8,232},{32,64},{40,8},{64,96},{72,40},{96,128},{104,72},{1... | collective-permute-start | bytes 884744 | tf_op jit(solution)/shard_map/ppermute | solution.py:45
  5.3 1.4 %collective-permute-start.2 = (bf16[64,1152]{1,0:T(8,128)(2,1)S(1)}, bf16[64,1152]{1,0:T(8,128)(2,1)S(1)}, u32[]{:S(2)}, u32[]{:S(2)}) collective-permute-start(bf16[64,1152]{1,0:T(8,128)(2,1)S(1)} %get-tuple-element.42.refs_0_), channel_id=1, source_target_pairs={{0,2},{1,3},{2,0},{3,1},{4,6},{5,7},{6,4},{7,5},{16,18},{17,19},{1... | collective-permute-start | bytes 442376 | tf_op jit(solution)/shard_map/ppermute | solution.py:35
  6.7 3.2 %collective-permute-start = (bf16[64,1152]{1,0:T(8,128)(2,1)S(1)}, bf16[64,1152]{1,0:T(8,128)(2,1)S(1)}, u32[]{:S(2)}, u32[]{:S(2)}) collective-permute-start(bf16[64,1152]{1,0:T(8,128)(2,1)S(1)} %get-tuple-element.42.refs_0_), channel_id=1, source_target_pairs={{0,1},{1,2},{2,3},{3,0},{4,5},{5,6},{6,7},{7,4},{16,17},{17,18},{1... | collective-permute-start | bytes 442376 | tf_op jit(solution)/shard_map/ppermute | solution.py:35
  10.0 2.1 %collective-permute-done.2.refs_3_ = bf16[64,1152]{1,0:T(8,128)(2,1)S(1)} collective-permute-done((bf16[64,1152]{1,0:T(8,128)(2,1)S(1)}, bf16[64,1152]{1,0:T(8,128)(2,1)S(1)}, u32[]{:S(2)}, u32[]{:S(2)}) %collective-permute-start.2) | collective-permute-done | bytes 147488 | tf_op jit(solution)/shard_map/ppermute | solution.py:35
  12.0 1.5 %collective-permute-done.1.refs_2_ = bf16[64,1152]{1,0:T(8,128)(2,1)S(1)} collective-permute-done((bf16[64,1152]{1,0:T(8,128)(2,1)S(1)}, bf16[64,1152]{1,0:T(8,128)(2,1)S(1)}, u32[]{:S(2)}, u32[]{:S(2)}) %collective-permute-start.1) | collective-permute-done | bytes 147488 | tf_op jit(solution)/shard_map/ppermute | solution.py:35
  14.0 4.2 %collective-permute-start.9 = (bf16[128,1152]{1,0:T(8,128)(2,1)S(1)}, bf16[128,1152]{1,0:T(8,128)(2,1)S(1)}, u32[]{:S(2)}, u32[]{:S(2)}) collective-permute-start(bf16[128,1152]{1,0:T(8,128)(2,1)S(1)} %collective-permute-done.4.refs_1_), channel_id=1, source_target_pairs={{0,8},{8,0},{1,9},{9,1},{2,10},{10,2},{3,11},{11,3},{4,12},{12,4},... | collective-permute-start | bytes 884744 | tf_op jit(solution)/shard_map/ppermute | solution.py:23
  21.6 4.5 %collective-permute-done.8.refs_0_ = bf16[128,1152]{1,0:T(8,128)(2,1)S(1)} collective-permute-done((bf16[128,1152]{1,0:T(8,128)(2,1)S(1)}, bf16[128,1152]{1,0:T(8,128)(2,1)S(1)}, u32[]{:S(2)}, u32[]{:S(2)}) %collective-permute-start.8) | collective-permute-done | bytes 294944 | tf_op jit(solution)/shard_map/ppermute | solution.py:45
  27.5 1.5 %shard_map.64 = (bf16[192,256]{1,0:T(8,128)(2,1)S(1)}, bf16[192,256]{1,0:T(8,128)(2,1)S(1)}, f32[192,1152]{1,0:T(8,128)S(1)}, f32[192,1152]{1,0:T(8,128)S(1)}) custom-call(f32[1]{0:T(128)S(6)} %copy.6.scale_ref, f32[1]{0:T(128)S(6)} %copy.7.bias_ref, bf16[256,1152]{1,0:T(8,128)(2,1)S(1)} %shard_map.60.refs_0_, ...), custom_call_target="tpu_custom_call" | custom-call | flops 452984832 | bytes 1474568 | tf_op jit(solution)/shard_map/pallas_call | solution.py:56
  29.0 5.0 %collective-permute-done.10.refs_1_ = bf16[128,1152]{1,0:T(8,128)(2,1)S(1)} collective-permute-done((bf16[128,1152]{1,0:T(8,128)(2,1)S(1)}, bf16[128,1152]{1,0:T(8,128)(2,1)S(1)}, u32[]{:S(2)}, u32[]{:S(2)}) %collective-permute-start.10) | collective-permute-done | bytes 294944 | tf_op jit(solution)/shard_map/ppermute | solution.py:45
  34.2 2.6 %collective-permute-done.6.refs_1_.refs_2_ = bf16[256,1152]{1,0:T(8,128)(2,1)S(1)} collective-permute-done((bf16[256,1152]{1,0:T(8,128)(2,1)S(1)}, bf16[256,1152]{1,0:T(8,128)(2,1)S(1)}, u32[]{:S(2)}, u32[]{:S(2)}) %collective-permute-start.6) | collective-permute-done | bytes 589856 | tf_op jit(solution)/shard_map/ppermute | solution.py:35
  36.8 2.7 %shard_map.65 = (bf16[192,768]{1,0:T(8,128)(2,1)S(1)}, bf16[192,768]{1,0:T(8,128)(2,1)S(1)}, f32[192,1152]{1,0:T(8,128)S(1)}, bf16[192,1152]{1,0:T(8,128)(2,1)S(1)}) custom-call(f32[1]{0:T(128)S(6)} %copy.6.scale_ref, f32[1]{0:T(128)S(6)} %copy.7.bias_ref, bf16[256,1152]{1,0:T(8,128)(2,1)S(1)} %collective-permute-done.5.refs_0_.refs_1_, ...), custom_call_target="tpu_custom_call" | custom-call | flops 1358954496 | bytes 4423688 | tf_op jit(solution)/shard_map/pallas_call | solution.py:56
  40.8 2.2 %collective-permute-done.13.refs_4_.refs_2_ = bf16[320,1152]{1,0:T(8,128)(2,1)S(1)} collective-permute-done((bf16[320,1152]{1,0:T(8,128)(2,1)S(1)}, bf16[320,1152]{1,0:T(8,128)(2,1)S(1)}, u32[]{:S(2)}, u32[]{:S(2)}) %collective-permute-start.13) | collective-permute-done | bytes 737312 | tf_op jit(solution)/shard_map/ppermute | solution.py:23
  43.0 2.7 %shard_map.69 = (bf16[320,1024]{1,0:T(8,128)(2,1)S(1)}, bf16[320,1152]{1,0:T(8,128)(2,1)S(1)}) custom-call(f32[1]{0:T(128)S(6)} %copy.6.scale_ref, f32[1]{0:T(128)S(6)} %copy.7.bias_ref, bf16[256,1152]{1,0:T(8,128)(2,1)S(1)} %shard_map.60.refs_0_, bf16[256,1152]{1,0:T(8,128)(2,1)S(1)} %collective-permute-done.5.refs_0_.refs_1_, ...), custom_call_target="tpu_custom_call" | custom-call | flops 1509949440 | bytes 3096584 | tf_op jit(solution)/shard_map/pallas_call | solution.py:56
  46.0 2.7 %shard_map.68 = (bf16[320,1024]{1,0:T(8,128)(2,1)S(1)}, f32[320,1152]{1,0:T(8,128)S(1)}) custom-call(f32[1]{0:T(128)S(6)} %copy.6.scale_ref, f32[1]{0:T(128)S(6)} %copy.7.bias_ref, bf16[256,1152]{1,0:T(8,128)(2,1)S(1)} %shard_map.60.refs_0_, bf16[256,1152]{1,0:T(8,128)(2,1)S(1)} %collective-permute-done.5.refs_0_.refs_1_, ...), custom_call_target="tpu_custom_call" | custom-call | flops 1509949440 | bytes 3096584 | tf_op jit(solution)/shard_map/pallas_call | solution.py:56
  48.8 2.3 %collective-permute-start.15 = (bf16[64,1152]{1,0:T(8,128)(2,1)S(1)}, bf16[64,1152]{1,0:T(8,128)(2,1)S(1)}, u32[]{:S(2)}, u32[]{:S(2)}) collective-permute-start(bf16[64,1152]{1,0:T(8,128)(2,1)S(1)} %get-tuple-element.64), channel_id=1, source_target_pairs={{0,224},{8,40},{32,0},{40,72},{64,32},{72,104},{96,64},{104,136},{... | collective-permute-start | bytes 442376 | tf_op jit(solution)/shard_map/ppermute | solution.py:45
  51.1 3.2 %shard_map.71 = (bf16[256,1152]{1,0:T(8,128)(2,1)S(1)}, bf16[256,1152]{1,0:T(8,128)(2,1)S(1)}, bf16[256,1152]{1,0:T(8,128)(2,1)S(1)}) custom-call(f32[1]{0:T(128)S(6)} %copy.6.scale_ref, bf16[192,1152]{1,0:T(8,128)(2,1)S(1)} %shard_map.62.refs_1_.refs_3_.refs_0_, bf16[192,1152]{1,0:T(8,128)(2,1)S(1)} %shard_map.63.refs_2_.refs_4_.refs_1_, ...), custom_call_target="tpu_custom_call" | custom-call | flops 1811939328 | bytes 4456452 | tf_op jit(solution)/shard_map/pallas_call | solution.py:56
  54.4 3.3 %collective-permute-start.16 = (bf16[128,1152]{1,0:T(8,128)(2,1)S(1)}, bf16[128,1152]{1,0:T(8,128)(2,1)S(1)}, u32[]{:S(2)}, u32[]{:S(2)}) collective-permute-start(bf16[128,1152]{1,0:T(8,128)(2,1)S(1)} %shard_map.72), channel_id=1, source_target_pairs={{0,224},{8,40},{32,0},{40,72},{64,32},{72,104},{96,64},{104,136},{... | collective-permute-start | bytes 884744 | tf_op jit(solution)/shard_map/ppermute | solution.py:45
  57.9 1.8 %collective-permute-start.21 = (bf16[256,1152]{1,0:T(8,128)(2,1)S(1)}, bf16[256,1152]{1,0:T(8,128)(2,1)S(1)}, u32[]{:S(2)}, u32[]{:S(2)}) collective-permute-start(bf16[256,1152]{1,0:T(8,128)(2,1)S(1)} %get-tuple-element.76), channel_id=1, source_target_pairs={{0,4},{1,5},{2,6},{3,7},{4,16},{5,17},{6,18},{7,19},{16,20},{17,21... | collective-permute-start | bytes 1769480 | tf_op jit(solution)/shard_map/ppermute | solution.py:35
  61.9 3.8 %collective-permute-start.17 = (bf16[128,1152]{1,0:T(8,128)(2,1)S(1)}, bf16[128,1152]{1,0:T(8,128)(2,1)S(1)}, u32[]{:S(2)}, u32[]{:S(2)}) collective-permute-start(bf16[128,1152]{1,0:T(8,128)(2,1)S(1)} %shard_map.73), channel_id=1, source_target_pairs={{0,224},{8,40},{32,0},{40,72},{64,32},{72,104},{96,64},{104,136},{... | collective-permute-start | bytes 884744 | tf_op jit(solution)/shard_map/ppermute | solution.py:45
  65.8 4.2 %collective-permute-done.17.b_ref = bf16[128,1152]{1,0:T(8,128)(2,1)S(1)} collective-permute-done((bf16[128,1152]{1,0:T(8,128)(2,1)S(1)}, bf16[128,1152]{1,0:T(8,128)(2,1)S(1)}, u32[]{:S(2)}, u32[]{:S(2)}) %collective-permute-start.17) | collective-permute-done | bytes 294944 | tf_op jit(solution)/shard_map/ppermute | solution.py:45
  70.0 4.0 %collective-permute-start.18 = (bf16[128,1152]{1,0:T(8,128)(2,1)S(1)}, bf16[128,1152]{1,0:T(8,128)(2,1)S(1)}, u32[]{:S(2)}, u32[]{:S(2)}) collective-permute-start(bf16[128,1152]{1,0:T(8,128)(2,1)S(1)} %shard_map.74), channel_id=1, source_target_pairs={{0,224},{8,40},{32,0},{40,72},{64,32},{72,104},{96,64},{104,136},{... | collective-permute-start | bytes 884744 | tf_op jit(solution)/shard_map/ppermute | solution.py:45
  76.5 2.3 %collective-permute-start.24 = (bf16[64,1152]{1,0:T(8,128)(2,1)S(1)}, bf16[64,1152]{1,0:T(8,128)(2,1)S(1)}, u32[]{:S(2)}, u32[]{:S(2)}) collective-permute-start(bf16[64,1152]{1,0:T(8,128)(2,1)S(1)} %get-tuple-element.80), channel_id=1, source_target_pairs={{0,1},{1,2},{2,3},{3,0},{4,5},{5,6},{6,7},{7,4},{16,17},{17,18},{1... | collective-permute-start | bytes 442376 | tf_op jit(solution)/shard_map/ppermute | solution.py:35
  79.2 2.8 %collective-permute-done.23.refs_1_ = bf16[64,1152]{1,0:T(8,128)(2,1)S(1)} collective-permute-done((bf16[64,1152]{1,0:T(8,128)(2,1)S(1)}, bf16[64,1152]{1,0:T(8,128)(2,1)S(1)}, u32[]{:S(2)}, u32[]{:S(2)}) %collective-permute-start.23) | collective-permute-done | bytes 147488 | tf_op jit(solution)/shard_map/ppermute | solution.py:35
  83.1 2.4 %collective-permute-done.25.refs_3_ = bf16[64,1152]{1,0:T(8,128)(2,1)S(1)} collective-permute-done((bf16[64,1152]{1,0:T(8,128)(2,1)S(1)}, bf16[64,1152]{1,0:T(8,128)(2,1)S(1)}, u32[]{:S(2)}, u32[]{:S(2)}) %collective-permute-start.25) | collective-permute-done | bytes 147488 | tf_op jit(solution)/shard_map/ppermute | solution.py:35
  (54 shorter events, 16.8 us)
Async XLA Ops:
  3.3 10.6 %collective-permute-start.4 = (bf16[128,1152]{1,0:T(8,128)(2,1)S(1)}, bf16[128,1152]{1,0:T(8,128)(2,1)S(1)}, u32[]{:S(2)}, u32[]{:S(2)}) collective-permute-start(bf16[128,1152]{1,0:T(8,128)(2,1)S(1)} %shard_map.61), channel_id=1, source_target_pairs={{0,32},{8,232},{32,64},{40,8},{64,96},{72,40},{96,128},{104,72},{1... | collective-permute-start | bytes 884744 | tf_op jit(solution)/shard_map/ppermute | solution.py:45
  5.3 6.7 %collective-permute-start.2 = (bf16[64,1152]{1,0:T(8,128)(2,1)S(1)}, bf16[64,1152]{1,0:T(8,128)(2,1)S(1)}, u32[]{:S(2)}, u32[]{:S(2)}) collective-permute-start(bf16[64,1152]{1,0:T(8,128)(2,1)S(1)} %get-tuple-element.42.refs_0_), channel_id=1, source_target_pairs={{0,2},{1,3},{2,0},{3,1},{4,6},{5,7},{6,4},{7,5},{16,18},{17,19},{1... | collective-permute-start | bytes 442376 | tf_op jit(solution)/shard_map/ppermute | solution.py:35
  6.7 6.8 %collective-permute-start.1 = (bf16[64,1152]{1,0:T(8,128)(2,1)S(1)}, bf16[64,1152]{1,0:T(8,128)(2,1)S(1)}, u32[]{:S(2)}, u32[]{:S(2)}) collective-permute-start(bf16[64,1152]{1,0:T(8,128)(2,1)S(1)} %get-tuple-element.42.refs_0_), channel_id=1, source_target_pairs={{0,3},{1,0},{2,1},{3,2},{4,7},{5,4},{6,5},{7,6},{16,19},{17,16},{1... | collective-permute-start | bytes 442376 | tf_op jit(solution)/shard_map/ppermute | solution.py:35
  6.7 6.8 %collective-permute-start = (bf16[64,1152]{1,0:T(8,128)(2,1)S(1)}, bf16[64,1152]{1,0:T(8,128)(2,1)S(1)}, u32[]{:S(2)}, u32[]{:S(2)}) collective-permute-start(bf16[64,1152]{1,0:T(8,128)(2,1)S(1)} %get-tuple-element.42.refs_0_), channel_id=1, source_target_pairs={{0,1},{1,2},{2,3},{3,0},{4,5},{5,6},{6,7},{7,4},{16,17},{17,18},{1... | collective-permute-start | bytes 442376 | tf_op jit(solution)/shard_map/ppermute | solution.py:35
  14.0 7.6 %collective-permute-start.9 = (bf16[128,1152]{1,0:T(8,128)(2,1)S(1)}, bf16[128,1152]{1,0:T(8,128)(2,1)S(1)}, u32[]{:S(2)}, u32[]{:S(2)}) collective-permute-start(bf16[128,1152]{1,0:T(8,128)(2,1)S(1)} %collective-permute-done.4.refs_1_), channel_id=1, source_target_pairs={{0,8},{8,0},{1,9},{9,1},{2,10},{10,2},{3,11},{11,3},{4,12},{12,4},... | collective-permute-start | bytes 884744 | tf_op jit(solution)/shard_map/ppermute | solution.py:23
  18.2 7.9 %collective-permute-start.8 = (bf16[128,1152]{1,0:T(8,128)(2,1)S(1)}, bf16[128,1152]{1,0:T(8,128)(2,1)S(1)}, u32[]{:S(2)}, u32[]{:S(2)}) collective-permute-start(bf16[128,1152]{1,0:T(8,128)(2,1)S(1)} %collective-permute-done.4.refs_1_), channel_id=1, source_target_pairs={{0,32},{8,232},{32,64},{40,8},{64,96},{72,40},{96,128},{104,72},{1... | collective-permute-start | bytes 884744 | tf_op jit(solution)/shard_map/ppermute | solution.py:45
  18.2 16.0 %collective-permute-start.7 = (bf16[256,1152]{1,0:T(8,128)(2,1)S(1)}, bf16[256,1152]{1,0:T(8,128)(2,1)S(1)}, u32[]{:S(2)}, u32[]{:S(2)}) collective-permute-start(bf16[256,1152]{1,0:T(8,128)(2,1)S(1)} %shard_map.60.refs_0_), channel_id=1, source_target_pairs={{0,20},{1,21},{2,22},{3,23},{4,0},{5,1},{6,2},{7,3},{16,4},{17,5},... | collective-permute-start | bytes 1769480 | tf_op jit(solution)/shard_map/ppermute | solution.py:35
  19.4 17.4 %collective-permute-start.6 = (bf16[256,1152]{1,0:T(8,128)(2,1)S(1)}, bf16[256,1152]{1,0:T(8,128)(2,1)S(1)}, u32[]{:S(2)}, u32[]{:S(2)}) collective-permute-start(bf16[256,1152]{1,0:T(8,128)(2,1)S(1)} %shard_map.60.refs_0_), channel_id=1, source_target_pairs={{0,4},{1,5},{2,6},{3,7},{4,16},{5,17},{6,18},{7,19},{16,20},{17,21... | collective-permute-start | bytes 1769480 | tf_op jit(solution)/shard_map/ppermute | solution.py:35
  20.2 16.6 %collective-permute-start.5 = (bf16[256,1152]{1,0:T(8,128)(2,1)S(1)}, bf16[256,1152]{1,0:T(8,128)(2,1)S(1)}, u32[]{:S(2)}, u32[]{:S(2)}) collective-permute-start(bf16[256,1152]{1,0:T(8,128)(2,1)S(1)} %shard_map.60.refs_0_), channel_id=1, source_target_pairs={{0,16},{1,17},{2,18},{3,19},{4,20},{5,21},{6,22},{7,23},{16,0},{17... | collective-permute-start | bytes 1769480 | tf_op jit(solution)/shard_map/ppermute | solution.py:35
  26.1 7.9 %collective-permute-start.10 = (bf16[128,1152]{1,0:T(8,128)(2,1)S(1)}, bf16[128,1152]{1,0:T(8,128)(2,1)S(1)}, u32[]{:S(2)}, u32[]{:S(2)}) collective-permute-start(bf16[128,1152]{1,0:T(8,128)(2,1)S(1)} %collective-permute-done.8.refs_0_), channel_id=1, source_target_pairs={{0,32},{8,232},{32,64},{40,8},{64,96},{72,40},{96,128},{104,72},{1... | collective-permute-start | bytes 884744 | tf_op jit(solution)/shard_map/ppermute | solution.py:45
  34.0 6.4 %collective-permute-start.11 = (bf16[64,1152]{1,0:T(8,128)(2,1)S(1)}, bf16[64,1152]{1,0:T(8,128)(2,1)S(1)}, u32[]{:S(2)}, u32[]{:S(2)}) collective-permute-start(bf16[64,1152]{1,0:T(8,128)(2,1)S(1)} %slice.9), channel_id=1, source_target_pairs={{0,32},{8,232},{32,64},{40,8},{64,96},{72,40},{96,128},{104,72},{1... | collective-permute-start | bytes 442376 | tf_op jit(solution)/shard_map/ppermute | solution.py:45
  45.7 2.9 %collective-permute-start.14 = (bf16[320,1152]{1,0:T(8,128)(2,1)S(1)}, bf16[320,1152]{1,0:T(8,128)(2,1)S(1)}, u32[]{:S(2)}, u32[]{:S(2)}) collective-permute-start(bf16[320,1152]{1,0:T(8,128)(2,1)S(1)} %get-tuple-element.60), channel_id=1, source_target_pairs={{0,8},{8,0},{1,9},{9,1},{2,10},{10,2},{3,11},{11,3},{4,12},{12,4},... | collective-permute-start | bytes 2211848 | tf_op jit(solution)/shard_map/ppermute | solution.py:23
  48.8 5.5 %collective-permute-start.15 = (bf16[64,1152]{1,0:T(8,128)(2,1)S(1)}, bf16[64,1152]{1,0:T(8,128)(2,1)S(1)}, u32[]{:S(2)}, u32[]{:S(2)}) collective-permute-start(bf16[64,1152]{1,0:T(8,128)(2,1)S(1)} %get-tuple-element.64), channel_id=1, source_target_pairs={{0,224},{8,40},{32,0},{40,72},{64,32},{72,104},{96,64},{104,136},{... | collective-permute-start | bytes 442376 | tf_op jit(solution)/shard_map/ppermute | solution.py:45
  54.4 7.5 %collective-permute-start.16 = (bf16[128,1152]{1,0:T(8,128)(2,1)S(1)}, bf16[128,1152]{1,0:T(8,128)(2,1)S(1)}, u32[]{:S(2)}, u32[]{:S(2)}) collective-permute-start(bf16[128,1152]{1,0:T(8,128)(2,1)S(1)} %shard_map.72), channel_id=1, source_target_pairs={{0,224},{8,40},{32,0},{40,72},{64,32},{72,104},{96,64},{104,136},{... | collective-permute-start | bytes 884744 | tf_op jit(solution)/shard_map/ppermute | solution.py:45
  57.6 8.1 %collective-permute-start.12 = (bf16[192,1152]{1,0:T(8,128)(2,1)S(1)}, bf16[192,1152]{1,0:T(8,128)(2,1)S(1)}, u32[]{:S(2)}, u32[]{:S(2)}) collective-permute-start(bf16[192,1152]{1,0:T(8,128)(2,1)S(1)} %get-tuple-element.55), channel_id=1, source_target_pairs={{0,8},{8,0},{1,9},{9,1},{2,10},{10,2},{3,11},{11,3},{4,12},{12,4},... | collective-permute-start | bytes 1327112 | tf_op jit(solution)/shard_map/ppermute | solution.py:23
  57.6 17.6 %collective-permute-start.20 = (bf16[256,1152]{1,0:T(8,128)(2,1)S(1)}, bf16[256,1152]{1,0:T(8,128)(2,1)S(1)}, u32[]{:S(2)}, u32[]{:S(2)}) collective-permute-start(bf16[256,1152]{1,0:T(8,128)(2,1)S(1)} %get-tuple-element.75), channel_id=1, source_target_pairs={{0,20},{1,21},{2,22},{3,23},{4,0},{5,1},{6,2},{7,3},{16,4},{17,5},... | collective-permute-start | bytes 1769480 | tf_op jit(solution)/shard_map/ppermute | solution.py:35
  57.9 17.4 %collective-permute-start.21 = (bf16[256,1152]{1,0:T(8,128)(2,1)S(1)}, bf16[256,1152]{1,0:T(8,128)(2,1)S(1)}, u32[]{:S(2)}, u32[]{:S(2)}) collective-permute-start(bf16[256,1152]{1,0:T(8,128)(2,1)S(1)} %get-tuple-element.76), channel_id=1, source_target_pairs={{0,4},{1,5},{2,6},{3,7},{4,16},{5,17},{6,18},{7,19},{16,20},{17,21... | collective-permute-start | bytes 1769480 | tf_op jit(solution)/shard_map/ppermute | solution.py:35
  59.6 15.6 %collective-permute-start.22 = (bf16[256,1152]{1,0:T(8,128)(2,1)S(1)}, bf16[256,1152]{1,0:T(8,128)(2,1)S(1)}, u32[]{:S(2)}, u32[]{:S(2)}) collective-permute-start(bf16[256,1152]{1,0:T(8,128)(2,1)S(1)} %get-tuple-element.77), channel_id=1, source_target_pairs={{0,16},{1,17},{2,18},{3,19},{4,20},{5,21},{6,22},{7,23},{16,0},{17... | collective-permute-start | bytes 1769480 | tf_op jit(solution)/shard_map/ppermute | solution.py:35
  61.9 8.0 %collective-permute-start.17 = (bf16[128,1152]{1,0:T(8,128)(2,1)S(1)}, bf16[128,1152]{1,0:T(8,128)(2,1)S(1)}, u32[]{:S(2)}, u32[]{:S(2)}) collective-permute-start(bf16[128,1152]{1,0:T(8,128)(2,1)S(1)} %shard_map.73), channel_id=1, source_target_pairs={{0,224},{8,40},{32,0},{40,72},{64,32},{72,104},{96,64},{104,136},{... | collective-permute-start | bytes 884744 | tf_op jit(solution)/shard_map/ppermute | solution.py:45
  70.0 9.0 %collective-permute-start.18 = (bf16[128,1152]{1,0:T(8,128)(2,1)S(1)}, bf16[128,1152]{1,0:T(8,128)(2,1)S(1)}, u32[]{:S(2)}, u32[]{:S(2)}) collective-permute-start(bf16[128,1152]{1,0:T(8,128)(2,1)S(1)} %shard_map.74), channel_id=1, source_target_pairs={{0,224},{8,40},{32,0},{40,72},{64,32},{72,104},{96,64},{104,136},{... | collective-permute-start | bytes 884744 | tf_op jit(solution)/shard_map/ppermute | solution.py:45
  75.6 6.4 %collective-permute-start.23 = (bf16[64,1152]{1,0:T(8,128)(2,1)S(1)}, bf16[64,1152]{1,0:T(8,128)(2,1)S(1)}, u32[]{:S(2)}, u32[]{:S(2)}) collective-permute-start(bf16[64,1152]{1,0:T(8,128)(2,1)S(1)} %get-tuple-element.79), channel_id=1, source_target_pairs={{0,3},{1,0},{2,1},{3,2},{4,7},{5,4},{6,5},{7,6},{16,19},{17,16},{1... | collective-permute-start | bytes 442376 | tf_op jit(solution)/shard_map/ppermute | solution.py:35
  76.5 6.6 %collective-permute-start.24 = (bf16[64,1152]{1,0:T(8,128)(2,1)S(1)}, bf16[64,1152]{1,0:T(8,128)(2,1)S(1)}, u32[]{:S(2)}, u32[]{:S(2)}) collective-permute-start(bf16[64,1152]{1,0:T(8,128)(2,1)S(1)} %get-tuple-element.80), channel_id=1, source_target_pairs={{0,1},{1,2},{2,3},{3,0},{4,5},{5,6},{6,7},{7,4},{16,17},{17,18},{1... | collective-permute-start | bytes 442376 | tf_op jit(solution)/shard_map/ppermute | solution.py:35
  78.9 6.6 %collective-permute-start.25 = (bf16[64,1152]{1,0:T(8,128)(2,1)S(1)}, bf16[64,1152]{1,0:T(8,128)(2,1)S(1)}, u32[]{:S(2)}, u32[]{:S(2)}) collective-permute-start(bf16[64,1152]{1,0:T(8,128)(2,1)S(1)} %get-tuple-element.81), channel_id=1, source_target_pairs={{0,2},{1,3},{2,0},{3,1},{4,6},{5,7},{6,4},{7,5},{16,18},{17,19},{1... | collective-permute-start | bytes 442376 | tf_op jit(solution)/shard_map/ppermute | solution.py:35
  79.1 7.3 %collective-permute-start.19 = (bf16[64,1152]{1,0:T(8,128)(2,1)S(1)}, bf16[64,1152]{1,0:T(8,128)(2,1)S(1)}, u32[]{:S(2)}, u32[]{:S(2)}) collective-permute-start(bf16[64,1152]{1,0:T(8,128)(2,1)S(1)} %get-tuple-element.82), channel_id=1, source_target_pairs={{0,8},{8,0},{1,9},{9,1},{2,10},{10,2},{3,11},{11,3},{4,12},{12,4},... | collective-permute-start | bytes 442376 | tf_op jit(solution)/shard_map/ppermute | solution.py:23
  (4 other events, 25.2 us)

commit v7 on v6

--- a/solution.py
+++ b/solution.py
@@ -156,14 +156,19 @@
     out_ref[pl.ds(rows, rows), :] = sib_ref[...]
 
 
-def end_kernel(raw_ref, *refs):
-    *parts, out_ref = refs
-    raw, grad = (raw_ref[...], parts[0][...].astype(F32))
+def gradient_of(raw, parts):
+    grad = parts[0][...].astype(F32)
     for part in parts[1:]:
         grad += part[...].astype(F32)
     inv = inverse(raw)
     across = jnp.sum(raw * grad, axis=1, keepdims=True)
-    out_ref[...] = inv * grad - raw * (inv * inv * inv) * across
+    return inv * grad - raw * (inv * inv * inv) * across
+
+
+def end_kernel(count, img_ref, txt_ref, *refs):
+    *parts, img_out, txt_out = refs
+    img_out[...] = gradient_of(img_ref[...], parts[:count])
+    txt_out[...] = gradient_of(txt_ref[...], parts[count:])
 
 
 def added(a, b):
@@ -206,16 +211,16 @@
     others = (texts3, texts1, texts2)
     z1_sib = shifted(z1, "c", 1)
     z2 = fanned(z1, 1)
-    z2, z1_sib = lax.optimization_barrier((z2, z1_sib))
-    keep_a, send_a = (join(img, z1), join(sib, z1_sib))
+    keep_a, send_a = (join(img, z1, z2), join(sib, z1_sib, shifted(z2, "c", 1)))
     w_a0, d_a0 = image_part(rows, (texts0,), (keep_a, send_a), (), (F32, F32))
     z3 = fanned(z2, 1)
     z3, *d_a0 = lax.optimization_barrier((z3, *d_a0))
     far = fanned(z3[:rows], 1)
+    far, *others = lax.optimization_barrier((far, *others))
+    keep_b = join(z3, far)
+    send_b = shifted(keep_b, "c", 1)
     w_a, (dk_a, ds_a) = image_part(0, others, (keep_a, send_a), d_a0, (F32, BF16))
-    far, ds_a = lax.optimization_barrier((far, ds_a))
-    keep_b = join(z2, z3, far)
-    send_b = shifted(keep_b, "c", 1)
+    send_b, ds_a = lax.optimization_barrier((send_b, ds_a))
 
     w_sb, (ds_b,) = image_part(0, (texts0, *others), (send_b,), (), (BF16,))
     back_b, back_a = (shifted(ds_b, "c", 1), shifted(ds_a, "c", 1))
@@ -234,14 +239,12 @@
     )
     d_texts0 = text_part([[(0, 0), (1, 0), (4, 0), (5, 0)]], F32)[0]
 
-    z2_sum, z3_own, z3_sib, far_sum = local(
+    z3_own, z3_sib, far_sum = local(
+        functools.partial(split_kernel, 2), [block] * 3, dk_b, back_b
+    )
+    own, z1_sum, z2_sum = local(
         functools.partial(split_kernel, 2),
-        [shaped((2 * rows, width), BF16), block, block, block],
-        dk_b, back_b,
-    )
-    own, z1_sum = local(
-        functools.partial(split_kernel, 2),
-        [shaped((rows, width), F32), shaped((2 * rows, width), BF16)],
+        [shaped((rows, width), F32)] + [shaped((2 * rows, width), BF16)] * 2,
         dk_a, back_a,
     )
     far_back = fanned(far_sum, -1)
@@ -257,6 +260,7 @@
     )
     returned = fanned(returned, -1)
     returned = fanned(added(z2_sum, returned), -1)
+    returned, back3 = lax.optimization_barrier((returned, back3))
     returned = fanned(added(z1_sum, returned), -1)
     other = shifted(returned[rows:], "c", 1)
     txt_own, d_ahead, d_behind, d_across = local(
@@ -271,10 +275,13 @@
     )
 
     whole = pl.BlockSpec((rows, width), lambda: (0, 0))
-    end = lambda raw, *parts: local(
-        end_kernel, shaped((rows, width), F32), raw, *parts, out_specs=whole
-    )
-    return (end(images, own, returned[:rows], other), end(texts, txt_own, d_ahead, d_behind, d_across))
+    img_parts = (own, returned[:rows], other)
+    return local(
+        functools.partial(end_kernel, len(img_parts)),
+        [shaped((rows, width), F32)] * 2,
+        images, texts, *img_parts, txt_own, d_ahead, d_behind, d_across,
+        out_specs=[whole, whole],
+    )
 
 
 def solution(mesh):

time: 87.4 us -> 83.2 us (0.952)
  the two profiles are of different devices: /device:TPU:6 before, /device:TPU:8 now
where the time goes in v7:
time: 83.2 us; the launch traced here: 82.6 us
  starting transfers between devices  32.4 us (39%)
  waiting for transfers between devices  31 us (37%)
  Pallas kernels  17 us (20%)
  between operations  2.12 us (3%)
    ppermute x12, starting transfers between devices, crossed(): return lax.ppermute(value, PLANE, pairs)  17.9 us
    pallas_call x19, Pallas kernels, local(): pl.pallas_call(kernel, out_shape=outs, in_specs=[SMEM] * scalars + [place...  17 us
    ppermute x8, waiting for transfers between devices, fanned(): return lax.ppermute(value, ('z', 'c'), pairs)  15.7 us
    ppermute x12, waiting for transfers between devices, crossed(): return lax.ppermute(value, PLANE, pairs)  13.9 us
    ppermute x8, starting transfers between devices, fanned(): return lax.ppermute(value, ('z', 'c'), pairs)  13.4 us
  transfers between devices with their start and end apart: 27, of which 16 were waited for; matrix products, arithmetic and copies ran while one was open for 0% of the time, Pallas kernels for 15%

profile of v7, /device:TPU:8, one launch (start us, length us, event | category | flops | bytes accessed | tf_op | source)
XLA Modules:
  0.0 82.6 jit_solution(4464635436287592046)
XLA Ops:
  3.3 2.0 %collective-permute-start.4 = (bf16[128,1152]{1,0:T(8,128)(2,1)S(1)}, bf16[128,1152]{1,0:T(8,128)(2,1)S(1)}, u32[]{:S(2)}, u32[]{:S(2)}) collective-permute-start(bf16[128,1152]{1,0:T(8,128)(2,1)S(1)} %shard_map.61), channel_id=1, source_target_pairs={{0,32},{8,232},{32,64},{40,8},{64,96},{72,40},{96,128},{104,72},{1... | collective-permute-start | bytes 884744 | tf_op jit(solution)/shard_map/ppermute | solution.py:45
  5.3 3.0 %collective-permute-start.2 = (bf16[64,1152]{1,0:T(8,128)(2,1)S(1)}, bf16[64,1152]{1,0:T(8,128)(2,1)S(1)}, u32[]{:S(2)}, u32[]{:S(2)}) collective-permute-start(bf16[64,1152]{1,0:T(8,128)(2,1)S(1)} %get-tuple-element.46.refs_0_), channel_id=1, source_target_pairs={{0,2},{1,3},{2,0},{3,1},{4,6},{5,7},{6,4},{7,5},{16,18},{17,19},{1... | collective-permute-start | bytes 442376 | tf_op jit(solution)/shard_map/ppermute | solution.py:35
  10.4 1.6 %collective-permute-done.2.refs_3_ = bf16[64,1152]{1,0:T(8,128)(2,1)S(1)} collective-permute-done((bf16[64,1152]{1,0:T(8,128)(2,1)S(1)}, bf16[64,1152]{1,0:T(8,128)(2,1)S(1)}, u32[]{:S(2)}, u32[]{:S(2)}) %collective-permute-start.2) | collective-permute-done | bytes 147488 | tf_op jit(solution)/shard_map/ppermute | solution.py:35
  12.0 1.7 %collective-permute-done.1.refs_2_ = bf16[64,1152]{1,0:T(8,128)(2,1)S(1)} collective-permute-done((bf16[64,1152]{1,0:T(8,128)(2,1)S(1)}, bf16[64,1152]{1,0:T(8,128)(2,1)S(1)}, u32[]{:S(2)}, u32[]{:S(2)}) %collective-permute-start.1) | collective-permute-done | bytes 147488 | tf_op jit(solution)/shard_map/ppermute | solution.py:35
  13.6 2.2 %collective-permute-done.refs_1_ = bf16[64,1152]{1,0:T(8,128)(2,1)S(1)} collective-permute-done((bf16[64,1152]{1,0:T(8,128)(2,1)S(1)}, bf16[64,1152]{1,0:T(8,128)(2,1)S(1)}, u32[]{:S(2)}, u32[]{:S(2)}) %collective-permute-start) | collective-permute-done | bytes 147488 | tf_op jit(solution)/shard_map/ppermute | solution.py:35
  15.9 2.0 %collective-permute-start.5 = (bf16[128,1152]{1,0:T(8,128)(2,1)S(1)}, bf16[128,1152]{1,0:T(8,128)(2,1)S(1)}, u32[]{:S(2)}, u32[]{:S(2)}) collective-permute-start(bf16[128,1152]{1,0:T(8,128)(2,1)S(1)} %collective-permute-done.4.refs_1_), channel_id=1, source_target_pairs={{0,32},{8,232},{32,64},{40,8},{64,96},{72,40},{96,128},{104,72},{1... | collective-permute-start | bytes 884744 | tf_op jit(solution)/shard_map/ppermute | solution.py:45
  17.9 1.7 %collective-permute-start.12 = (bf16[256,1152]{1,0:T(8,128)(2,1)S(1)}, bf16[256,1152]{1,0:T(8,128)(2,1)S(1)}, u32[]{:S(2)}, u32[]{:S(2)}) collective-permute-start(bf16[256,1152]{1,0:T(8,128)(2,1)S(1)} %shard_map.60.refs_0_), channel_id=1, source_target_pairs={{0,20},{1,21},{2,22},{3,23},{4,0},{5,1},{6,2},{7,3},{16,4},{17,5},... | collective-permute-start | bytes 1769480 | tf_op jit(solution)/shard_map/ppermute | solution.py:35
  19.9 3.5 %collective-permute-start.10 = (bf16[256,1152]{1,0:T(8,128)(2,1)S(1)}, bf16[256,1152]{1,0:T(8,128)(2,1)S(1)}, u32[]{:S(2)}, u32[]{:S(2)}) collective-permute-start(bf16[256,1152]{1,0:T(8,128)(2,1)S(1)} %shard_map.60.refs_0_), channel_id=1, source_target_pairs={{0,16},{1,17},{2,18},{3,19},{4,20},{5,21},{6,22},{7,23},{16,0},{17... | collective-permute-start | bytes 1769480 | tf_op jit(solution)/shard_map/ppermute | solution.py:35
  26.9 2.0 %shard_map.64 = (bf16[320,256]{1,0:T(8,128)(2,1)S(1)}, bf16[320,256]{1,0:T(8,128)(2,1)S(1)}, f32[320,1152]{1,0:T(8,128)S(1)}, f32[320,1152]{1,0:T(8,128)S(1)}) custom-call(f32[1]{0:T(128)S(6)} %copy.6.scale_ref, f32[1]{0:T(128)S(6)} %copy.7.bias_ref, bf16[256,1152]{1,0:T(8,128)(2,1)S(1)} %shard_map.60.refs_0_, ...), custom_call_target="tpu_custom_call" | custom-call | flops 754974720 | bytes 2064392 | tf_op jit(solution)/shard_map/pallas_call | solution.py:56
  28.8 3.8 %collective-permute-done.6.refs_0_ = bf16[128,1152]{1,0:T(8,128)(2,1)S(1)} collective-permute-done((bf16[128,1152]{1,0:T(8,128)(2,1)S(1)}, bf16[128,1152]{1,0:T(8,128)(2,1)S(1)}, u32[]{:S(2)}, u32[]{:S(2)}) %collective-permute-start.6) | collective-permute-done | bytes 294944 | tf_op jit(solution)/shard_map/ppermute | solution.py:45
  32.9 2.2 %collective-permute-done.10.refs_0_.refs_1_ = bf16[256,1152]{1,0:T(8,128)(2,1)S(1)} collective-permute-done((bf16[256,1152]{1,0:T(8,128)(2,1)S(1)}, bf16[256,1152]{1,0:T(8,128)(2,1)S(1)}, u32[]{:S(2)}, u32[]{:S(2)}) %collective-permute-start.10) | collective-permute-done | bytes 589856 | tf_op jit(solution)/shard_map/ppermute | solution.py:35
  35.1 4.0 %collective-permute-done.9.refs_1_ = bf16[64,1152]{1,0:T(8,128)(2,1)S(1)} collective-permute-done((bf16[64,1152]{1,0:T(8,128)(2,1)S(1)}, bf16[64,1152]{1,0:T(8,128)(2,1)S(1)}, u32[]{:S(2)}, u32[]{:S(2)}) %collective-permute-start.9) | collective-permute-done | bytes 147488 | tf_op jit(solution)/shard_map/ppermute | solution.py:45
  39.4 3.3 %shard_map.65 = (bf16[320,768]{1,0:T(8,128)(2,1)S(1)}, bf16[320,768]{1,0:T(8,128)(2,1)S(1)}, f32[320,1152]{1,0:T(8,128)S(1)}, bf16[320,1152]{1,0:T(8,128)(2,1)S(1)}) custom-call(f32[1]{0:T(128)S(6)} %copy.6.scale_ref, f32[1]{0:T(128)S(6)} %copy.7.bias_ref, bf16[256,1152]{1,0:T(8,128)(2,1)S(1)} %collective-permute-done.10.refs_0_.refs_1_, ...), custom_call_target="tpu_custom_call" | custom-call | flops 2264924160 | bytes 6193160 | tf_op jit(solution)/shard_map/pallas_call | solution.py:56
  42.8 2.1 %shard_map.69 = (bf16[192,1024]{1,0:T(8,128)(2,1)S(1)}, bf16[192,1152]{1,0:T(8,128)(2,1)S(1)}) custom-call(f32[1]{0:T(128)S(6)} %copy.6.scale_ref, f32[1]{0:T(128)S(6)} %copy.7.bias_ref, bf16[256,1152]{1,0:T(8,128)(2,1)S(1)} %shard_map.60.refs_0_, bf16[256,1152]{1,0:T(8,128)(2,1)S(1)} %collective-permute-done.10.refs_0_.refs_1_, ...), custom_call_target="tpu_custom_call" | custom-call | flops 905969664 | bytes 2801672 | tf_op jit(solution)/shard_map/pallas_call | solution.py:56
  45.6 2.1 %shard_map.68 = (bf16[192,1024]{1,0:T(8,128)(2,1)S(1)}, f32[192,1152]{1,0:T(8,128)S(1)}) custom-call(f32[1]{0:T(128)S(6)} %copy.6.scale_ref, f32[1]{0:T(128)S(6)} %copy.7.bias_ref, bf16[256,1152]{1,0:T(8,128)(2,1)S(1)} %shard_map.60.refs_0_, bf16[256,1152]{1,0:T(8,128)(2,1)S(1)} %collective-permute-done.10.refs_0_.refs_1_, ...), custom_call_target="tpu_custom_call" | custom-call | flops 905969664 | bytes 2801672 | tf_op jit(solution)/shard_map/pallas_call | solution.py:56
  48.2 3.2 %shard_map.71 = (bf16[256,1152]{1,0:T(8,128)(2,1)S(1)}, bf16[256,1152]{1,0:T(8,128)(2,1)S(1)}, bf16[256,1152]{1,0:T(8,128)(2,1)S(1)}) custom-call(f32[1]{0:T(128)S(6)} %copy.6.scale_ref, bf16[320,1152]{1,0:T(8,128)(2,1)S(1)} %shard_map.62.refs_1_.refs_3_.refs_0_, bf16[320,1152]{1,0:T(8,128)(2,1)S(1)} %shard_map.63.refs_2_.refs_4_.refs_1_, ...), custom_call_target="tpu_custom_call" | custom-call | flops 1811939328 | bytes 4456452 | tf_op jit(solution)/shard_map/pallas_call | solution.py:56
  51.4 1.7 %collective-permute-done.16.far_ref = bf16[64,1152]{1,0:T(8,128)(2,1)S(1)} collective-permute-done((bf16[64,1152]{1,0:T(8,128)(2,1)S(1)}, bf16[64,1152]{1,0:T(8,128)(2,1)S(1)}, u32[]{:S(2)}, u32[]{:S(2)}) %collective-permute-start.16) | collective-permute-done | bytes 147488 | tf_op jit(solution)/shard_map/ppermute | solution.py:45
  54.7 2.4 %collective-permute-start.19 = (bf16[256,1152]{1,0:T(8,128)(2,1)S(1)}, bf16[256,1152]{1,0:T(8,128)(2,1)S(1)}, u32[]{:S(2)}, u32[]{:S(2)}) collective-permute-start(bf16[256,1152]{1,0:T(8,128)(2,1)S(1)} %get-tuple-element.81), channel_id=1, source_target_pairs={{0,16},{1,17},{2,18},{3,19},{4,20},{5,21},{6,22},{7,23},{16,0},{17... | collective-permute-start | bytes 1769480 | tf_op jit(solution)/shard_map/ppermute | solution.py:35
  60.0 2.8 %collective-permute-start.18 = (bf16[128,1152]{1,0:T(8,128)(2,1)S(1)}, bf16[128,1152]{1,0:T(8,128)(2,1)S(1)}, u32[]{:S(2)}, u32[]{:S(2)}) collective-permute-start(bf16[128,1152]{1,0:T(8,128)(2,1)S(1)} %shard_map.73), channel_id=1, source_target_pairs={{0,224},{8,40},{32,0},{40,72},{64,32},{72,104},{96,64},{104,136},{... | collective-permute-start | bytes 884744 | tf_op jit(solution)/shard_map/ppermute | solution.py:45
  62.8 4.2 %collective-permute-done.18.b_ref = bf16[128,1152]{1,0:T(8,128)(2,1)S(1)} collective-permute-done((bf16[128,1152]{1,0:T(8,128)(2,1)S(1)}, bf16[128,1152]{1,0:T(8,128)(2,1)S(1)}, u32[]{:S(2)}, u32[]{:S(2)}) %collective-permute-start.18) | collective-permute-done | bytes 294944 | tf_op jit(solution)/shard_map/ppermute | solution.py:45
  67.1 3.8 %collective-permute-start.20 = (bf16[128,1152]{1,0:T(8,128)(2,1)S(1)}, bf16[128,1152]{1,0:T(8,128)(2,1)S(1)}, u32[]{:S(2)}, u32[]{:S(2)}) collective-permute-start(bf16[128,1152]{1,0:T(8,128)(2,1)S(1)} %shard_map.74), channel_id=1, source_target_pairs={{0,224},{8,40},{32,0},{40,72},{64,32},{72,104},{96,64},{104,136},{... | collective-permute-start | bytes 884744 | tf_op jit(solution)/shard_map/ppermute | solution.py:45
  75.7 2.3 %collective-permute-done.24.refs_4_ = bf16[64,1152]{1,0:T(8,128)(2,1)S(1)} collective-permute-done((bf16[64,1152]{1,0:T(8,128)(2,1)S(1)}, bf16[64,1152]{1,0:T(8,128)(2,1)S(1)}, u32[]{:S(2)}, u32[]{:S(2)}) %collective-permute-start.24) | collective-permute-done | bytes 147488 | tf_op jit(solution)/shard_map/ppermute | solution.py:35
  78.0 1.8 %collective-permute-done.25.refs_5_ = bf16[64,1152]{1,0:T(8,128)(2,1)S(1)} collective-permute-done((bf16[64,1152]{1,0:T(8,128)(2,1)S(1)}, bf16[64,1152]{1,0:T(8,128)(2,1)S(1)}, u32[]{:S(2)}, u32[]{:S(2)}) %collective-permute-start.25) | collective-permute-done | bytes 147488 | tf_op jit(solution)/shard_map/ppermute | solution.py:35
  79.8 1.7 %collective-permute-done.26.refs_6_ = bf16[64,1152]{1,0:T(8,128)(2,1)S(1)} collective-permute-done((bf16[64,1152]{1,0:T(8,128)(2,1)S(1)}, bf16[64,1152]{1,0:T(8,128)(2,1)S(1)}, u32[]{:S(2)}, u32[]{:S(2)}) %collective-permute-start.26) | collective-permute-done | bytes 147488 | tf_op jit(solution)/shard_map/ppermute | solution.py:35
  (55 shorter events, 19.3 us)
Async XLA Ops:
  3.3 12.6 %collective-permute-start.4 = (bf16[128,1152]{1,0:T(8,128)(2,1)S(1)}, bf16[128,1152]{1,0:T(8,128)(2,1)S(1)}, u32[]{:S(2)}, u32[]{:S(2)}) collective-permute-start(bf16[128,1152]{1,0:T(8,128)(2,1)S(1)} %shard_map.61), channel_id=1, source_target_pairs={{0,32},{8,232},{32,64},{40,8},{64,96},{72,40},{96,128},{104,72},{1... | collective-permute-start | bytes 884744 | tf_op jit(solution)/shard_map/ppermute | solution.py:45
  5.3 6.6 %collective-permute-start.2 = (bf16[64,1152]{1,0:T(8,128)(2,1)S(1)}, bf16[64,1152]{1,0:T(8,128)(2,1)S(1)}, u32[]{:S(2)}, u32[]{:S(2)}) collective-permute-start(bf16[64,1152]{1,0:T(8,128)(2,1)S(1)} %get-tuple-element.46.refs_0_), channel_id=1, source_target_pairs={{0,2},{1,3},{2,0},{3,1},{4,6},{5,7},{6,4},{7,5},{16,18},{17,19},{1... | collective-permute-start | bytes 442376 | tf_op jit(solution)/shard_map/ppermute | solution.py:35
  8.3 5.3 %collective-permute-start.1 = (bf16[64,1152]{1,0:T(8,128)(2,1)S(1)}, bf16[64,1152]{1,0:T(8,128)(2,1)S(1)}, u32[]{:S(2)}, u32[]{:S(2)}) collective-permute-start(bf16[64,1152]{1,0:T(8,128)(2,1)S(1)} %get-tuple-element.46.refs_0_), channel_id=1, source_target_pairs={{0,3},{1,0},{2,1},{3,2},{4,7},{5,4},{6,5},{7,6},{16,19},{17,16},{1... | collective-permute-start | bytes 442376 | tf_op jit(solution)/shard_map/ppermute | solution.py:35
  9.5 6.4 %collective-permute-start = (bf16[64,1152]{1,0:T(8,128)(2,1)S(1)}, bf16[64,1152]{1,0:T(8,128)(2,1)S(1)}, u32[]{:S(2)}, u32[]{:S(2)}) collective-permute-start(bf16[64,1152]{1,0:T(8,128)(2,1)S(1)} %get-tuple-element.46.refs_0_), channel_id=1, source_target_pairs={{0,1},{1,2},{2,3},{3,0},{4,5},{5,6},{6,7},{7,4},{16,17},{17,18},{1... | collective-permute-start | bytes 442376 | tf_op jit(solution)/shard_map/ppermute | solution.py:35
  15.9 8.8 %collective-permute-start.5 = (bf16[128,1152]{1,0:T(8,128)(2,1)S(1)}, bf16[128,1152]{1,0:T(8,128)(2,1)S(1)}, u32[]{:S(2)}, u32[]{:S(2)}) collective-permute-start(bf16[128,1152]{1,0:T(8,128)(2,1)S(1)} %collective-permute-done.4.refs_1_), channel_id=1, source_target_pairs={{0,32},{8,232},{32,64},{40,8},{64,96},{72,40},{96,128},{104,72},{1... | collective-permute-start | bytes 884744 | tf_op jit(solution)/shard_map/ppermute | solution.py:45
  17.9 6.8 %collective-permute-start.7 = (bf16[128,1152]{1,0:T(8,128)(2,1)S(1)}, bf16[128,1152]{1,0:T(8,128)(2,1)S(1)}, u32[]{:S(2)}, u32[]{:S(2)}) collective-permute-start(bf16[128,1152]{1,0:T(8,128)(2,1)S(1)} %collective-permute-done.4.refs_1_), channel_id=1, source_target_pairs={{0,8},{8,0},{1,9},{9,1},{2,10},{10,2},{3,11},{11,3},{4,12},{12,4},... | collective-permute-start | bytes 884744 | tf_op jit(solution)/shard_map/ppermute | solution.py:23
  17.9 15.0 %collective-permute-start.12 = (bf16[256,1152]{1,0:T(8,128)(2,1)S(1)}, bf16[256,1152]{1,0:T(8,128)(2,1)S(1)}, u32[]{:S(2)}, u32[]{:S(2)}) collective-permute-start(bf16[256,1152]{1,0:T(8,128)(2,1)S(1)} %shard_map.60.refs_0_), channel_id=1, source_target_pairs={{0,20},{1,21},{2,22},{3,23},{4,0},{5,1},{6,2},{7,3},{16,4},{17,5},... | collective-permute-start | bytes 1769480 | tf_op jit(solution)/shard_map/ppermute | solution.py:35
  19.6 13.3 %collective-permute-start.11 = (bf16[256,1152]{1,0:T(8,128)(2,1)S(1)}, bf16[256,1152]{1,0:T(8,128)(2,1)S(1)}, u32[]{:S(2)}, u32[]{:S(2)}) collective-permute-start(bf16[256,1152]{1,0:T(8,128)(2,1)S(1)} %shard_map.60.refs_0_), channel_id=1, source_target_pairs={{0,4},{1,5},{2,6},{3,7},{4,16},{5,17},{6,18},{7,19},{16,20},{17,21... | collective-permute-start | bytes 1769480 | tf_op jit(solution)/shard_map/ppermute | solution.py:35
  19.9 15.2 %collective-permute-start.10 = (bf16[256,1152]{1,0:T(8,128)(2,1)S(1)}, bf16[256,1152]{1,0:T(8,128)(2,1)S(1)}, u32[]{:S(2)}, u32[]{:S(2)}) collective-permute-start(bf16[256,1152]{1,0:T(8,128)(2,1)S(1)} %shard_map.60.refs_0_), channel_id=1, source_target_pairs={{0,16},{1,17},{2,18},{3,19},{4,20},{5,21},{6,22},{7,23},{16,0},{17... | collective-permute-start | bytes 1769480 | tf_op jit(solution)/shard_map/ppermute | solution.py:35
  24.7 7.9 %collective-permute-start.6 = (bf16[128,1152]{1,0:T(8,128)(2,1)S(1)}, bf16[128,1152]{1,0:T(8,128)(2,1)S(1)}, u32[]{:S(2)}, u32[]{:S(2)}) collective-permute-start(bf16[128,1152]{1,0:T(8,128)(2,1)S(1)} %collective-permute-done.5.refs_2_), channel_id=1, source_target_pairs={{0,32},{8,232},{32,64},{40,8},{64,96},{72,40},{96,128},{104,72},{1... | collective-permute-start | bytes 884744 | tf_op jit(solution)/shard_map/ppermute | solution.py:45
  32.7 6.4 %collective-permute-start.9 = (bf16[64,1152]{1,0:T(8,128)(2,1)S(1)}, bf16[64,1152]{1,0:T(8,128)(2,1)S(1)}, u32[]{:S(2)}, u32[]{:S(2)}) collective-permute-start(bf16[64,1152]{1,0:T(8,128)(2,1)S(1)} %slice.9), channel_id=1, source_target_pairs={{0,32},{8,232},{32,64},{40,8},{64,96},{72,40},{96,128},{104,72},{1... | collective-permute-start | bytes 442376 | tf_op jit(solution)/shard_map/ppermute | solution.py:45
  39.1 3.6 %collective-permute-start.13 = (bf16[192,1152]{1,0:T(8,128)(2,1)S(1)}, bf16[192,1152]{1,0:T(8,128)(2,1)S(1)}, u32[]{:S(2)}, u32[]{:S(2)}) collective-permute-start(bf16[192,1152]{1,0:T(8,128)(2,1)S(1)} %shard_map.66.refs_4_.refs_3_), channel_id=1, source_target_pairs={{0,8},{8,0},{1,9},{9,1},{2,10},{10,2},{3,11},{11,3},{4,12},{12,4},... | collective-permute-start | bytes 1327112 | tf_op jit(solution)/shard_map/ppermute | solution.py:23
  45.5 13.6 %collective-permute-start.14 = (bf16[320,1152]{1,0:T(8,128)(2,1)S(1)}, bf16[320,1152]{1,0:T(8,128)(2,1)S(1)}, u32[]{:S(2)}, u32[]{:S(2)}) collective-permute-start(bf16[320,1152]{1,0:T(8,128)(2,1)S(1)} %get-tuple-element.61), channel_id=1, source_target_pairs={{0,8},{8,0},{1,9},{9,1},{2,10},{10,2},{3,11},{11,3},{4,12},{12,4},... | collective-permute-start | bytes 2211848 | tf_op jit(solution)/shard_map/ppermute | solution.py:23
  47.9 5.2 %collective-permute-start.16 = (bf16[64,1152]{1,0:T(8,128)(2,1)S(1)}, bf16[64,1152]{1,0:T(8,128)(2,1)S(1)}, u32[]{:S(2)}, u32[]{:S(2)}) collective-permute-start(bf16[64,1152]{1,0:T(8,128)(2,1)S(1)} %get-tuple-element.70), channel_id=1, source_target_pairs={{0,224},{8,40},{32,0},{40,72},{64,32},{72,104},{96,64},{104,136},{... | collective-permute-start | bytes 442376 | tf_op jit(solution)/shard_map/ppermute | solution.py:45
  53.1 6.8 %collective-permute-start.17 = (bf16[128,1152]{1,0:T(8,128)(2,1)S(1)}, bf16[128,1152]{1,0:T(8,128)(2,1)S(1)}, u32[]{:S(2)}, u32[]{:S(2)}) collective-permute-start(bf16[128,1152]{1,0:T(8,128)(2,1)S(1)} %shard_map.72), channel_id=1, source_target_pairs={{0,224},{8,40},{32,0},{40,72},{64,32},{72,104},{96,64},{104,136},{... | collective-permute-start | bytes 884744 | tf_op jit(solution)/shard_map/ppermute | solution.py:45
  54.7 12.3 %collective-permute-start.19 = (bf16[256,1152]{1,0:T(8,128)(2,1)S(1)}, bf16[256,1152]{1,0:T(8,128)(2,1)S(1)}, u32[]{:S(2)}, u32[]{:S(2)}) collective-permute-start(bf16[256,1152]{1,0:T(8,128)(2,1)S(1)} %get-tuple-element.81), channel_id=1, source_target_pairs={{0,16},{1,17},{2,18},{3,19},{4,20},{5,21},{6,22},{7,23},{16,0},{17... | collective-permute-start | bytes 1769480 | tf_op jit(solution)/shard_map/ppermute | solution.py:35
  57.1 15.3 %collective-permute-start.22 = (bf16[256,1152]{1,0:T(8,128)(2,1)S(1)}, bf16[256,1152]{1,0:T(8,128)(2,1)S(1)}, u32[]{:S(2)}, u32[]{:S(2)}) collective-permute-start(bf16[256,1152]{1,0:T(8,128)(2,1)S(1)} %get-tuple-element.83), channel_id=1, source_target_pairs={{0,20},{1,21},{2,22},{3,23},{4,0},{5,1},{6,2},{7,3},{16,4},{17,5},... | collective-permute-start | bytes 1769480 | tf_op jit(solution)/shard_map/ppermute | solution.py:35
  58.3 14.2 %collective-permute-start.23 = (bf16[256,1152]{1,0:T(8,128)(2,1)S(1)}, bf16[256,1152]{1,0:T(8,128)(2,1)S(1)}, u32[]{:S(2)}, u32[]{:S(2)}) collective-permute-start(bf16[256,1152]{1,0:T(8,128)(2,1)S(1)} %get-tuple-element.84), channel_id=1, source_target_pairs={{0,4},{1,5},{2,6},{3,7},{4,16},{5,17},{6,18},{7,19},{16,20},{17,21... | collective-permute-start | bytes 1769480 | tf_op jit(solution)/shard_map/ppermute | solution.py:35
  60.0 7.0 %collective-permute-start.18 = (bf16[128,1152]{1,0:T(8,128)(2,1)S(1)}, bf16[128,1152]{1,0:T(8,128)(2,1)S(1)}, u32[]{:S(2)}, u32[]{:S(2)}) collective-permute-start(bf16[128,1152]{1,0:T(8,128)(2,1)S(1)} %shard_map.73), channel_id=1, source_target_pairs={{0,224},{8,40},{32,0},{40,72},{64,32},{72,104},{96,64},{104,136},{... | collective-permute-start | bytes 884744 | tf_op jit(solution)/shard_map/ppermute | solution.py:45
  67.1 8.5 %collective-permute-start.20 = (bf16[128,1152]{1,0:T(8,128)(2,1)S(1)}, bf16[128,1152]{1,0:T(8,128)(2,1)S(1)}, u32[]{:S(2)}, u32[]{:S(2)}) collective-permute-start(bf16[128,1152]{1,0:T(8,128)(2,1)S(1)} %shard_map.74), channel_id=1, source_target_pairs={{0,224},{8,40},{32,0},{40,72},{64,32},{72,104},{96,64},{104,136},{... | collective-permute-start | bytes 884744 | tf_op jit(solution)/shard_map/ppermute | solution.py:45
  72.8 5.2 %collective-permute-start.24 = (bf16[64,1152]{1,0:T(8,128)(2,1)S(1)}, bf16[64,1152]{1,0:T(8,128)(2,1)S(1)}, u32[]{:S(2)}, u32[]{:S(2)}) collective-permute-start(bf16[64,1152]{1,0:T(8,128)(2,1)S(1)} %get-tuple-element.87), channel_id=1, source_target_pairs={{0,3},{1,0},{2,1},{3,2},{4,7},{5,4},{6,5},{7,6},{16,19},{17,16},{1... | collective-permute-start | bytes 442376 | tf_op jit(solution)/shard_map/ppermute | solution.py:35
  73.5 6.4 %collective-permute-start.25 = (bf16[64,1152]{1,0:T(8,128)(2,1)S(1)}, bf16[64,1152]{1,0:T(8,128)(2,1)S(1)}, u32[]{:S(2)}, u32[]{:S(2)}) collective-permute-start(bf16[64,1152]{1,0:T(8,128)(2,1)S(1)} %get-tuple-element.88), channel_id=1, source_target_pairs={{0,1},{1,2},{2,3},{3,0},{4,5},{5,6},{6,7},{7,4},{16,17},{17,18},{1... | collective-permute-start | bytes 442376 | tf_op jit(solution)/shard_map/ppermute | solution.py:35
  74.9 6.6 %collective-permute-start.26 = (bf16[64,1152]{1,0:T(8,128)(2,1)S(1)}, bf16[64,1152]{1,0:T(8,128)(2,1)S(1)}, u32[]{:S(2)}, u32[]{:S(2)}) collective-permute-start(bf16[64,1152]{1,0:T(8,128)(2,1)S(1)} %get-tuple-element.89), channel_id=1, source_target_pairs={{0,2},{1,3},{2,0},{3,1},{4,6},{5,7},{6,4},{7,5},{16,18},{17,19},{1... | collective-permute-start | bytes 442376 | tf_op jit(solution)/shard_map/ppermute | solution.py:35
  75.6 5.9 %collective-permute-start.21 = (bf16[64,1152]{1,0:T(8,128)(2,1)S(1)}, bf16[64,1152]{1,0:T(8,128)(2,1)S(1)}, u32[]{:S(2)}, u32[]{:S(2)}) collective-permute-start(bf16[64,1152]{1,0:T(8,128)(2,1)S(1)} %get-tuple-element.90), channel_id=1, source_target_pairs={{0,8},{8,0},{1,9},{9,1},{2,10},{10,2},{3,11},{11,3},{4,12},{12,4},... | collective-permute-start | bytes 442376 | tf_op jit(solution)/shard_map/ppermute | solution.py:23
  (5 other events, 25.4 us)

commit v8 on v7

--- a/solution.py
+++ b/solution.py
@@ -248,7 +248,7 @@
         dk_a, back_a,
     )
     far_back = fanned(far_sum, -1)
-    far_back, d_texts3, d_texts1, d_texts2 = lax.optimization_barrier((far_back, d_texts3, d_texts1, d_texts2))
+    far_back, *_ = lax.optimization_barrier((far_back, d_texts3, d_texts1, d_texts2))
     back3, back1, back2 = (
         crossed(d_texts3, False, 2),
         crossed(d_texts1, False, -1),
@@ -260,7 +260,7 @@
     )
     returned = fanned(returned, -1)
     returned = fanned(added(z2_sum, returned), -1)
-    returned, back3 = lax.optimization_barrier((returned, back3))
+    returned, back3, d_texts0 = lax.optimization_barrier((returned, back3, d_texts0))
     returned = fanned(added(z1_sum, returned), -1)
     other = shifted(returned[rows:], "c", 1)
     txt_own, d_ahead, d_behind, d_across = local(

time: 83.2 us -> 83.2 us (level)
    ppermute x8, waiting for transfers between devices: 15.7 us -> 12.3 us  [fanned(): return lax.ppermute(value, ('z', 'c'), pairs)]
    ppermute x12, waiting for transfers between devices: 13.9 us -> 17.3 us  [crossed(): return lax.ppermute(value, PLANE, pairs)]
  transfers between devices with their start and end apart: 27 -> 27, of which waited for: 16 -> 17; matrix products, arithmetic and copies ran while one was open for 0% -> 0% of each run, Pallas kernels for 15% -> 15%
where the time goes in v8:
time: 83.2 us; the launch traced here: 82.6 us
  starting transfers between devices  32.4 us (39%)
  waiting for transfers between devices  31 us (37%)
  Pallas kernels  17 us (20%)
  between operations  2.12 us (3%)
    ppermute x12, starting transfers between devices, crossed(): return lax.ppermute(value, PLANE, pairs)  17.9 us
    ppermute x12, waiting for transfers between devices, crossed(): return lax.ppermute(value, PLANE, pairs)  17.3 us
    pallas_call x19, Pallas kernels, local(): pl.pallas_call(kernel, out_shape=outs, in_specs=[SMEM] * scalars + [place...  17 us
    ppermute x8, starting transfers between devices, fanned(): return lax.ppermute(value, ('z', 'c'), pairs)  13.4 us
    ppermute x8, waiting for transfers between devices, fanned(): return lax.ppermute(value, ('z', 'c'), pairs)  12.3 us
  transfers between devices with their start and end apart: 27, of which 17 were waited for; matrix products, arithmetic and copies ran while one was open for 0% of the time, Pallas kernels for 15%

profile of v8, /device:TPU:8, one launch (start us, length us, event | category | flops | bytes accessed | tf_op | source)
XLA Modules:
  0.0 82.6 jit_solution(13595393185110831866)
XLA Ops:
  3.3 2.0 %collective-permute-start.4 = (bf16[128,1152]{1,0:T(8,128)(2,1)S(1)}, bf16[128,1152]{1,0:T(8,128)(2,1)S(1)}, u32[]{:S(2)}, u32[]{:S(2)}) collective-permute-start(bf16[128,1152]{1,0:T(8,128)(2,1)S(1)} %shard_map.61), channel_id=1, source_target_pairs={{0,32},{8,232},{32,64},{40,8},{64,96},{72,40},{96,128},{104,72},{1... | collective-permute-start | bytes 884744 | tf_op jit(solution)/shard_map/ppermute | solution.py:45
  5.3 3.0 %collective-permute-start.2 = (bf16[64,1152]{1,0:T(8,128)(2,1)S(1)}, bf16[64,1152]{1,0:T(8,128)(2,1)S(1)}, u32[]{:S(2)}, u32[]{:S(2)}) collective-permute-start(bf16[64,1152]{1,0:T(8,128)(2,1)S(1)} %get-tuple-element.44.refs_0_), channel_id=1, source_target_pairs={{0,2},{1,3},{2,0},{3,1},{4,6},{5,7},{6,4},{7,5},{16,18},{17,19},{1... | collective-permute-start | bytes 442376 | tf_op jit(solution)/shard_map/ppermute | solution.py:35
  10.4 1.6 %collective-permute-done.2.refs_3_ = bf16[64,1152]{1,0:T(8,128)(2,1)S(1)} collective-permute-done((bf16[64,1152]{1,0:T(8,128)(2,1)S(1)}, bf16[64,1152]{1,0:T(8,128)(2,1)S(1)}, u32[]{:S(2)}, u32[]{:S(2)}) %collective-permute-start.2) | collective-permute-done | bytes 147488 | tf_op jit(solution)/shard_map/ppermute | solution.py:35
  12.0 1.7 %collective-permute-done.1.refs_2_ = bf16[64,1152]{1,0:T(8,128)(2,1)S(1)} collective-permute-done((bf16[64,1152]{1,0:T(8,128)(2,1)S(1)}, bf16[64,1152]{1,0:T(8,128)(2,1)S(1)}, u32[]{:S(2)}, u32[]{:S(2)}) %collective-permute-start.1) | collective-permute-done | bytes 147488 | tf_op jit(solution)/shard_map/ppermute | solution.py:35
  13.6 2.2 %collective-permute-done.refs_1_ = bf16[64,1152]{1,0:T(8,128)(2,1)S(1)} collective-permute-done((bf16[64,1152]{1,0:T(8,128)(2,1)S(1)}, bf16[64,1152]{1,0:T(8,128)(2,1)S(1)}, u32[]{:S(2)}, u32[]{:S(2)}) %collective-permute-start) | collective-permute-done | bytes 147488 | tf_op jit(solution)/shard_map/ppermute | solution.py:35
  15.9 2.0 %collective-permute-start.5 = (bf16[128,1152]{1,0:T(8,128)(2,1)S(1)}, bf16[128,1152]{1,0:T(8,128)(2,1)S(1)}, u32[]{:S(2)}, u32[]{:S(2)}) collective-permute-start(bf16[128,1152]{1,0:T(8,128)(2,1)S(1)} %collective-permute-done.4.refs_1_), channel_id=1, source_target_pairs={{0,32},{8,232},{32,64},{40,8},{64,96},{72,40},{96,128},{104,72},{1... | collective-permute-start | bytes 884744 | tf_op jit(solution)/shard_map/ppermute | solution.py:45
  17.9 1.7 %collective-permute-start.12 = (bf16[256,1152]{1,0:T(8,128)(2,1)S(1)}, bf16[256,1152]{1,0:T(8,128)(2,1)S(1)}, u32[]{:S(2)}, u32[]{:S(2)}) collective-permute-start(bf16[256,1152]{1,0:T(8,128)(2,1)S(1)} %shard_map.60.refs_0_), channel_id=1, source_target_pairs={{0,20},{1,21},{2,22},{3,23},{4,0},{5,1},{6,2},{7,3},{16,4},{17,5},... | collective-permute-start | bytes 1769480 | tf_op jit(solution)/shard_map/ppermute | solution.py:35
  19.9 3.5 %collective-permute-start.10 = (bf16[256,1152]{1,0:T(8,128)(2,1)S(1)}, bf16[256,1152]{1,0:T(8,128)(2,1)S(1)}, u32[]{:S(2)}, u32[]{:S(2)}) collective-permute-start(bf16[256,1152]{1,0:T(8,128)(2,1)S(1)} %shard_map.60.refs_0_), channel_id=1, source_target_pairs={{0,16},{1,17},{2,18},{3,19},{4,20},{5,21},{6,22},{7,23},{16,0},{17... | collective-permute-start | bytes 1769480 | tf_op jit(solution)/shard_map/ppermute | solution.py:35
  26.9 2.0 %shard_map.64 = (bf16[320,256]{1,0:T(8,128)(2,1)S(1)}, bf16[320,256]{1,0:T(8,128)(2,1)S(1)}, f32[320,1152]{1,0:T(8,128)S(1)}, f32[320,1152]{1,0:T(8,128)S(1)}) custom-call(f32[1]{0:T(128)S(6)} %copy.6.scale_ref, f32[1]{0:T(128)S(6)} %copy.7.bias_ref, bf16[256,1152]{1,0:T(8,128)(2,1)S(1)} %shard_map.60.refs_0_, ...), custom_call_target="tpu_custom_call" | custom-call | flops 754974720 | bytes 2064392 | tf_op jit(solution)/shard_map/pallas_call | solution.py:56
  28.8 3.8 %collective-permute-done.6.refs_0_ = bf16[128,1152]{1,0:T(8,128)(2,1)S(1)} collective-permute-done((bf16[128,1152]{1,0:T(8,128)(2,1)S(1)}, bf16[128,1152]{1,0:T(8,128)(2,1)S(1)}, u32[]{:S(2)}, u32[]{:S(2)}) %collective-permute-start.6) | collective-permute-done | bytes 294944 | tf_op jit(solution)/shard_map/ppermute | solution.py:45
  32.9 2.2 %collective-permute-done.10.refs_0_.refs_1_ = bf16[256,1152]{1,0:T(8,128)(2,1)S(1)} collective-permute-done((bf16[256,1152]{1,0:T(8,128)(2,1)S(1)}, bf16[256,1152]{1,0:T(8,128)(2,1)S(1)}, u32[]{:S(2)}, u32[]{:S(2)}) %collective-permute-start.10) | collective-permute-done | bytes 589856 | tf_op jit(solution)/shard_map/ppermute | solution.py:35
  35.1 4.0 %collective-permute-done.9.refs_1_ = bf16[64,1152]{1,0:T(8,128)(2,1)S(1)} collective-permute-done((bf16[64,1152]{1,0:T(8,128)(2,1)S(1)}, bf16[64,1152]{1,0:T(8,128)(2,1)S(1)}, u32[]{:S(2)}, u32[]{:S(2)}) %collective-permute-start.9) | collective-permute-done | bytes 147488 | tf_op jit(solution)/shard_map/ppermute | solution.py:45
  39.4 3.3 %shard_map.65 = (bf16[320,768]{1,0:T(8,128)(2,1)S(1)}, bf16[320,768]{1,0:T(8,128)(2,1)S(1)}, f32[320,1152]{1,0:T(8,128)S(1)}, bf16[320,1152]{1,0:T(8,128)(2,1)S(1)}) custom-call(f32[1]{0:T(128)S(6)} %copy.6.scale_ref, f32[1]{0:T(128)S(6)} %copy.7.bias_ref, bf16[256,1152]{1,0:T(8,128)(2,1)S(1)} %collective-permute-done.10.refs_0_.refs_1_, ...), custom_call_target="tpu_custom_call" | custom-call | flops 2264924160 | bytes 6193160 | tf_op jit(solution)/shard_map/pallas_call | solution.py:56
  42.8 2.1 %shard_map.69 = (bf16[192,1024]{1,0:T(8,128)(2,1)S(1)}, bf16[192,1152]{1,0:T(8,128)(2,1)S(1)}) custom-call(f32[1]{0:T(128)S(6)} %copy.6.scale_ref, f32[1]{0:T(128)S(6)} %copy.7.bias_ref, bf16[256,1152]{1,0:T(8,128)(2,1)S(1)} %shard_map.60.refs_0_, bf16[256,1152]{1,0:T(8,128)(2,1)S(1)} %collective-permute-done.10.refs_0_.refs_1_, ...), custom_call_target="tpu_custom_call" | custom-call | flops 905969664 | bytes 2801672 | tf_op jit(solution)/shard_map/pallas_call | solution.py:56
  45.6 2.1 %shard_map.68 = (bf16[192,1024]{1,0:T(8,128)(2,1)S(1)}, f32[192,1152]{1,0:T(8,128)S(1)}) custom-call(f32[1]{0:T(128)S(6)} %copy.6.scale_ref, f32[1]{0:T(128)S(6)} %copy.7.bias_ref, bf16[256,1152]{1,0:T(8,128)(2,1)S(1)} %shard_map.60.refs_0_, bf16[256,1152]{1,0:T(8,128)(2,1)S(1)} %collective-permute-done.10.refs_0_.refs_1_, ...), custom_call_target="tpu_custom_call" | custom-call | flops 905969664 | bytes 2801672 | tf_op jit(solution)/shard_map/pallas_call | solution.py:56
  48.2 3.2 %shard_map.71 = (bf16[256,1152]{1,0:T(8,128)(2,1)S(1)}, bf16[256,1152]{1,0:T(8,128)(2,1)S(1)}, bf16[256,1152]{1,0:T(8,128)(2,1)S(1)}) custom-call(f32[1]{0:T(128)S(6)} %copy.6.scale_ref, bf16[320,1152]{1,0:T(8,128)(2,1)S(1)} %shard_map.62.refs_1_.refs_3_.refs_0_, bf16[320,1152]{1,0:T(8,128)(2,1)S(1)} %shard_map.63.refs_2_.refs_4_.refs_1_, ...), custom_call_target="tpu_custom_call" | custom-call | flops 1811939328 | bytes 4456452 | tf_op jit(solution)/shard_map/pallas_call | solution.py:56
  51.4 1.7 %collective-permute-done.16.far_ref = bf16[64,1152]{1,0:T(8,128)(2,1)S(1)} collective-permute-done((bf16[64,1152]{1,0:T(8,128)(2,1)S(1)}, bf16[64,1152]{1,0:T(8,128)(2,1)S(1)}, u32[]{:S(2)}, u32[]{:S(2)}) %collective-permute-start.16) | collective-permute-done | bytes 147488 | tf_op jit(solution)/shard_map/ppermute | solution.py:45
  54.7 2.4 %collective-permute-start.19 = (bf16[256,1152]{1,0:T(8,128)(2,1)S(1)}, bf16[256,1152]{1,0:T(8,128)(2,1)S(1)}, u32[]{:S(2)}, u32[]{:S(2)}) collective-permute-start(bf16[256,1152]{1,0:T(8,128)(2,1)S(1)} %get-tuple-element.75), channel_id=1, source_target_pairs={{0,16},{1,17},{2,18},{3,19},{4,20},{5,21},{6,22},{7,23},{16,0},{17... | collective-permute-start | bytes 1769480 | tf_op jit(solution)/shard_map/ppermute | solution.py:35
  60.0 2.8 %collective-permute-start.18 = (bf16[128,1152]{1,0:T(8,128)(2,1)S(1)}, bf16[128,1152]{1,0:T(8,128)(2,1)S(1)}, u32[]{:S(2)}, u32[]{:S(2)}) collective-permute-start(bf16[128,1152]{1,0:T(8,128)(2,1)S(1)} %shard_map.73), channel_id=1, source_target_pairs={{0,224},{8,40},{32,0},{40,72},{64,32},{72,104},{96,64},{104,136},{... | collective-permute-start | bytes 884744 | tf_op jit(solution)/shard_map/ppermute | solution.py:45
  64.0 2.2 %collective-permute-done.19.refs_3_ = bf16[256,1152]{1,0:T(8,128)(2,1)S(1)} collective-permute-done((bf16[256,1152]{1,0:T(8,128)(2,1)S(1)}, bf16[256,1152]{1,0:T(8,128)(2,1)S(1)}, u32[]{:S(2)}, u32[]{:S(2)}) %collective-permute-start.19) | collective-permute-done | bytes 589856 | tf_op jit(solution)/shard_map/ppermute | solution.py:35
  67.1 3.8 %collective-permute-start.20 = (bf16[128,1152]{1,0:T(8,128)(2,1)S(1)}, bf16[128,1152]{1,0:T(8,128)(2,1)S(1)}, u32[]{:S(2)}, u32[]{:S(2)}) collective-permute-start(bf16[128,1152]{1,0:T(8,128)(2,1)S(1)} %shard_map.75), channel_id=1, source_target_pairs={{0,224},{8,40},{32,0},{40,72},{64,32},{72,104},{96,64},{104,136},{... | collective-permute-start | bytes 884744 | tf_op jit(solution)/shard_map/ppermute | solution.py:45
  75.7 2.3 %collective-permute-done.24.refs_4_ = bf16[64,1152]{1,0:T(8,128)(2,1)S(1)} collective-permute-done((bf16[64,1152]{1,0:T(8,128)(2,1)S(1)}, bf16[64,1152]{1,0:T(8,128)(2,1)S(1)}, u32[]{:S(2)}, u32[]{:S(2)}) %collective-permute-start.24) | collective-permute-done | bytes 147488 | tf_op jit(solution)/shard_map/ppermute | solution.py:35
  78.0 1.8 %collective-permute-done.25.refs_5_ = bf16[64,1152]{1,0:T(8,128)(2,1)S(1)} collective-permute-done((bf16[64,1152]{1,0:T(8,128)(2,1)S(1)}, bf16[64,1152]{1,0:T(8,128)(2,1)S(1)}, u32[]{:S(2)}, u32[]{:S(2)}) %collective-permute-start.25) | collective-permute-done | bytes 147488 | tf_op jit(solution)/shard_map/ppermute | solution.py:35
  79.8 1.7 %collective-permute-done.26.refs_6_ = bf16[64,1152]{1,0:T(8,128)(2,1)S(1)} collective-permute-done((bf16[64,1152]{1,0:T(8,128)(2,1)S(1)}, bf16[64,1152]{1,0:T(8,128)(2,1)S(1)}, u32[]{:S(2)}, u32[]{:S(2)}) %collective-permute-start.26) | collective-permute-done | bytes 147488 | tf_op jit(solution)/shard_map/ppermute | solution.py:35
  (55 shorter events, 21.3 us)
Async XLA Ops:
  3.3 12.6 %collective-permute-start.4 = (bf16[128,1152]{1,0:T(8,128)(2,1)S(1)}, bf16[128,1152]{1,0:T(8,128)(2,1)S(1)}, u32[]{:S(2)}, u32[]{:S(2)}) collective-permute-start(bf16[128,1152]{1,0:T(8,128)(2,1)S(1)} %shard_map.61), channel_id=1, source_target_pairs={{0,32},{8,232},{32,64},{40,8},{64,96},{72,40},{96,128},{104,72},{1... | collective-permute-start | bytes 884744 | tf_op jit(solution)/shard_map/ppermute | solution.py:45
  5.3 6.6 %collective-permute-start.2 = (bf16[64,1152]{1,0:T(8,128)(2,1)S(1)}, bf16[64,1152]{1,0:T(8,128)(2,1)S(1)}, u32[]{:S(2)}, u32[]{:S(2)}) collective-permute-start(bf16[64,1152]{1,0:T(8,128)(2,1)S(1)} %get-tuple-element.44.refs_0_), channel_id=1, source_target_pairs={{0,2},{1,3},{2,0},{3,1},{4,6},{5,7},{6,4},{7,5},{16,18},{17,19},{1... | collective-permute-start | bytes 442376 | tf_op jit(solution)/shard_map/ppermute | solution.py:35
  8.3 5.3 %collective-permute-start.1 = (bf16[64,1152]{1,0:T(8,128)(2,1)S(1)}, bf16[64,1152]{1,0:T(8,128)(2,1)S(1)}, u32[]{:S(2)}, u32[]{:S(2)}) collective-permute-start(bf16[64,1152]{1,0:T(8,128)(2,1)S(1)} %get-tuple-element.44.refs_0_), channel_id=1, source_target_pairs={{0,3},{1,0},{2,1},{3,2},{4,7},{5,4},{6,5},{7,6},{16,19},{17,16},{1... | collective-permute-start | bytes 442376 | tf_op jit(solution)/shard_map/ppermute | solution.py:35
  9.5 6.4 %collective-permute-start = (bf16[64,1152]{1,0:T(8,128)(2,1)S(1)}, bf16[64,1152]{1,0:T(8,128)(2,1)S(1)}, u32[]{:S(2)}, u32[]{:S(2)}) collective-permute-start(bf16[64,1152]{1,0:T(8,128)(2,1)S(1)} %get-tuple-element.44.refs_0_), channel_id=1, source_target_pairs={{0,1},{1,2},{2,3},{3,0},{4,5},{5,6},{6,7},{7,4},{16,17},{17,18},{1... | collective-permute-start | bytes 442376 | tf_op jit(solution)/shard_map/ppermute | solution.py:35
  15.9 8.8 %collective-permute-start.5 = (bf16[128,1152]{1,0:T(8,128)(2,1)S(1)}, bf16[128,1152]{1,0:T(8,128)(2,1)S(1)}, u32[]{:S(2)}, u32[]{:S(2)}) collective-permute-start(bf16[128,1152]{1,0:T(8,128)(2,1)S(1)} %collective-permute-done.4.refs_1_), channel_id=1, source_target_pairs={{0,32},{8,232},{32,64},{40,8},{64,96},{72,40},{96,128},{104,72},{1... | collective-permute-start | bytes 884744 | tf_op jit(solution)/shard_map/ppermute | solution.py:45
  17.9 6.8 %collective-permute-start.7 = (bf16[128,1152]{1,0:T(8,128)(2,1)S(1)}, bf16[128,1152]{1,0:T(8,128)(2,1)S(1)}, u32[]{:S(2)}, u32[]{:S(2)}) collective-permute-start(bf16[128,1152]{1,0:T(8,128)(2,1)S(1)} %collective-permute-done.4.refs_1_), channel_id=1, source_target_pairs={{0,8},{8,0},{1,9},{9,1},{2,10},{10,2},{3,11},{11,3},{4,12},{12,4},... | collective-permute-start | bytes 884744 | tf_op jit(solution)/shard_map/ppermute | solution.py:23
  17.9 15.0 %collective-permute-start.12 = (bf16[256,1152]{1,0:T(8,128)(2,1)S(1)}, bf16[256,1152]{1,0:T(8,128)(2,1)S(1)}, u32[]{:S(2)}, u32[]{:S(2)}) collective-permute-start(bf16[256,1152]{1,0:T(8,128)(2,1)S(1)} %shard_map.60.refs_0_), channel_id=1, source_target_pairs={{0,20},{1,21},{2,22},{3,23},{4,0},{5,1},{6,2},{7,3},{16,4},{17,5},... | collective-permute-start | bytes 1769480 | tf_op jit(solution)/shard_map/ppermute | solution.py:35
  19.6 13.3 %collective-permute-start.11 = (bf16[256,1152]{1,0:T(8,128)(2,1)S(1)}, bf16[256,1152]{1,0:T(8,128)(2,1)S(1)}, u32[]{:S(2)}, u32[]{:S(2)}) collective-permute-start(bf16[256,1152]{1,0:T(8,128)(2,1)S(1)} %shard_map.60.refs_0_), channel_id=1, source_target_pairs={{0,4},{1,5},{2,6},{3,7},{4,16},{5,17},{6,18},{7,19},{16,20},{17,21... | collective-permute-start | bytes 1769480 | tf_op jit(solution)/shard_map/ppermute | solution.py:35
  19.9 15.2 %collective-permute-start.10 = (bf16[256,1152]{1,0:T(8,128)(2,1)S(1)}, bf16[256,1152]{1,0:T(8,128)(2,1)S(1)}, u32[]{:S(2)}, u32[]{:S(2)}) collective-permute-start(bf16[256,1152]{1,0:T(8,128)(2,1)S(1)} %shard_map.60.refs_0_), channel_id=1, source_target_pairs={{0,16},{1,17},{2,18},{3,19},{4,20},{5,21},{6,22},{7,23},{16,0},{17... | collective-permute-start | bytes 1769480 | tf_op jit(solution)/shard_map/ppermute | solution.py:35
  24.7 7.9 %collective-permute-start.6 = (bf16[128,1152]{1,0:T(8,128)(2,1)S(1)}, bf16[128,1152]{1,0:T(8,128)(2,1)S(1)}, u32[]{:S(2)}, u32[]{:S(2)}) collective-permute-start(bf16[128,1152]{1,0:T(8,128)(2,1)S(1)} %collective-permute-done.5.refs_2_), channel_id=1, source_target_pairs={{0,32},{8,232},{32,64},{40,8},{64,96},{72,40},{96,128},{104,72},{1... | collective-permute-start | bytes 884744 | tf_op jit(solution)/shard_map/ppermute | solution.py:45
  32.7 6.4 %collective-permute-start.9 = (bf16[64,1152]{1,0:T(8,128)(2,1)S(1)}, bf16[64,1152]{1,0:T(8,128)(2,1)S(1)}, u32[]{:S(2)}, u32[]{:S(2)}) collective-permute-start(bf16[64,1152]{1,0:T(8,128)(2,1)S(1)} %slice.9), channel_id=1, source_target_pairs={{0,32},{8,232},{32,64},{40,8},{64,96},{72,40},{96,128},{104,72},{1... | collective-permute-start | bytes 442376 | tf_op jit(solution)/shard_map/ppermute | solution.py:45
  39.1 3.6 %collective-permute-start.13 = (bf16[192,1152]{1,0:T(8,128)(2,1)S(1)}, bf16[192,1152]{1,0:T(8,128)(2,1)S(1)}, u32[]{:S(2)}, u32[]{:S(2)}) collective-permute-start(bf16[192,1152]{1,0:T(8,128)(2,1)S(1)} %shard_map.66.refs_4_.refs_3_), channel_id=1, source_target_pairs={{0,8},{8,0},{1,9},{9,1},{2,10},{10,2},{3,11},{11,3},{4,12},{12,4},... | collective-permute-start | bytes 1327112 | tf_op jit(solution)/shard_map/ppermute | solution.py:23
  45.5 13.6 %collective-permute-start.14 = (bf16[320,1152]{1,0:T(8,128)(2,1)S(1)}, bf16[320,1152]{1,0:T(8,128)(2,1)S(1)}, u32[]{:S(2)}, u32[]{:S(2)}) collective-permute-start(bf16[320,1152]{1,0:T(8,128)(2,1)S(1)} %get-tuple-element.59), channel_id=1, source_target_pairs={{0,8},{8,0},{1,9},{9,1},{2,10},{10,2},{3,11},{11,3},{4,12},{12,4},... | collective-permute-start | bytes 2211848 | tf_op jit(solution)/shard_map/ppermute | solution.py:23
  47.9 5.2 %collective-permute-start.16 = (bf16[64,1152]{1,0:T(8,128)(2,1)S(1)}, bf16[64,1152]{1,0:T(8,128)(2,1)S(1)}, u32[]{:S(2)}, u32[]{:S(2)}) collective-permute-start(bf16[64,1152]{1,0:T(8,128)(2,1)S(1)} %get-tuple-element.68), channel_id=1, source_target_pairs={{0,224},{8,40},{32,0},{40,72},{64,32},{72,104},{96,64},{104,136},{... | collective-permute-start | bytes 442376 | tf_op jit(solution)/shard_map/ppermute | solution.py:45
  53.1 6.8 %collective-permute-start.17 = (bf16[128,1152]{1,0:T(8,128)(2,1)S(1)}, bf16[128,1152]{1,0:T(8,128)(2,1)S(1)}, u32[]{:S(2)}, u32[]{:S(2)}) collective-permute-start(bf16[128,1152]{1,0:T(8,128)(2,1)S(1)} %shard_map.72), channel_id=1, source_target_pairs={{0,224},{8,40},{32,0},{40,72},{64,32},{72,104},{96,64},{104,136},{... | collective-permute-start | bytes 884744 | tf_op jit(solution)/shard_map/ppermute | solution.py:45
  54.7 11.5 %collective-permute-start.19 = (bf16[256,1152]{1,0:T(8,128)(2,1)S(1)}, bf16[256,1152]{1,0:T(8,128)(2,1)S(1)}, u32[]{:S(2)}, u32[]{:S(2)}) collective-permute-start(bf16[256,1152]{1,0:T(8,128)(2,1)S(1)} %get-tuple-element.75), channel_id=1, source_target_pairs={{0,16},{1,17},{2,18},{3,19},{4,20},{5,21},{6,22},{7,23},{16,0},{17... | collective-permute-start | bytes 1769480 | tf_op jit(solution)/shard_map/ppermute | solution.py:35
  57.1 15.3 %collective-permute-start.22 = (bf16[256,1152]{1,0:T(8,128)(2,1)S(1)}, bf16[256,1152]{1,0:T(8,128)(2,1)S(1)}, u32[]{:S(2)}, u32[]{:S(2)}) collective-permute-start(bf16[256,1152]{1,0:T(8,128)(2,1)S(1)} %get-tuple-element.76), channel_id=1, source_target_pairs={{0,20},{1,21},{2,22},{3,23},{4,0},{5,1},{6,2},{7,3},{16,4},{17,5},... | collective-permute-start | bytes 1769480 | tf_op jit(solution)/shard_map/ppermute | solution.py:35
  58.3 14.2 %collective-permute-start.23 = (bf16[256,1152]{1,0:T(8,128)(2,1)S(1)}, bf16[256,1152]{1,0:T(8,128)(2,1)S(1)}, u32[]{:S(2)}, u32[]{:S(2)}) collective-permute-start(bf16[256,1152]{1,0:T(8,128)(2,1)S(1)} %get-tuple-element.77), channel_id=1, source_target_pairs={{0,4},{1,5},{2,6},{3,7},{4,16},{5,17},{6,18},{7,19},{16,20},{17,21... | collective-permute-start | bytes 1769480 | tf_op jit(solution)/shard_map/ppermute | solution.py:35
  60.0 7.0 %collective-permute-start.18 = (bf16[128,1152]{1,0:T(8,128)(2,1)S(1)}, bf16[128,1152]{1,0:T(8,128)(2,1)S(1)}, u32[]{:S(2)}, u32[]{:S(2)}) collective-permute-start(bf16[128,1152]{1,0:T(8,128)(2,1)S(1)} %shard_map.73), channel_id=1, source_target_pairs={{0,224},{8,40},{32,0},{40,72},{64,32},{72,104},{96,64},{104,136},{... | collective-permute-start | bytes 884744 | tf_op jit(solution)/shard_map/ppermute | solution.py:45
  67.1 8.5 %collective-permute-start.20 = (bf16[128,1152]{1,0:T(8,128)(2,1)S(1)}, bf16[128,1152]{1,0:T(8,128)(2,1)S(1)}, u32[]{:S(2)}, u32[]{:S(2)}) collective-permute-start(bf16[128,1152]{1,0:T(8,128)(2,1)S(1)} %shard_map.75), channel_id=1, source_target_pairs={{0,224},{8,40},{32,0},{40,72},{64,32},{72,104},{96,64},{104,136},{... | collective-permute-start | bytes 884744 | tf_op jit(solution)/shard_map/ppermute | solution.py:45
  72.8 5.2 %collective-permute-start.24 = (bf16[64,1152]{1,0:T(8,128)(2,1)S(1)}, bf16[64,1152]{1,0:T(8,128)(2,1)S(1)}, u32[]{:S(2)}, u32[]{:S(2)}) collective-permute-start(bf16[64,1152]{1,0:T(8,128)(2,1)S(1)} %get-tuple-element.83), channel_id=1, source_target_pairs={{0,3},{1,0},{2,1},{3,2},{4,7},{5,4},{6,5},{7,6},{16,19},{17,16},{1... | collective-permute-start | bytes 442376 | tf_op jit(solution)/shard_map/ppermute | solution.py:35
  73.5 6.4 %collective-permute-start.25 = (bf16[64,1152]{1,0:T(8,128)(2,1)S(1)}, bf16[64,1152]{1,0:T(8,128)(2,1)S(1)}, u32[]{:S(2)}, u32[]{:S(2)}) collective-permute-start(bf16[64,1152]{1,0:T(8,128)(2,1)S(1)} %get-tuple-element.84), channel_id=1, source_target_pairs={{0,1},{1,2},{2,3},{3,0},{4,5},{5,6},{6,7},{7,4},{16,17},{17,18},{1... | collective-permute-start | bytes 442376 | tf_op jit(solution)/shard_map/ppermute | solution.py:35
  74.9 6.6 %collective-permute-start.26 = (bf16[64,1152]{1,0:T(8,128)(2,1)S(1)}, bf16[64,1152]{1,0:T(8,128)(2,1)S(1)}, u32[]{:S(2)}, u32[]{:S(2)}) collective-permute-start(bf16[64,1152]{1,0:T(8,128)(2,1)S(1)} %get-tuple-element.85), channel_id=1, source_target_pairs={{0,2},{1,3},{2,0},{3,1},{4,6},{5,7},{6,4},{7,5},{16,18},{17,19},{1... | collective-permute-start | bytes 442376 | tf_op jit(solution)/shard_map/ppermute | solution.py:35
  75.6 5.9 %collective-permute-start.21 = (bf16[64,1152]{1,0:T(8,128)(2,1)S(1)}, bf16[64,1152]{1,0:T(8,128)(2,1)S(1)}, u32[]{:S(2)}, u32[]{:S(2)}) collective-permute-start(bf16[64,1152]{1,0:T(8,128)(2,1)S(1)} %get-tuple-element.86), channel_id=1, source_target_pairs={{0,8},{8,0},{1,9},{9,1},{2,10},{10,2},{3,11},{11,3},{4,12},{12,4},... | collective-permute-start | bytes 442376 | tf_op jit(solution)/shard_map/ppermute | solution.py:23
  (5 other events, 35.3 us)
